TPU v7x, 32 devices: a whole 2x2x4 slice. The times are simulated.
32 devices in a mesh: dp: 8 (over z, x), tensor: 4 (over y, core).
Axes of the slice: x: 2, y: 2, z: 4, core: 2. Of those that a mesh axis runs over, the one named last changes fastest.
Arguments:
- d_out: bfloat16 [2048, 3072], P('dp'), may hold values from -12 to 12
- gate: bfloat16 [2048, 4096], P('dp', 'tensor'), may hold values from -6 to 6
- up_proj: bfloat16 [2048, 4096], P('dp', 'tensor'), may hold values from -12 to 12
- master: float32 [4096, 3072], P(('tensor', 'dp')), may hold values from -0.09375 to 0.09375
- moment_one: float32 [4096, 3072], P(('tensor', 'dp')), may hold values from -4 to 4
- moment_two: float32 [4096, 3072], P(('tensor', 'dp')), may hold values from 0.05 to 2
Outputs:
- gate_grad: bfloat16 [2048, 4096], P('dp', 'tensor')
- up_grad: bfloat16 [2048, 4096], P('dp', 'tensor')
- master_next: float32 [4096, 3072], P(('tensor', 'dp'))
- moment_one_next: float32 [4096, 3072], P(('tensor', 'dp'))
- moment_two_next: float32 [4096, 3072], P(('tensor', 'dp'))
- weight_next: bfloat16 [4096, 3072], P('tensor')
All inputs are finite; a program needn't handle non-finite values.
Results may differ from a plain program's by a relative error of at most 0.005.
Values may be sent and summed in bfloat16 or wider, within the bound.
No kernel may reach another device: no remote copies, remote signals or barrier semaphores. Data moves between devices by JAX's collectives and lax.ppermute only.
A program may use at most 64 MiB of HBM per device.

v0:
```python
import jax
import jax.numpy as jnp
from jax import lax
from jax.sharding import PartitionSpec as P

D = 3072
FF = 4096


def on_device(d_out, gate, up_proj, master, moment_one, moment_two):
    weight = master.astype(jnp.bfloat16)
    gate_f = gate.astype(jnp.float32)
    up_f = up_proj.astype(jnp.float32)
    silu_gate = jax.nn.silu(gate_f)
    hidden = (silu_gate * up_f).astype(jnp.bfloat16)
    d_hidden = lax.dot_general(
        d_out,
        lax.all_gather(weight, "dp", axis=0, tiled=True),
        (((1,), (1,)), ((), ())),
        preferred_element_type=jnp.float32,
    )
    partial_term = lax.dot_general(
        hidden, d_out, (((0,), (0,)), ((), ())), preferred_element_type=jnp.float32
    )
    grad = lax.psum_scatter(partial_term, "dp", scatter_dimension=0, tiled=True)
    up_grad = (d_hidden * silu_gate).astype(jnp.bfloat16)
    sigm = jax.nn.sigmoid(gate_f)
    gate_grad = (d_hidden * up_f * sigm * (1.0 + gate_f * (1.0 - sigm))).astype(jnp.bfloat16)
    local_squares = jnp.sum(grad * grad)
    total = lax.psum(local_squares, ("dp", "tensor"))
    factor = 1.0 / jnp.sqrt(total / (FF * D) + 1e-06)
    clipped = grad * factor
    moment_one_next = 0.9 * moment_one + 0.1 * clipped
    moment_two_next = 0.95 * moment_two + 0.05 * clipped * clipped
    master_next = master - 0.003 * (
        moment_one_next / (jnp.sqrt(moment_two_next) + 1e-08) + 0.1 * master
    )
    shard_next = master_next.astype(jnp.bfloat16)
    weight_next = lax.all_gather(shard_next, "dp", axis=0, tiled=True)
    return (gate_grad, up_grad, master_next, moment_one_next, moment_two_next, weight_next)


def solution(mesh):
    placed = (
        P("dp", None),
        P("dp", "tensor"),
        P("dp", "tensor"),
        P(("tensor", "dp"), None),
        P(("tensor", "dp"), None),
        P(("tensor", "dp"), None),
    )
    return jax.shard_map(
        on_device,
        mesh=mesh,
        in_specs=placed,
        out_specs=(
            P("dp", "tensor"),
            P("dp", "tensor"),
            P(("tensor", "dp"), None),
            P(("tensor", "dp"), None),
            P(("tensor", "dp"), None),
            P("tensor", None),
        ),
        check_vma=False,
    )
```

profile of v0, /device:TPU:0, one launch (start us, length us, event | category | flops | bytes accessed | tf_op | source)
XLA Modules:
  0.0 487.3 jit_solution(13127717741184371122)
XLA Ops:
  7.2 0.0 copy-start
  7.2 0.0 reduce-scatter.2.cloned.1.call-start
  7.2 1.4 copy-done
  8.6 7.7 %fusion.9 = f32[1024,3072]{1,0:T(8,128)} fusion(bf16[256,3072]{1,0:T(8,128)(2,1)S(1)} %copy-done, bf16[256,1024]{1,0:T(8,128)(2,1)} %param.8, bf16[256,1024]{1,0:T(8,128)(2,1)} %param.7), kind=kOutput, calls=%fused_computation.19 | convolution fusion | flops 1612709888 | bytes 15204352 | tf_op jit(solution)/shard_map/dot_general | solution.py:22
  16.3 0.0 reduce-scatter.2.cloned.1.call-update
  16.3 0.0 all-gather.3.cloned.1.call-start
  16.3 210.0 %reduce-scatter.2.cloned.1.call-done = f32[128,3072]{1,0:T(8,128)} async-done(((f32[1024,3072]{1,0:T(8,128)}), f32[128,3072]{1,0:T(8,128)}) %reduce-scatter.2.cloned.1.call-update) | async-done | bytes 1572880 | tf_op jit(solution)/shard_map/reduce_scatter | solution.py:25
  226.4 0.0 copy-start.1
  226.4 2.5 multiply_reduce_fusion
  228.9 39.6 %psum.7 = f32[]{:T(128)} all-reduce(f32[]{:T(128)} %multiply_reduce_fusion), channel_id=1, replica_groups=mesh['dp'=8,'tensor'=4] {'dp','tensor'}, use_global_device_ids=true, to_apply=%region_2.3 | all-reduce | flops 1 | bytes 8 | tf_op jit(solution)/shard_map/psum | solution.py:30
  269.2 0.0 copy-done.1
  269.2 6.5 %fusion.12 = (bf16[128,3072]{1,0:T(8,128)(2,1)}, f32[128,3072]{1,0:T(8,128)}, f32[128,3072]{1,0:T(8,128)}, f32[128,3072]{1,0:T(8,128)}, bf16[128,3072]{1,0:T(8,128)(2,1)}) fusion(f32[128,3072]{1,0:T(8,128)} %param.9, f32[128,3072]{1,0:T(8,128)S(1)} %copy-done.1, f32[]{:T(128)S(6)} %sqrt.6, f32[128,3072]{1,0:T(8,128)} %param.11, f32[128,3072]{1,0:T(8,128)} %param.10), kind=kLoop, calls=%fused_computation.21 | loop fusion | flops 6291456 | bytes 12582916 | tf_op jit(solution)/shard_map/convert_element_type | solution.py:38
  275.7 0.0 copy-start.2
  275.7 0.0 copy-start.3
  275.7 0.0 all-gather.3.cloned.1.call-update
  275.7 0.0 all-gather.5.cloned.1.call-start
  275.7 0.7 all-gather.5.cloned.1.call-update
  276.4 98.4 %all-gather.3.cloned.1.call-done = bf16[1024,3072]{1,0:T(8,128)(2,1)} async-done(((bf16[128,3072]{1,0:T(8,128)(2,1)}), bf16[1024,3072]{1,0:T(8,128)(2,1)}) %all-gather.3.cloned.1.call-update) | async-done | bytes 6291472 | tf_op jit(solution)/shard_map/all_gather | solution.py:18
  374.8 0.0 copy-done.2
  374.8 0.0 copy-done.3
  374.8 5.9 %multiply_convert_fusion = (bf16[256,1024]{1,0:T(8,128)(2,1)}, bf16[256,1024]{1,0:T(8,128)(2,1)}) fusion(bf16[256,1024]{1,0:T(8,128)(2,1)S(1)} %copy-done.2, bf16[256,1024]{1,0:T(8,128)(2,1)S(1)} %copy-done.3, bf16[256,3072]{1,0:T(8,128)(2,1)S(1)} %copy-done, bf16[1024,3072]{1,0:T(8,128)(2,1)} %all-gather.3.cloned.1.call-done), kind=kOutput, calls=%fused_computation.18 | convolution fusion | flops 1614544896 | bytes 9961472 | tf_op jit(solution)/shard_map/dot_general | solution.py:16
  380.8 94.1 %all-gather.5.cloned.1.call-done = bf16[1024,3072]{1,0:T(8,128)(2,1)} async-done(((bf16[128,3072]{1,0:T(8,128)(2,1)}), bf16[1024,3072]{1,0:T(8,128)(2,1)}) %all-gather.5.cloned.1.call-update) | async-done | bytes 6291472 | tf_op jit(solution)/shard_map/all_gather | solution.py:39
  474.9 5.9 %copy.13 = bf16[1024,3072]{1,0:T(8,128)(2,1)} copy(bf16[1024,3072]{1,0:T(8,128)(2,1)} %all-gather.5.cloned.1.call-done) | data formatting | bytes 12582912
Async XLA Ops:
  7.2 1.4 copy-start
  7.2 219.2 %reduce-scatter.2.cloned.1.call-start = ((), (), s32[]{:S(2)}) async-start(), calls=%async_computation.2 | async-start | bytes 14155776 | tf_op jit(solution)/shard_map/reduce_scatter | solution.py:25
  16.3 358.5 %all-gather.3.cloned.1.call-start = ((), (), s32[]{:S(2)}) async-start(), calls=%async_computation.1 | async-start | bytes 7077888 | tf_op jit(solution)/shard_map/all_gather | solution.py:18
  226.4 42.8 %copy-start.1 = (f32[128,3072]{1,0:T(8,128)S(1)}, f32[128,3072]{1,0:T(8,128)}, u32[]{:S(2)}) copy-start(f32[128,3072]{1,0:T(8,128)} %reduce-scatter.2.cloned.1.call-done) | copy-start | bytes 4718596
  275.7 99.2 %copy-start.2 = (bf16[256,1024]{1,0:T(8,128)(2,1)S(1)}, bf16[256,1024]{1,0:T(8,128)(2,1)}, u32[]{:S(2)}) copy-start(bf16[256,1024]{1,0:T(8,128)(2,1)} %param.7) | copy-start | bytes 1572868
  275.7 99.2 %copy-start.3 = (bf16[256,1024]{1,0:T(8,128)(2,1)S(1)}, bf16[256,1024]{1,0:T(8,128)(2,1)}, u32[]{:S(2)}) copy-start(bf16[256,1024]{1,0:T(8,128)(2,1)} %param.8) | copy-start | bytes 1572868
  275.7 199.2 %all-gather.5.cloned.1.call-start = ((), (), s32[]{:S(2)}) async-start(), calls=%async_computation.3 | async-start | bytes 7077888 | tf_op jit(solution)/shard_map/all_gather | solution.py:39
Sparse Core Ops, SparseCore 0:
  16.4 209.8 reduce-scatter.1
  275.8 98.9 all-gather.2
  377.6 97.1 all-gather.4
where the time goes:
time: 488 us; the launch traced here: 487 us
  waiting for transfers between devices  403 us (83%)
  blocking collectives  39.6 us (8%)
  between operations  14.5 us (3%)
  matrix products  13.6 us (3%)
  other arithmetic  9.02 us (2%)
  local copies, waits for them, and re-layouts  7.3 us (1%)
    reduce_scatter x1, waiting for transfers between devices, on_device(): grad = lax.psum_scatter(partial_term, 'dp', scatter_dimension=0, tiled=True)  210 us
    all_gather x1, waiting for transfers between devices, on_device(): lax.all_gather(weight, 'dp', axis=0, tiled=True)  98.4 us
    all_gather x1, waiting for transfers between devices, on_device(): weight_next = lax.all_gather(shard_next, 'dp', axis=0, tiled=True)  94.1 us
    psum x1, blocking collectives, on_device(): total = lax.psum(local_squares, ('dp', 'tensor'))  39.6 us
  transfers between devices with their start and end apart: 3, of which 3 were waited for; matrix products, arithmetic and copies ran while one was open for 1% of the time, Pallas kernels for 0%

commit v1 on v0

v1 whole, which is shorter than its diff:
```python
import jax
import jax.numpy as jnp
from jax import lax
from jax.sharding import PartitionSpec as P

D = 3072
FF = 4096
CELL = 8
BF16 = jnp.bfloat16
F32 = jnp.float32

ENDS, MIDS, ALL = (0, 3), (1, 2), (0, 1, 2, 3)
NEIGHBOURS = ((0, 1), (1, 0), (2, 3), (3, 2))
MIDDLE = ((1, 2), (2, 1))
INWARD = ((0, 1), (3, 2))
OUTWARD = ((1, 0), (2, 3))


def on_device(n, d_out, gate, up_proj, master, moment_one, moment_two):
    outer = n // CELL
    place = lax.axis_index("dp")
    z, x = place % CELL // 2, place % 2
    t = lax.axis_index("tensor")
    tokens, width = gate.shape
    rows = master.shape[0]
    part = width // CELL
    cols = D // 4
    ends = (z == 0) | (z == 3)
    same_pair = [[k + CELL * j for j in range(outer)] for k in range(CELL)]

    def line(value, moves):
        return lax.ppermute(
            value,
            "dp",
            [(i, i - i % CELL + b * 2 + i % 2) for i in range(n) for a, b in moves if i % CELL // 2 == a],
        )

    def line_xor(value, m):
        return lax.ppermute(value, "dp", [(i, i ^ (2 * m)) for i in range(n)])

    def pair(value, where):
        return lax.ppermute(value, "dp", [(i, i ^ 1) for i in range(n) if i % CELL // 2 in where])

    def swap(value, m):
        return lax.ppermute(value, "tensor", [(i, i ^ m) for i in range(4)])

    def gather_cell(own):
        size = own.shape[0]
        half = size // 2
        near = line(own, NEIGHBOURS)
        mid = line(own, MIDDLE)
        own_x = pair(own, ALL)
        mid_far = line(near, MIDDLE)
        end_far = line(mid, OUTWARD)
        near_x_mid = line(own_x, INWARD)
        near_x_end = pair(near, ENDS)
        mid_x = pair(mid, MIDS)
        end_last = line(mid_far, OUTWARD)
        end_far_x = pair(end_far, ENDS)
        mid_far_x = pair(mid_far, MIDS)
        last_x_low = pair(end_last[:half], ENDS)
        last_x_high = line(mid_far_x[half:], OUTWARD)
        out = jnp.zeros((CELL * size,) + own.shape[1:], own.dtype)

        def put(out, value, at_z, at_x, shift=0):
            return lax.dynamic_update_slice(out, value, ((at_z * 2 + at_x) * size + shift, 0))

        third = jnp.where(z < 2, 2, 1)
        fourth = jnp.where(z < 2, 3, 0)
        out = put(out, own, z, x)
        out = put(out, own_x, z, 1 - x)
        out = put(out, near, z ^ 1, x)
        out = put(out, jnp.where(ends, near_x_end, near_x_mid), z ^ 1, 1 - x)
        out = put(out, jnp.where(ends, end_far, mid), third, x)
        out = put(out, jnp.where(ends, end_far_x, mid_x), third, 1 - x)
        out = put(out, jnp.where(ends, end_last, mid_far), fourth, x)
        out = put(out, jnp.where(ends, last_x_low, mid_far_x[:half]), fourth, 1 - x)
        return put(out, jnp.where(ends, last_x_high, mid_far_x[half:]), fourth, 1 - x, half)

    d_out_all = gather_cell(lax.dynamic_slice(d_out, (0, t * cols), (tokens, cols)))

    weight = master.astype(BF16)
    if outer > 1:
        weight = lax.all_gather(weight, "dp", axis=0, tiled=True, axis_index_groups=same_pair)
    weight_cols = [
        lax.dynamic_slice(weight, (0, (t ^ m) * cols), (part, cols)) for m in range(4)
    ]
    weight_rows = jnp.concatenate(
        [weight_cols[0]] + [swap(weight_cols[m], m) for m in (1, 2, 3)], axis=0
    )

    gate_f = gate.astype(F32)
    up_f = up_proj.astype(F32)
    silu_gate = jax.nn.silu(gate_f)
    hidden = (silu_gate * up_f).astype(BF16)
    hidden = hidden.reshape(tokens, outer, CELL, rows).transpose(2, 0, 1, 3).reshape(4, 2, tokens, part)
    kept = lax.dynamic_index_in_dim(hidden, x, 1, keepdims=False)
    given = lax.dynamic_index_in_dim(hidden, 1 - x, 1, keepdims=False)
    came = pair(given, ALL)
    first = jnp.where(x == 0, kept, came)
    second = jnp.where(x == 0, came, kept)
    both = jnp.concatenate([first, second], axis=1)
    blocks = [lax.dynamic_index_in_dim(both, z ^ m, 0, keepdims=False) for m in range(4)]
    blocks = [blocks[0]] + [line_xor(blocks[m], m) for m in (1, 2, 3)]
    hidden_mine = jnp.zeros((CELL * tokens, part), BF16)
    for m in range(4):
        hidden_mine = lax.dynamic_update_slice(hidden_mine, blocks[m], ((z ^ m) * 2 * tokens, 0))
    hidden_two = jnp.concatenate([hidden_mine, swap(hidden_mine, 2)], axis=1)
    hidden_far = swap(hidden_two, 1)
    grad_here = jnp.concatenate(
        [
            lax.dot_general(h, d_out_all, (((0,), (0,)), ((), ())), preferred_element_type=F32)
            for h in (hidden_two, hidden_far)
        ],
        axis=0,
    ).reshape(4, part, cols)
    if outer > 1:
        grad_here = lax.psum_scatter(
            grad_here.reshape(4, outer, rows, cols),
            "dp",
            scatter_dimension=1,
            axis_index_groups=same_pair,
        )
    total = jnp.broadcast_to(jnp.sum(grad_here * grad_here), (8, 128))
    for m in (1, 2):
        total = total + swap(total, m)
    step = 1
    while step < n:
        total = total + lax.ppermute(total, "dp", [(i, i ^ step) for i in range(n)])
        step *= 2
    total = total[0, 0]

    grad = jnp.zeros((rows, D), F32)
    pieces = (grad_here[0], swap(grad_here[2], 1), swap(grad_here[1], 2), swap(grad_here[3], 3))
    for m in range(4):
        grad = lax.dynamic_update_slice(grad, pieces[m], (0, (t ^ m) * cols))

    factor = 1.0 / jnp.sqrt(total / (FF * D) + 1e-06)
    clipped = grad * factor
    moment_one_next = 0.9 * moment_one + 0.1 * clipped
    moment_two_next = 0.95 * moment_two + 0.05 * clipped * clipped
    master_next = master - 0.003 * (
        moment_one_next / (jnp.sqrt(moment_two_next) + 1e-08) + 0.1 * master
    )
    shard_next = master_next.astype(BF16)
    if outer > 1:
        shard_next = lax.all_gather(shard_next, "dp", axis=0, tiled=True, axis_index_groups=same_pair)
    weight_next = gather_cell(shard_next)
    if outer > 1:
        weight_next = (
            weight_next.reshape(CELL, outer, rows, D).transpose(1, 0, 2, 3).reshape(width, D)
        )

    def d_hidden_part(weight_part):
        return lax.dot_general(
            d_out_all, weight_part, (((1,), (1,)), ((), ())), preferred_element_type=F32
        )

    weight_rows = weight_rows.reshape(4, part, cols)
    keep = d_hidden_part(weight_rows[0::2].reshape(2 * part, cols))
    give = d_hidden_part(weight_rows[1::2].reshape(2 * part, cols))
    keep = keep + swap(give, 1)
    d_mine = (keep[:, :part] + swap(keep[:, part:], 2)).astype(BF16)
    d_mine = d_mine.reshape(4, 2 * tokens, part)
    blocks = [lax.dynamic_index_in_dim(d_mine, z ^ m, 0, keepdims=False) for m in range(4)]
    blocks = [blocks[0]] + [line_xor(blocks[m], m) for m in (1, 2, 3)]
    mine = jnp.zeros((4, 2 * tokens, part), BF16)
    for m in range(4):
        mine = lax.dynamic_update_slice(mine, blocks[m][None], (z ^ m, 0, 0))
    mine = mine.reshape(4, 2, tokens, part)
    kept = lax.dynamic_index_in_dim(mine, x, 1, keepdims=False)
    came = pair(lax.dynamic_index_in_dim(mine, 1 - x, 1, keepdims=False), ALL)
    first = jnp.where(x == 0, kept, came)
    second = jnp.where(x == 0, came, kept)
    d_hidden = jnp.stack([first, second], axis=1)
    d_hidden = (
        d_hidden.reshape(CELL, tokens, outer, rows).transpose(1, 2, 0, 3).reshape(tokens, width)
    ).astype(F32)

    up_grad = (d_hidden * silu_gate).astype(BF16)
    sigm = jax.nn.sigmoid(gate_f)
    gate_grad = (d_hidden * up_f * sigm * (1.0 + gate_f * (1.0 - sigm))).astype(BF16)
    return (gate_grad, up_grad, master_next, moment_one_next, moment_two_next, weight_next)


def solution(mesh):
    n = mesh.shape["dp"]
    placed = (
        P("dp", None),
        P("dp", "tensor"),
        P("dp", "tensor"),
        P(("tensor", "dp"), None),
        P(("tensor", "dp"), None),
        P(("tensor", "dp"), None),
    )
    return jax.shard_map(
        lambda *args: on_device(n, *args),
        mesh=mesh,
        in_specs=placed,
        out_specs=(
            P("dp", "tensor"),
            P("dp", "tensor"),
            P(("tensor", "dp"), None),
            P(("tensor", "dp"), None),
            P(("tensor", "dp"), None),
            P("tensor", None),
        ),
        check_vma=False,
    )
```

time: 488 us -> 283 us (0.58)
  waiting for transfers between devices: 403 us -> 125 us
  starting transfers between devices: 0.12 us -> 81.9 us
  blocking collectives: 39.6 us -> 0 us
  local copies, waits for them, and re-layouts: 7.3 us -> 38.9 us
  other arithmetic: 9.02 us -> 30.2 us
  between operations: 14.5 us -> 1.89 us
  matrix products: 13.6 us -> 4.17 us
    reduce_scatter x1 -> x0, waiting for transfers between devices: 210 us -> none  [on_device(): grad = lax.psum_scatter(partial_term, 'dp', scatter_dimension=0, tiled=True)]
    all_gather x2 -> x0, waiting for transfers between devices: 193 us -> none  [the longest x1 98.4 us: on_device(): lax.all_gather(weight, 'dp', axis=0, tiled=True)]
    ppermute x0 -> x49, waiting for transfers between devices: none -> 125 us  [the longest x12 43 us: swap(): return lax.ppermute(value, 'tensor', [(i, i ^ m) for i in range(4)])]
    ppermute x0 -> x49, starting transfers between devices: none -> 81.9 us  [the longest x14 29.8 us: line(): lax.ppermute(value, 'dp', [(i, i - i % CELL + b * 2 + i % 2) for i in ran...]
    psum x1 -> x0, blocking collectives: 39.6 us -> none  [on_device(): total = lax.psum(local_squares, ('dp', 'tensor'))]
    dynamic_update_slice x0 -> x12, other arithmetic: none -> 15.4 us  [the longest x11 14.5 us: put(): lax.dynamic_update_slice(out, value, ((at_z * 2 + at_x) * size + shift, 0))]
    dynamic_update_slice x0 -> x14, local copies, waits for them, and re-layouts: none -> 11.1 us  [the longest x5 5.73 us: put(): lax.dynamic_update_slice(out, value, ((at_z * 2 + at_x) * size + shift, 0))]
    dot_general x2 -> x4, matrix products: 13.6 us -> 4.17 us  [the longest x2 2.14 us: d_hidden_part(): lax.dot_general(d_out_all, weight_part, (((1,), (1,)), ((), ())), preferr...]
  transfers between devices with their start and end apart: 3 -> 49, of which waited for: 3 -> 25; matrix products, arithmetic and copies ran while one was open for 1% -> 13% of each run, Pallas kernels for 0% -> 0%
where the time goes in v1:
time: 283 us; the launch traced here: 282 us
  waiting for transfers between devices  125 us (44%)
  starting transfers between devices  81.9 us (29%)
  local copies, waits for them, and re-layouts  38.9 us (14%)
  other arithmetic  30.2 us (11%)
  matrix products  4.17 us (1%)
    ppermute x12, waiting for transfers between devices, swap(): return lax.ppermute(value, 'tensor', [(i, i ^ m) for i in range(4)])  43 us
    ppermute x14, waiting for transfers between devices, line(): lax.ppermute(value, 'dp', [(i, i - i % CELL + b * 2 + i % 2) for i in ran...  41.3 us
    ppermute x14, starting transfers between devices, line(): lax.ppermute(value, 'dp', [(i, i - i % CELL + b * 2 + i % 2) for i in ran...  29.8 us
    ppermute x14, starting transfers between devices, pair(): lax.ppermute(value, 'dp', [(i, i ^ 1) for i in range(n) if i % CELL // 2...  25.8 us
    ppermute x14, waiting for transfers between devices, pair(): lax.ppermute(value, 'dp', [(i, i ^ 1) for i in range(n) if i % CELL // 2...  20.7 us
    dynamic_update_slice x11, other arithmetic, put(): lax.dynamic_update_slice(out, value, ((at_z * 2 + at_x) * size + shift, 0))  14.5 us
    ppermute x6, waiting for transfers between devices, line_xor(): return lax.ppermute(value, 'dp', [(i, i ^ 2 * m) for i in range(n)])  13.4 us
    ppermute x12, starting transfers between devices, swap(): return lax.ppermute(value, 'tensor', [(i, i ^ m) for i in range(4)])  9.77 us
  transfers between devices with their start and end apart: 49, of which 25 were waited for; matrix products, arithmetic and copies ran while one was open for 13% of the time, Pallas kernels for 0%

profile of v1, /device:TPU:0, one launch (start us, length us, event | category | flops | bytes accessed | tf_op | source)
XLA Modules:
  0.0 281.6 jit_solution(9622281663133052531)
XLA Ops:
  0.9 1.8 constant_dynamic-update-slice_fusion.11
  2.7 2.9 %collective-permute-start = (bf16[256,768]{1,0:T(8,128)(2,1)}, bf16[256,768]{1,0:T(8,128)(2,1)}, u32[]{:S(2)}, u32[]{:S(2)}) collective-permute-start(bf16[256,768]{1,0:T(8,128)(2,1)} %get-tuple-element.18), channel_id=1, source_target_pairs={{0,4},{4,0},{8,12},{12,8},{16,20},{20,16},{24,28},{28,24},{1,5},{5... | collective-permute-start | bytes 1179656 | tf_op jit(solution)/shard_map/ppermute | solution.py:42
  5.6 1.6 collective-permute-start.1
  7.2 1.4 collective-permute-start.4
  8.6 2.4 convert_element_type.36
  12.4 1.6 collective-permute-start.14
  15.1 1.4 collective-permute-done.1
  16.5 1.4 collective-permute-start.8
  17.9 2.3 collective-permute-done.14
  20.3 2.4 collective-permute-start.2
  24.0 6.1 %collective-permute-start.3 = (bf16[256,768]{1,0:T(8,128)(2,1)}, bf16[256,768]{1,0:T(8,128)(2,1)}, u32[]{:S(2)}, u32[]{:S(2)}) collective-permute-start(bf16[256,768]{1,0:T(8,128)(2,1)} %collective-permute-done), channel_id=1, source_target_pairs={{0,8},{4,12},{24,16},{28,20},{1,9},{5,13},{25,17},{29,21},{2,10},{... | collective-permute-start | bytes 1179656 | tf_op jit(solution)/shard_map/ppermute | solution.py:32
  36.0 3.4 %collective-permute-start.6 = (bf16[256,768]{1,0:T(8,128)(2,1)}, bf16[256,768]{1,0:T(8,128)(2,1)S(1)}, u32[]{:S(2)}, u32[]{:S(2)}) collective-permute-start(bf16[256,768]{1,0:T(8,128)(2,1)} %collective-permute-done.5), channel_id=1, source_target_pairs={{0,4},{4,0},{24,28},{28,24},{1,5},{5,1},{25,29},{29,25},{2,6},{6,2... | collective-permute-start | bytes 1179656 | tf_op jit(solution)/shard_map/ppermute | solution.py:42
  41.7 4.4 %collective-permute-done.9 = bf16[256,768]{1,0:T(8,128)(2,1)S(1)} collective-permute-done((bf16[256,768]{1,0:T(8,128)(2,1)}, bf16[256,768]{1,0:T(8,128)(2,1)S(1)}, u32[]{:S(2)}, u32[]{:S(2)}) %collective-permute-start.9) | collective-permute-done | bytes 393248 | tf_op jit(solution)/shard_map/ppermute | solution.py:32
  46.1 2.9 %collective-permute-start.10 = (bf16[128,768]{1,0:T(8,128)(2,1)S(1)}, bf16[128,768]{1,0:T(8,128)(2,1)S(1)}, u32[]{:S(2)}, u32[]{:S(2)}) collective-permute-start(bf16[128,768]{1,0:T(8,128)(2,1)S(1)} %slice.70), channel_id=1, source_target_pairs={{0,4},{4,0},{24,28},{28,24},{1,5},{5,1},{25,29},{29,25},{2,6},{6,2... | collective-permute-start | bytes 589832 | tf_op jit(solution)/shard_map/ppermute | solution.py:42
  49.2 4.4 %collective-permute-done.10 = bf16[128,768]{1,0:T(8,128)(2,1)S(1)} collective-permute-done((bf16[128,768]{1,0:T(8,128)(2,1)S(1)}, bf16[128,768]{1,0:T(8,128)(2,1)S(1)}, u32[]{:S(2)}, u32[]{:S(2)}) %collective-permute-start.10) | collective-permute-done | bytes 196640 | tf_op jit(solution)/shard_map/ppermute | solution.py:42
  53.7 1.5 collective-permute-start.12
  55.2 6.0 %collective-permute-done.12 = bf16[128,768]{1,0:T(8,128)(2,1)S(1)} collective-permute-done((bf16[128,768]{1,0:T(8,128)(2,1)S(1)}, bf16[128,768]{1,0:T(8,128)(2,1)S(1)}, u32[]{:S(2)}, u32[]{:S(2)}) %collective-permute-start.12) | collective-permute-done | bytes 196640 | tf_op jit(solution)/shard_map/ppermute | solution.py:32
  62.4 4.1 %collective-permute-done.16 = f32[2048,256]{1,0:T(8,128)S(1)} collective-permute-done((f32[2048,256]{1,0:T(8,128)S(1)}, f32[2048,256]{1,0:T(8,128)S(1)}, u32[]{:S(2)}, u32[]{:S(2)}) %collective-permute-start.16) | collective-permute-done | bytes 2097184 | tf_op jit(solution)/shard_map/ppermute | solution.py:45
  70.0 1.5 collective-permute-start.17
  71.6 24.0 %collective-permute-done.17 = f32[2048,128]{1,0:T(8,128)} collective-permute-done((f32[2048,128]{1,0:T(8,128)}, f32[2048,128]{1,0:T(8,128)}, u32[]{:S(2)}, u32[]{:S(2)}) %collective-permute-start.17) | collective-permute-done | bytes 1048608 | tf_op jit(solution)/shard_map/ppermute | solution.py:45
  95.6 1.6 fusion.10
  98.8 2.5 collective-permute-start.19
  101.3 1.9 collective-permute-start.20
  103.2 2.4 collective-permute-done.18
  106.2 5.2 %collective-permute-done.19 = bf16[512,128]{1,0:T(8,128)(2,1)S(1)} collective-permute-done((bf16[512,128]{1,0:T(8,128)(2,1)S(1)}, bf16[512,128]{1,0:T(8,128)(2,1)S(1)}, u32[]{:S(2)}, u32[]{:S(2)}) %collective-permute-start.19) | collective-permute-done | bytes 131104 | tf_op jit(solution)/shard_map/ppermute | solution.py:39
  112.8 1.7 dynamic-slice_bitcast_fusion.1
  115.6 2.0 copy.18
  117.6 2.0 copy.19
  119.6 1.4 collective-permute-done.21
  123.2 2.5 copy.17
  125.7 3.4 %fusion.11 = (bf16[256,1024]{0,1:T(8,128)(2,1)}, bf16[256,1024]{0,1:T(8,128)(2,1)}, bf16[256,1024]{0,1:T(8,128)(2,1)}) fusion(f32[256,1,8,128]{0,3,2,1:T(8,128)} %copy.17, bf16[256,1024]{0,1:T(8,128)(2,1)} %copy.19, bf16[256,1024]{0,1:T(8,128)(2,1)} %copy.18), kind=kLoop, calls=%fused_computation.24 | loop fusion | flops 4456448 | bytes 3670016 | tf_op jit(solution)/shard_map/convert_element_type | solution.py:180
  129.1 2.0 copy.20
  133.3 5.3 %collective-permute-done.22 = bf16[4,256,128]{2,1,0:T(8,128)(2,1)S(1)} collective-permute-done((bf16[4,256,128]{2,1,0:T(8,128)(2,1)S(1)}, bf16[4,256,128]{2,1,0:T(8,128)(2,1)S(1)}, u32[]{:S(2)}, u32[]{:S(2)}) %collective-permute-start.22) | collective-permute-done | bytes 262176 | tf_op jit(solution)/shard_map/ppermute | solution.py:42
  141.0 1.5 collective-permute-start.23
  143.5 1.9 collective-permute-start.25
  146.4 1.8 collective-permute-done.23
  148.1 4.0 %collective-permute-done.24 = bf16[512,128]{1,0:T(8,128)(2,1)S(1)} collective-permute-done((bf16[512,128]{1,0:T(8,128)(2,1)}, bf16[512,128]{1,0:T(8,128)(2,1)S(1)}, u32[]{:S(2)}, u32[]{:S(2)}) %collective-permute-start.24) | collective-permute-done | bytes 131104 | tf_op jit(solution)/shard_map/ppermute | solution.py:39
  152.2 1.6 collective-permute-start.26
  153.8 7.7 %collective-permute-done.26 = bf16[2048,128]{1,0:T(8,128)(2,1)S(1)} collective-permute-done((bf16[2048,128]{1,0:T(8,128)(2,1)S(1)}, bf16[2048,128]{1,0:T(8,128)(2,1)S(1)}, u32[]{:S(2)}, u32[]{:S(2)}) %collective-permute-start.26) | collective-permute-done | bytes 524320 | tf_op jit(solution)/shard_map/ppermute | solution.py:45
  164.8 1.5 collective-permute-start.29
  172.5 4.3 %collective-permute-done.32 = f32[8,128]{1,0:T(8,128)S(1)} collective-permute-done((f32[8,128]{1,0:T(8,128)S(1)}, f32[8,128]{1,0:T(8,128)S(1)}, u32[]{:S(2)}, u32[]{:S(2)}) %collective-permute-start.32) | collective-permute-done | bytes 4128 | tf_op jit(solution)/shard_map/ppermute | solution.py:45
  178.5 2.6 collective-permute-done.33
  181.1 4.2 %collective-permute-start.34 = (f32[8,128]{1,0:T(8,128)S(1)}, f32[8,128]{1,0:T(8,128)S(1)}, u32[]{:S(2)}, u32[]{:S(2)}) collective-permute-start(f32[8,128]{1,0:T(8,128)S(1)} %add.254), channel_id=1, source_target_pairs={{0,8},{4,12},{8,0},{12,4},{16,24},{20,28},{24,16},{28,20},{1,9},{5... | collective-permute-start | bytes 12296 | tf_op jit(solution)/shard_map/ppermute | solution.py:129
  185.3 1.6 collective-permute-done.34
  186.9 2.5 collective-permute-start.35
  189.4 2.0 collective-permute-done.35
  193.4 1.8 constant_dynamic-update-slice_fusion.4
  196.0 3.6 %broadcast_in_dim.36 = bf16[1024,3072]{1,0:T(8,128)(2,1)} broadcast(bf16[]{:T(256)} %constant.106.clone.1), dimensions={} | broadcast | bytes 6291458 | tf_op jit(solution)/shard_map/broadcast_in_dim | solution.py:63
  199.9 4.7 %constant_dynamic-update-slice_fusion.2 = (bf16[1024,3072]{1,0:T(8,128)(2,1)}, bf16[128,3072]{1,0:T(8,128)(2,1)S(1)}, f32[128,3072]{1,0:T(8,128)}, f32[128,3072]{1,0:T(8,128)}, f32[128,3072]{1,0:T(8,128)}) fusion(bf16[1024,3072]{1,0:T(8,128)(2,1)} %broadcast_in_dim.36, s32[]{:T(128)S(6)} %select_n.262, f32[128,3072]{1,0:T(8,128)S(1)} %copy-done.1, ...), kind=kLoop, calls=%fused_computation.76 | loop fusion | flops 5898240 | bytes 12583428 | tf_op jit(solution)/shard_map/dynamic_update_slice | solution.py:66
  204.5 2.0 collective-permute-start.37
  206.5 1.5 collective-permute-start.40
  209.0 11.8 %collective-permute-done.37 = bf16[128,3072]{1,0:T(8,128)(2,1)S(1)} collective-permute-done((bf16[128,3072]{1,0:T(8,128)(2,1)S(1)}, bf16[128,3072]{1,0:T(8,128)(2,1)S(1)}, u32[]{:S(2)}, u32[]{:S(2)}) %collective-permute-start.37) | collective-permute-done | bytes 786464 | tf_op jit(solution)/shard_map/ppermute | solution.py:32
  220.8 1.6 collective-permute-start.44
  222.4 3.0 %collective-permute-start.38 = (bf16[128,3072]{1,0:T(8,128)(2,1)S(1)}, bf16[128,3072]{1,0:T(8,128)(2,1)}, u32[]{:S(2)}, u32[]{:S(2)}) collective-permute-start(bf16[128,3072]{1,0:T(8,128)(2,1)S(1)} %collective-permute-done.37), channel_id=1, source_target_pairs={{0,4},{4,0},{24,28},{28,24},{1,5},{5,1},{25,29},{29,25},{2,6},{6,2... | collective-permute-start | bytes 2359304 | tf_op jit(solution)/shard_map/ppermute | solution.py:42
  226.7 6.3 %collective-permute-start.39 = (bf16[128,3072]{1,0:T(8,128)(2,1)S(1)}, bf16[128,3072]{1,0:T(8,128)(2,1)}, u32[]{:S(2)}, u32[]{:S(2)}) collective-permute-start(bf16[128,3072]{1,0:T(8,128)(2,1)S(1)} %collective-permute-done.36), channel_id=1, source_target_pairs={{0,8},{4,12},{24,16},{28,20},{1,9},{5,13},{25,17},{29,21},{2,10},{... | collective-permute-start | bytes 2359304 | tf_op jit(solution)/shard_map/ppermute | solution.py:32
  236.9 3.8 %collective-permute-done.38 = bf16[128,3072]{1,0:T(8,128)(2,1)} collective-permute-done((bf16[128,3072]{1,0:T(8,128)(2,1)S(1)}, bf16[128,3072]{1,0:T(8,128)(2,1)}, u32[]{:S(2)}, u32[]{:S(2)}) %collective-permute-start.38) | collective-permute-done | bytes 786464 | tf_op jit(solution)/shard_map/ppermute | solution.py:42
  241.5 3.6 %collective-permute-done.41 = bf16[128,3072]{1,0:T(8,128)(2,1)} collective-permute-done((bf16[128,3072]{1,0:T(8,128)(2,1)}, bf16[128,3072]{1,0:T(8,128)(2,1)}, u32[]{:S(2)}, u32[]{:S(2)}) %collective-permute-start.41) | collective-permute-done | bytes 786464 | tf_op jit(solution)/shard_map/ppermute | solution.py:32
  245.0 2.4 collective-permute-start.42
  247.4 2.2 select_dynamic-update-slice_fusion.3
  249.6 2.2 select_dynamic-update-slice_fusion.2
  251.8 7.6 %collective-permute-done.45 = bf16[128,3072]{1,0:T(8,128)(2,1)S(1)} collective-permute-done((bf16[128,3072]{1,0:T(8,128)(2,1)}, bf16[128,3072]{1,0:T(8,128)(2,1)S(1)}, u32[]{:S(2)}, u32[]{:S(2)}) %collective-permute-start.45) | collective-permute-done | bytes 786464 | tf_op jit(solution)/shard_map/ppermute | solution.py:32
  259.5 2.8 %collective-permute-start.46 = (bf16[64,3072]{1,0:T(8,128)(2,1)S(1)}, bf16[64,3072]{1,0:T(8,128)(2,1)S(1)}, u32[]{:S(2)}, u32[]{:S(2)}) collective-permute-start(bf16[64,3072]{1,0:T(8,128)(2,1)S(1)} %slice.79), channel_id=1, source_target_pairs={{0,4},{4,0},{24,28},{28,24},{1,5},{5,1},{25,29},{29,25},{2,6},{6,2... | collective-permute-start | bytes 1179656 | tf_op jit(solution)/shard_map/ppermute | solution.py:42
  264.5 5.7 %collective-permute-done.46 = bf16[64,3072]{1,0:T(8,128)(2,1)S(1)} collective-permute-done((bf16[64,3072]{1,0:T(8,128)(2,1)S(1)}, bf16[64,3072]{1,0:T(8,128)(2,1)S(1)}, u32[]{:S(2)}, u32[]{:S(2)}) %collective-permute-start.46) | collective-permute-done | bytes 393248 | tf_op jit(solution)/shard_map/ppermute | solution.py:42
  274.3 6.4 %collective-permute-done.48 = bf16[64,3072]{1,0:T(8,128)(2,1)S(1)} collective-permute-done((bf16[64,3072]{1,0:T(8,128)(2,1)S(1)}, bf16[64,3072]{1,0:T(8,128)(2,1)S(1)}, u32[]{:S(2)}, u32[]{:S(2)}) %collective-permute-start.48) | collective-permute-done | bytes 393248 | tf_op jit(solution)/shard_map/ppermute | solution.py:32
  (123 shorter events, 57.8 us)
Async XLA Ops:
  2.7 21.3 %collective-permute-start = (bf16[256,768]{1,0:T(8,128)(2,1)}, bf16[256,768]{1,0:T(8,128)(2,1)}, u32[]{:S(2)}, u32[]{:S(2)}) collective-permute-start(bf16[256,768]{1,0:T(8,128)(2,1)} %get-tuple-element.18), channel_id=1, source_target_pairs={{0,4},{4,0},{8,12},{12,8},{16,20},{20,16},{24,28},{28,24},{1,5},{5... | collective-permute-start | bytes 1179656 | tf_op jit(solution)/shard_map/ppermute | solution.py:42
  5.6 10.9 %collective-permute-start.1 = (bf16[256,768]{1,0:T(8,128)(2,1)}, bf16[256,768]{1,0:T(8,128)(2,1)}, u32[]{:S(2)}, u32[]{:S(2)}) collective-permute-start(bf16[256,768]{1,0:T(8,128)(2,1)} %get-tuple-element.18), channel_id=1, source_target_pairs={{0,8},{4,12},{8,0},{12,4},{16,24},{20,28},{24,16},{28,20},{1,9},{5... | collective-permute-start | bytes 1179656 | tf_op jit(solution)/shard_map/ppermute | solution.py:32
  7.2 15.5 %collective-permute-start.4 = (bf16[256,768]{1,0:T(8,128)(2,1)}, bf16[256,768]{1,0:T(8,128)(2,1)}, u32[]{:S(2)}, u32[]{:S(2)}) collective-permute-start(bf16[256,768]{1,0:T(8,128)(2,1)} %get-tuple-element.18), channel_id=1, source_target_pairs={{8,16},{12,20},{16,8},{20,12},{9,17},{13,21},{17,9},{21,13},{10,18... | collective-permute-start | bytes 1179656 | tf_op jit(solution)/shard_map/ppermute | solution.py:32
  12.3 1.7 collective-permute-start.13
  12.4 7.9 %collective-permute-start.14 = (bf16[128,768]{1,0:T(8,128)(2,1)S(1)}, bf16[128,768]{1,0:T(8,128)(2,1)}, u32[]{:S(2)}, u32[]{:S(2)}) collective-permute-start(bf16[128,768]{1,0:T(8,128)(2,1)S(1)} %get-tuple-element.36), channel_id=1, source_target_pairs={{0,2},{1,3},{2,0},{3,1},{4,6},{5,7},{6,4},{7,5},{8,10},{9,11},{10,... | collective-permute-start | bytes 589832 | tf_op jit(solution)/shard_map/ppermute | solution.py:45
  14.0 1.1 copy-start.8
  14.0 16.1 %collective-permute-start.15 = (bf16[128,768]{1,0:T(8,128)(2,1)S(1)}, bf16[128,768]{1,0:T(8,128)(2,1)}, u32[]{:S(2)}, u32[]{:S(2)}) collective-permute-start(bf16[128,768]{1,0:T(8,128)(2,1)S(1)} %get-tuple-element.35), channel_id=1, source_target_pairs={{0,3},{1,2},{2,1},{3,0},{4,7},{5,6},{6,5},{7,4},{8,11},{9,10},{10,... | collective-permute-start | bytes 589832 | tf_op jit(solution)/shard_map/ppermute | solution.py:45
  16.5 17.5 %collective-permute-start.8 = (bf16[256,768]{1,0:T(8,128)(2,1)}, bf16[256,768]{1,0:T(8,128)(2,1)}, u32[]{:S(2)}, u32[]{:S(2)}) collective-permute-start(bf16[256,768]{1,0:T(8,128)(2,1)} %collective-permute-done.1), channel_id=1, source_target_pairs={{8,16},{12,20},{16,8},{20,12},{9,17},{13,21},{17,9},{21,13},{10,18... | collective-permute-start | bytes 1179656 | tf_op jit(solution)/shard_map/ppermute | solution.py:32
  20.3 15.1 %collective-permute-start.2 = (bf16[256,768]{1,0:T(8,128)(2,1)}, bf16[256,768]{1,0:T(8,128)(2,1)}, u32[]{:S(2)}, u32[]{:S(2)}) collective-permute-start(bf16[256,768]{1,0:T(8,128)(2,1)} %collective-permute-done.1), channel_id=1, source_target_pairs={{0,4},{4,0},{24,28},{28,24},{1,5},{5,1},{25,29},{29,25},{2,6},{6,2... | collective-permute-start | bytes 1179656 | tf_op jit(solution)/shard_map/ppermute | solution.py:42
  22.7 13.3 %collective-permute-start.5 = (bf16[256,768]{1,0:T(8,128)(2,1)}, bf16[256,768]{1,0:T(8,128)(2,1)}, u32[]{:S(2)}, u32[]{:S(2)}) collective-permute-start(bf16[256,768]{1,0:T(8,128)(2,1)} %collective-permute-done.4), channel_id=1, source_target_pairs={{8,0},{12,4},{16,24},{20,28},{9,1},{13,5},{17,25},{21,29},{10,2},{... | collective-permute-start | bytes 1179656 | tf_op jit(solution)/shard_map/ppermute | solution.py:32
  24.0 15.4 %collective-permute-start.3 = (bf16[256,768]{1,0:T(8,128)(2,1)}, bf16[256,768]{1,0:T(8,128)(2,1)}, u32[]{:S(2)}, u32[]{:S(2)}) collective-permute-start(bf16[256,768]{1,0:T(8,128)(2,1)} %collective-permute-done), channel_id=1, source_target_pairs={{0,8},{4,12},{24,16},{28,20},{1,9},{5,13},{25,17},{29,21},{2,10},{... | collective-permute-start | bytes 1179656 | tf_op jit(solution)/shard_map/ppermute | solution.py:32
  31.3 17.7 %collective-permute-start.7 = (bf16[256,768]{1,0:T(8,128)(2,1)}, bf16[256,768]{1,0:T(8,128)(2,1)S(1)}, u32[]{:S(2)}, u32[]{:S(2)}) collective-permute-start(bf16[256,768]{1,0:T(8,128)(2,1)} %collective-permute-done.4), channel_id=1, source_target_pairs={{8,12},{12,8},{16,20},{20,16},{9,13},{13,9},{17,21},{21,17},{10,14... | collective-permute-start | bytes 1179656 | tf_op jit(solution)/shard_map/ppermute | solution.py:42
  34.0 12.0 %collective-permute-start.9 = (bf16[256,768]{1,0:T(8,128)(2,1)}, bf16[256,768]{1,0:T(8,128)(2,1)S(1)}, u32[]{:S(2)}, u32[]{:S(2)}) collective-permute-start(bf16[256,768]{1,0:T(8,128)(2,1)} %collective-permute-done.8), channel_id=1, source_target_pairs={{8,0},{12,4},{16,24},{20,28},{9,1},{13,5},{17,25},{21,29},{10,2},{... | collective-permute-start | bytes 1179656 | tf_op jit(solution)/shard_map/ppermute | solution.py:32
  35.3 13.9 %collective-permute-start.11 = (bf16[256,768]{1,0:T(8,128)(2,1)}, bf16[256,768]{1,0:T(8,128)(2,1)S(1)}, u32[]{:S(2)}, u32[]{:S(2)}) collective-permute-start(bf16[256,768]{1,0:T(8,128)(2,1)} %collective-permute-done.8), channel_id=1, source_target_pairs={{8,12},{12,8},{16,20},{20,16},{9,13},{13,9},{17,21},{21,17},{10,14... | collective-permute-start | bytes 1179656 | tf_op jit(solution)/shard_map/ppermute | solution.py:42
  36.0 12.9 %collective-permute-start.6 = (bf16[256,768]{1,0:T(8,128)(2,1)}, bf16[256,768]{1,0:T(8,128)(2,1)S(1)}, u32[]{:S(2)}, u32[]{:S(2)}) collective-permute-start(bf16[256,768]{1,0:T(8,128)(2,1)} %collective-permute-done.5), channel_id=1, source_target_pairs={{0,4},{4,0},{24,28},{28,24},{1,5},{5,1},{25,29},{29,25},{2,6},{6,2... | collective-permute-start | bytes 1179656 | tf_op jit(solution)/shard_map/ppermute | solution.py:42
  46.1 7.6 %collective-permute-start.10 = (bf16[128,768]{1,0:T(8,128)(2,1)S(1)}, bf16[128,768]{1,0:T(8,128)(2,1)S(1)}, u32[]{:S(2)}, u32[]{:S(2)}) collective-permute-start(bf16[128,768]{1,0:T(8,128)(2,1)S(1)} %slice.70), channel_id=1, source_target_pairs={{0,4},{4,0},{24,28},{28,24},{1,5},{5,1},{25,29},{29,25},{2,6},{6,2... | collective-permute-start | bytes 589832 | tf_op jit(solution)/shard_map/ppermute | solution.py:42
  53.7 7.6 %collective-permute-start.12 = (bf16[128,768]{1,0:T(8,128)(2,1)S(1)}, bf16[128,768]{1,0:T(8,128)(2,1)S(1)}, u32[]{:S(2)}, u32[]{:S(2)}) collective-permute-start(bf16[128,768]{1,0:T(8,128)(2,1)S(1)} %get-tuple-element.45), channel_id=1, source_target_pairs={{8,0},{12,4},{16,24},{20,28},{9,1},{13,5},{17,25},{21,29},{10,2},{... | collective-permute-start | bytes 589832 | tf_op jit(solution)/shard_map/ppermute | solution.py:32
  62.3 4.2 %collective-permute-start.16 = (f32[2048,256]{1,0:T(8,128)S(1)}, f32[2048,256]{1,0:T(8,128)S(1)}, u32[]{:S(2)}, u32[]{:S(2)}) collective-permute-start(f32[2048,256]{1,0:T(8,128)S(1)} %fusion.32), channel_id=1, source_target_pairs={{0,1},{1,0},{2,3},{3,2},{4,5},{5,4},{6,7},{7,6},{8,9},{9,8},{10,11... | collective-permute-start | bytes 6291464 | tf_op jit(solution)/shard_map/ppermute | solution.py:45
  67.7 1.3 copy-start
  70.0 25.5 %collective-permute-start.17 = (f32[2048,128]{1,0:T(8,128)}, f32[2048,128]{1,0:T(8,128)}, u32[]{:S(2)}, u32[]{:S(2)}) collective-permute-start(f32[2048,128]{1,0:T(8,128)} %slice.74), channel_id=1, source_target_pairs={{0,2},{1,3},{2,0},{3,1},{4,6},{5,7},{6,4},{7,5},{8,10},{9,11},{10,... | collective-permute-start | bytes 3145736 | tf_op jit(solution)/shard_map/ppermute | solution.py:45
  98.0 0.8 copy-start.5
  98.8 6.8 %collective-permute-start.18 = (bf16[512,128]{1,0:T(8,128)(2,1)}, bf16[512,128]{1,0:T(8,128)(2,1)S(1)}, u32[]{:S(2)}, u32[]{:S(2)}) collective-permute-start(bf16[512,128]{1,0:T(8,128)(2,1)} %get-tuple-element.43), channel_id=1, source_target_pairs={{0,8},{4,12},{8,0},{12,4},{16,24},{20,28},{24,16},{28,20},{1,9},{5... | collective-permute-start | bytes 393224 | tf_op jit(solution)/shard_map/ppermute | solution.py:39
  98.8 12.7 %collective-permute-start.19 = (bf16[512,128]{1,0:T(8,128)(2,1)S(1)}, bf16[512,128]{1,0:T(8,128)(2,1)S(1)}, u32[]{:S(2)}, u32[]{:S(2)}) collective-permute-start(bf16[512,128]{1,0:T(8,128)(2,1)S(1)} %get-tuple-element.42), channel_id=1, source_target_pairs={{0,16},{4,20},{8,24},{12,28},{16,0},{20,4},{24,8},{28,12},{1,17},{... | collective-permute-start | bytes 393224 | tf_op jit(solution)/shard_map/ppermute | solution.py:39
  101.3 10.8 %collective-permute-start.20 = (bf16[512,128]{1,0:T(8,128)(2,1)S(1)}, bf16[512,128]{1,0:T(8,128)(2,1)S(1)}, u32[]{:S(2)}, u32[]{:S(2)}) collective-permute-start(bf16[512,128]{1,0:T(8,128)(2,1)S(1)} %get-tuple-element.41), channel_id=1, source_target_pairs={{0,24},{4,28},{8,16},{12,20},{16,8},{20,12},{24,0},{28,4},{1,25},{... | collective-permute-start | bytes 393224 | tf_op jit(solution)/shard_map/ppermute | solution.py:39
  114.5 6.6 %collective-permute-start.21 = (bf16[4,256,128]{2,1,0:T(8,128)(2,1)}, bf16[4,256,128]{2,1,0:T(8,128)(2,1)S(1)}, u32[]{:S(2)}, u32[]{:S(2)}) collective-permute-start(bf16[4,256,128]{2,1,0:T(8,128)(2,1)} %dynamic-slice_bitcast_fusion.1), channel_id=1, source_target_pairs={{0,4},{4,0},{8,12},{12,8},{16,20},{20,16},{24,28},{28,24},{1,5},{5... | collective-permute-start | bytes 786440 | tf_op jit(solution)/shard_map/ppermute | solution.py:42
  132.1 6.4 %collective-permute-start.22 = (bf16[4,256,128]{2,1,0:T(8,128)(2,1)S(1)}, bf16[4,256,128]{2,1,0:T(8,128)(2,1)S(1)}, u32[]{:S(2)}, u32[]{:S(2)}) collective-permute-start(bf16[4,256,128]{2,1,0:T(8,128)(2,1)S(1)} %dynamic-slice_bitcast_fusion), channel_id=1, source_target_pairs={{0,4},{4,0},{8,12},{12,8},{16,20},{20,16},{24,28},{28,24},{1,5},{5... | collective-permute-start | bytes 786440 | tf_op jit(solution)/shard_map/ppermute | solution.py:42
  139.6 0.7 copy-start.2
  141.0 7.1 %collective-permute-start.23 = (bf16[512,128]{1,0:T(8,128)(2,1)}, bf16[512,128]{1,0:T(8,128)(2,1)S(1)}, u32[]{:S(2)}, u32[]{:S(2)}) collective-permute-start(bf16[512,128]{1,0:T(8,128)(2,1)} %get-tuple-element.39), channel_id=1, source_target_pairs={{0,8},{4,12},{8,0},{12,4},{16,24},{20,28},{24,16},{28,20},{1,9},{5... | collective-permute-start | bytes 393224 | tf_op jit(solution)/shard_map/ppermute | solution.py:39
  142.6 9.6 %collective-permute-start.24 = (bf16[512,128]{1,0:T(8,128)(2,1)}, bf16[512,128]{1,0:T(8,128)(2,1)S(1)}, u32[]{:S(2)}, u32[]{:S(2)}) collective-permute-start(bf16[512,128]{1,0:T(8,128)(2,1)} %get-tuple-element.40), channel_id=1, source_target_pairs={{0,16},{4,20},{8,24},{12,28},{16,0},{20,4},{24,8},{28,12},{1,17},{... | collective-permute-start | bytes 393224 | tf_op jit(solution)/shard_map/ppermute | solution.py:39
  143.5 8.6 %collective-permute-start.25 = (bf16[512,128]{1,0:T(8,128)(2,1)}, bf16[512,128]{1,0:T(8,128)(2,1)S(1)}, u32[]{:S(2)}, u32[]{:S(2)}) collective-permute-start(bf16[512,128]{1,0:T(8,128)(2,1)} %get-tuple-element.38), channel_id=1, source_target_pairs={{0,24},{4,28},{8,16},{12,20},{16,8},{20,12},{24,0},{28,4},{1,25},{... | collective-permute-start | bytes 393224 | tf_op jit(solution)/shard_map/ppermute | solution.py:39
  152.2 9.2 %collective-permute-start.26 = (bf16[2048,128]{1,0:T(8,128)(2,1)S(1)}, bf16[2048,128]{1,0:T(8,128)(2,1)S(1)}, u32[]{:S(2)}, u32[]{:S(2)}) collective-permute-start(bf16[2048,128]{1,0:T(8,128)(2,1)S(1)} %constant_dynamic-update-slice_fusion.6), channel_id=1, source_target_pairs={{0,2},{1,3},{2,0},{3,1},{4,6},{5,7},{6,4},{7,5},{8,10},{9,11},{10,... | collective-permute-start | bytes 1572872 | tf_op jit(solution)/shard_map/ppermute | solution.py:45
  161.6 4.7 %collective-permute-start.27 = (bf16[2048,256]{1,0:T(8,128)(2,1)S(1)}, bf16[2048,256]{1,0:T(8,128)(2,1)S(1)}, u32[]{:S(2)}, u32[]{:S(2)}) collective-permute-start(bf16[2048,256]{1,0:T(8,128)(2,1)S(1)} %pad_maximum_fusion), channel_id=1, source_target_pairs={{0,1},{1,0},{2,3},{3,2},{4,5},{5,4},{6,7},{7,6},{8,9},{9,8},{10,11... | collective-permute-start | bytes 3145736 | tf_op jit(solution)/shard_map/ppermute | solution.py:45
  164.8 28.7 %collective-permute-start.29 = (f32[128,768]{1,0:T(8,128)S(1)}, f32[128,768]{1,0:T(8,128)}, u32[]{:S(2)}, u32[]{:S(2)}) collective-permute-start(f32[128,768]{1,0:T(8,128)S(1)} %get-tuple-element.26), channel_id=1, source_target_pairs={{0,2},{1,3},{2,0},{3,1},{4,6},{5,7},{6,4},{7,5},{8,10},{9,11},{10,... | collective-permute-start | bytes 1179656 | tf_op jit(solution)/shard_map/ppermute | solution.py:45
  169.0 1.2 collective-permute-start.31
  169.3 23.4 %collective-permute-start.28 = (f32[128,768]{1,0:T(8,128)S(1)}, f32[128,768]{1,0:T(8,128)S(1)}, u32[]{:S(2)}, u32[]{:S(2)}) collective-permute-start(f32[128,768]{1,0:T(8,128)S(1)} %get-tuple-element.25), channel_id=1, source_target_pairs={{0,1},{1,0},{2,3},{3,2},{4,5},{5,4},{6,7},{7,6},{8,9},{9,8},{10,11... | collective-permute-start | bytes 1179656 | tf_op jit(solution)/shard_map/ppermute | solution.py:45
  170.8 5.9 %collective-permute-start.32 = (f32[8,128]{1,0:T(8,128)S(1)}, f32[8,128]{1,0:T(8,128)S(1)}, u32[]{:S(2)}, u32[]{:S(2)}) collective-permute-start(f32[8,128]{1,0:T(8,128)S(1)} %broadcast_add_fusion), channel_id=1, source_target_pairs={{0,2},{1,3},{2,0},{3,1},{4,6},{5,7},{6,4},{7,5},{8,10},{9,11},{10,... | collective-permute-start | bytes 12296 | tf_op jit(solution)/shard_map/ppermute | solution.py:45
  171.4 23.8 %collective-permute-start.30 = (f32[128,768]{1,0:T(8,128)S(1)}, f32[128,768]{1,0:T(8,128)S(1)}, u32[]{:S(2)}, u32[]{:S(2)}) collective-permute-start(f32[128,768]{1,0:T(8,128)S(1)} %get-tuple-element.24), channel_id=1, source_target_pairs={{0,3},{1,2},{2,1},{3,0},{4,7},{5,6},{6,5},{7,4},{8,11},{9,10},{10,... | collective-permute-start | bytes 1179656 | tf_op jit(solution)/shard_map/ppermute | solution.py:45
  177.4 3.7 %collective-permute-start.33 = (f32[8,128]{1,0:T(8,128)S(1)}, f32[8,128]{1,0:T(8,128)S(1)}, u32[]{:S(2)}, u32[]{:S(2)}) collective-permute-start(f32[8,128]{1,0:T(8,128)S(1)} %fusion.41), channel_id=1, source_target_pairs={{0,4},{4,0},{8,12},{12,8},{16,20},{20,16},{24,28},{28,24},{1,5},{5... | collective-permute-start | bytes 12296 | tf_op jit(solution)/shard_map/ppermute | solution.py:129
  181.1 5.8 %collective-permute-start.34 = (f32[8,128]{1,0:T(8,128)S(1)}, f32[8,128]{1,0:T(8,128)S(1)}, u32[]{:S(2)}, u32[]{:S(2)}) collective-permute-start(f32[8,128]{1,0:T(8,128)S(1)} %add.254), channel_id=1, source_target_pairs={{0,8},{4,12},{8,0},{12,4},{16,24},{20,28},{24,16},{28,20},{1,9},{5... | collective-permute-start | bytes 12296 | tf_op jit(solution)/shard_map/ppermute | solution.py:129
  186.9 4.5 %collective-permute-start.35 = (f32[8,128]{1,0:T(8,128)S(1)}, f32[8,128]{1,0:T(8,128)S(1)}, u32[]{:S(2)}, u32[]{:S(2)}) collective-permute-start(f32[8,128]{1,0:T(8,128)S(1)} %add.255), channel_id=1, source_target_pairs={{0,16},{4,20},{8,24},{12,28},{16,0},{20,4},{24,8},{28,12},{1,17},{... | collective-permute-start | bytes 12296 | tf_op jit(solution)/shard_map/ppermute | solution.py:129
  196.0 3.6 %copy-start.1 = (f32[128,3072]{1,0:T(8,128)S(1)}, f32[128,3072]{1,0:T(8,128)}, u32[]{:S(2)}) copy-start(f32[128,3072]{1,0:T(8,128)} %param.9) | copy-start | bytes 4718596
  196.0 3.6 %copy-start.6 = (f32[128,3072]{1,0:T(8,128)S(1)}, f32[128,3072]{1,0:T(8,128)}, u32[]{:S(2)}) copy-start(f32[128,3072]{1,0:T(8,128)} %param.11) | copy-start | bytes 4718596
  196.0 3.9 %copy-start.7 = (f32[128,3072]{1,0:T(8,128)S(1)}, f32[128,3072]{1,0:T(8,128)}, u32[]{:S(2)}) copy-start(f32[128,3072]{1,0:T(8,128)} %param.10) | copy-start | bytes 4718596
  204.5 16.3 %collective-permute-start.37 = (bf16[128,3072]{1,0:T(8,128)(2,1)S(1)}, bf16[128,3072]{1,0:T(8,128)(2,1)S(1)}, u32[]{:S(2)}, u32[]{:S(2)}) collective-permute-start(bf16[128,3072]{1,0:T(8,128)(2,1)S(1)} %get-tuple-element.13), channel_id=1, source_target_pairs={{0,8},{4,12},{8,0},{12,4},{16,24},{20,28},{24,16},{28,20},{1,9},{5... | collective-permute-start | bytes 2359304 | tf_op jit(solution)/shard_map/ppermute | solution.py:32
  206.5 18.9 %collective-permute-start.40 = (bf16[128,3072]{1,0:T(8,128)(2,1)S(1)}, bf16[128,3072]{1,0:T(8,128)(2,1)}, u32[]{:S(2)}, u32[]{:S(2)}) collective-permute-start(bf16[128,3072]{1,0:T(8,128)(2,1)S(1)} %get-tuple-element.13), channel_id=1, source_target_pairs={{8,16},{12,20},{16,8},{20,12},{9,17},{13,21},{17,9},{21,13},{10,18... | collective-permute-start | bytes 2359304 | tf_op jit(solution)/shard_map/ppermute | solution.py:32
  208.1 18.6 %collective-permute-start.36 = (bf16[128,3072]{1,0:T(8,128)(2,1)S(1)}, bf16[128,3072]{1,0:T(8,128)(2,1)S(1)}, u32[]{:S(2)}, u32[]{:S(2)}) collective-permute-start(bf16[128,3072]{1,0:T(8,128)(2,1)S(1)} %get-tuple-element.13), channel_id=1, source_target_pairs={{0,4},{4,0},{8,12},{12,8},{16,20},{20,16},{24,28},{28,24},{1,5},{5... | collective-permute-start | bytes 2359304 | tf_op jit(solution)/shard_map/ppermute | solution.py:42
  220.8 14.8 %collective-permute-start.44 = (bf16[128,3072]{1,0:T(8,128)(2,1)S(1)}, bf16[128,3072]{1,0:T(8,128)(2,1)}, u32[]{:S(2)}, u32[]{:S(2)}) collective-permute-start(bf16[128,3072]{1,0:T(8,128)(2,1)S(1)} %collective-permute-done.37), channel_id=1, source_target_pairs={{8,16},{12,20},{16,8},{20,12},{9,17},{13,21},{17,9},{21,13},{10,18... | collective-permute-start | bytes 2359304 | tf_op jit(solution)/shard_map/ppermute | solution.py:32
  222.4 18.4 %collective-permute-start.38 = (bf16[128,3072]{1,0:T(8,128)(2,1)S(1)}, bf16[128,3072]{1,0:T(8,128)(2,1)}, u32[]{:S(2)}, u32[]{:S(2)}) collective-permute-start(bf16[128,3072]{1,0:T(8,128)(2,1)S(1)} %collective-permute-done.37), channel_id=1, source_target_pairs={{0,4},{4,0},{24,28},{28,24},{1,5},{5,1},{25,29},{29,25},{2,6},{6,2... | collective-permute-start | bytes 2359304 | tf_op jit(solution)/shard_map/ppermute | solution.py:42
  225.4 19.6 %collective-permute-start.41 = (bf16[128,3072]{1,0:T(8,128)(2,1)}, bf16[128,3072]{1,0:T(8,128)(2,1)}, u32[]{:S(2)}, u32[]{:S(2)}) collective-permute-start(bf16[128,3072]{1,0:T(8,128)(2,1)} %collective-permute-done.40), channel_id=1, source_target_pairs={{8,0},{12,4},{16,24},{20,28},{9,1},{13,5},{17,25},{21,29},{10,2},{... | collective-permute-start | bytes 2359304 | tf_op jit(solution)/shard_map/ppermute | solution.py:32
  226.7 20.7 %collective-permute-start.39 = (bf16[128,3072]{1,0:T(8,128)(2,1)S(1)}, bf16[128,3072]{1,0:T(8,128)(2,1)}, u32[]{:S(2)}, u32[]{:S(2)}) collective-permute-start(bf16[128,3072]{1,0:T(8,128)(2,1)S(1)} %collective-permute-done.36), channel_id=1, source_target_pairs={{0,8},{4,12},{24,16},{28,20},{1,9},{5,13},{25,17},{29,21},{2,10},{... | collective-permute-start | bytes 2359304 | tf_op jit(solution)/shard_map/ppermute | solution.py:32
  233.0 29.3 %collective-permute-start.43 = (bf16[128,3072]{1,0:T(8,128)(2,1)}, bf16[128,3072]{1,0:T(8,128)(2,1)S(1)}, u32[]{:S(2)}, u32[]{:S(2)}) collective-permute-start(bf16[128,3072]{1,0:T(8,128)(2,1)} %collective-permute-done.40), channel_id=1, source_target_pairs={{8,12},{12,8},{16,20},{20,16},{9,13},{13,9},{17,21},{21,17},{10,14... | collective-permute-start | bytes 2359304 | tf_op jit(solution)/shard_map/ppermute | solution.py:42
  235.6 23.8 %collective-permute-start.45 = (bf16[128,3072]{1,0:T(8,128)(2,1)}, bf16[128,3072]{1,0:T(8,128)(2,1)S(1)}, u32[]{:S(2)}, u32[]{:S(2)}) collective-permute-start(bf16[128,3072]{1,0:T(8,128)(2,1)} %collective-permute-done.44), channel_id=1, source_target_pairs={{8,0},{12,4},{16,24},{20,28},{9,1},{13,5},{17,25},{21,29},{10,2},{... | collective-permute-start | bytes 2359304 | tf_op jit(solution)/shard_map/ppermute | solution.py:32
  240.7 23.7 %collective-permute-start.47 = (bf16[128,3072]{1,0:T(8,128)(2,1)}, bf16[128,3072]{1,0:T(8,128)(2,1)S(1)}, u32[]{:S(2)}, u32[]{:S(2)}) collective-permute-start(bf16[128,3072]{1,0:T(8,128)(2,1)} %collective-permute-done.44), channel_id=1, source_target_pairs={{8,12},{12,8},{16,20},{20,16},{9,13},{13,9},{17,21},{21,17},{10,14... | collective-permute-start | bytes 2359304 | tf_op jit(solution)/shard_map/ppermute | solution.py:42
  245.0 17.3 %collective-permute-start.42 = (bf16[128,3072]{1,0:T(8,128)(2,1)}, bf16[128,3072]{1,0:T(8,128)(2,1)S(1)}, u32[]{:S(2)}, u32[]{:S(2)}) collective-permute-start(bf16[128,3072]{1,0:T(8,128)(2,1)} %collective-permute-done.41), channel_id=1, source_target_pairs={{0,4},{4,0},{24,28},{28,24},{1,5},{5,1},{25,29},{29,25},{2,6},{6,2... | collective-permute-start | bytes 2359304 | tf_op jit(solution)/shard_map/ppermute | solution.py:42
  259.5 10.7 %collective-permute-start.46 = (bf16[64,3072]{1,0:T(8,128)(2,1)S(1)}, bf16[64,3072]{1,0:T(8,128)(2,1)S(1)}, u32[]{:S(2)}, u32[]{:S(2)}) collective-permute-start(bf16[64,3072]{1,0:T(8,128)(2,1)S(1)} %slice.79), channel_id=1, source_target_pairs={{0,4},{4,0},{24,28},{28,24},{1,5},{5,1},{25,29},{29,25},{2,6},{6,2... | collective-permute-start | bytes 1179656 | tf_op jit(solution)/shard_map/ppermute | solution.py:42
  263.4 8.9 %copy-start.4 = (bf16[256,1024]{0,1:T(8,128)(2,1)S(1)}, bf16[256,1024]{0,1:T(8,128)(2,1)}, u32[]{:S(2)}) copy-start(bf16[256,1024]{0,1:T(8,128)(2,1)} %get-tuple-element.20) | copy-start | bytes 1572868
  264.5 8.9 %copy-start.3 = (bf16[256,1024]{0,1:T(8,128)(2,1)S(1)}, bf16[256,1024]{0,1:T(8,128)(2,1)}, u32[]{:S(2)}) copy-start(bf16[256,1024]{0,1:T(8,128)(2,1)} %get-tuple-element.19) | copy-start | bytes 1572868
  271.0 9.8 %collective-permute-start.48 = (bf16[64,3072]{1,0:T(8,128)(2,1)S(1)}, bf16[64,3072]{1,0:T(8,128)(2,1)S(1)}, u32[]{:S(2)}, u32[]{:S(2)}) collective-permute-start(bf16[64,3072]{1,0:T(8,128)(2,1)S(1)} %get-tuple-element.22), channel_id=1, source_target_pairs={{8,0},{12,4},{16,24},{20,28},{9,1},{13,5},{17,25},{21,29},{10,2},{... | collective-permute-start | bytes 1179656 | tf_op jit(solution)/shard_map/ppermute | solution.py:32

commit v2 on v0

v2 whole, which is shorter than its diff:
```python
import jax
import jax.numpy as jnp
from jax import lax
from jax.experimental import pallas as pl
from jax.experimental.pallas import tpu as pltpu
from jax.sharding import PartitionSpec as P

D = 3072
FF = 4096
CELL = 8
BF16 = jnp.bfloat16
F32 = jnp.float32
SMEM = pl.BlockSpec(memory_space=pltpu.SMEM)
HBM = pl.BlockSpec(memory_space=pltpu.HBM)

def shaped(shape, dtype):
    return jax.ShapeDtypeStruct(shape, dtype)


def call(body, outs, args, flops=0, moved=0, limit=60, after=()):
    args, after = tuple(args), tuple(after)
    n_in, n_out = len(args) - 1, len(outs)

    def kernel(spot, *refs):
        given, refs = refs[:n_in], refs[n_in + len(after) :]
        results, refs = refs[:n_out], refs[n_out:]
        ins, parts, in_sems, out_sems = refs[:n_in], refs[n_in : n_in + n_out], refs[-2], refs[-1]
        loads = [pltpu.make_async_copy(g, v, in_sems.at[i]) for i, (g, v) in enumerate(zip(given, ins))]
        for load in loads:
            load.start()
        waiting, sent = set(range(n_in)), []

        def need(*which):
            for i in which:
                if i in waiting:
                    loads[i].wait()
                    waiting.remove(i)

        def done(o, *index):
            copy = pltpu.make_async_copy(
                parts[o].at[index] if index else parts[o],
                results[o].at[index] if index else results[o],
                out_sems.at[len(sent)],
            )
            copy.start()
            sent.append(copy)

        body(spot, ins, parts, need, done)
        need(*range(n_in))
        for copy in sent:
            copy.wait()

    return pl.pallas_call(
        kernel,
        out_shape=tuple(outs),
        in_specs=[SMEM] + [HBM] * (n_in + len(after)),
        out_specs=(HBM,) * n_out,
        scratch_shapes=[pltpu.VMEM(a.shape, a.dtype) for a in args[1:]]
        + [pltpu.VMEM(o.shape, o.dtype) for o in outs]
        + [pltpu.SemaphoreType.DMA((n_in,)), pltpu.SemaphoreType.DMA((32,))],
        compiler_params=pltpu.CompilerParams(vmem_limit_bytes=limit << 20),
        cost_estimate=pl.CostEstimate(flops=flops, bytes_accessed=moved, transcendentals=0),
    )(*args, *after)


def hidden_body(spot, ins, outs, need, done):
    gate, up = ins
    kept, given = outs
    z, x = spot[0], spot[1]
    part = kept.shape[1]
    need(0, 1)
    for o, out, side in ((1, given, 1 - x), (0, kept, x)):
        for m in range(4):
            cols = pl.ds(pl.multiple_of((2 * (z ^ m) + side) * part, part), part)
            gate_f = gate[:, cols].astype(F32)
            silu = gate_f * (1.0 / (1.0 + jnp.exp(-gate_f)))
            out[m] = (silu * up[:, cols].astype(F32)).T.astype(BF16)
        done(o)


def turn_body(spot, ins, outs, need, done):
    del spot
    kept, came = ins
    need(0, 1)
    for m in (3, 2, 1, 0):
        outs[m][0] = kept[m]
        outs[m][1] = came[m]
        done(m)


def in_pairs(pieces):
    own, own_x, near, near_x, last, last_x, far, low, high = pieces
    return [((i,), lambda p=p: p[...]) for i, p in enumerate((own, own_x, near, near_x))] + [
        ((6,), lambda: far[...]),
        ((7, 8), lambda: jnp.concatenate([low[...], high[...]], axis=0)),
        ((4,), lambda: last[...]),
        ((5,), lambda: last_x[...]),
    ]


def grad_body(spot, ins, outs, need, done):
    del spot
    pieces, hidden, squares = ins[:9], ins[9:], outs[4]
    part = outs[0].shape[0]
    total = None
    for m, (numbers, right) in enumerate(in_pairs(pieces)):
        need(*numbers, *range(9, 13))
        left = jnp.concatenate([h[m // 2, m % 2] for h in hidden], axis=0)
        term = jnp.dot(left, right(), preferred_element_type=F32)
        total = term if total is None else total + term
    for i in (3, 2, 1, 0):
        outs[i][...] = total[i * part : (i + 1) * part].astype(outs[i].dtype)
        done(i)
    squares[...] = jnp.broadcast_to(jnp.sum(total * total), squares.shape)
    done(4)


def d_hidden_body(spot, ins, outs, need, done):
    del spot
    pieces, weights = ins[:9], ins[9:]
    keep, give = outs
    part = weights[0].shape[0]
    tokens = pieces[0].shape[0]
    need(*range(9, 13))
    weight = jnp.concatenate([w[...] for w in weights], axis=0)
    for m, (numbers, side) in enumerate(in_pairs(pieces)):
        need(*numbers)
        out = lax.dot_general(side(), weight, (((1,), (1,)), ((), ())), preferred_element_type=F32)
        rows = slice(m * tokens, (m + 1) * tokens)
        keep[0, rows] = out[:, :part]
        give[0, rows] = out[:, part : 2 * part]
        keep[1, rows] = out[:, 2 * part : 3 * part]
        give[1, rows] = out[:, 3 * part :]
        at = pl.ds(m * tokens, tokens)
        done(0, slice(None), at)
        done(1, slice(None), at)


def add_body(spot, ins, outs, need, done):
    del spot
    keep, give = ins
    mine, sent = outs
    need(0, 1)
    sent[...] = keep[1] + give[1]
    done(1)
    mine[...] = keep[0] + give[0]
    done(0)


def back_body(spot, ins, outs, need, done):
    del spot
    mine, came = ins
    rows = outs[0].shape[0]
    need(0, 1)
    for m in (3, 2, 1, 0):
        at = slice(m * rows, (m + 1) * rows)
        outs[m][...] = (mine[at] + came[at]).astype(BF16)
        done(m)


def adam_body(spot, ins, outs, need, done):
    total, grads = ins[0], ins[1:5]
    master, one, two = ins[5:]
    master_next, one_next, two_next, shard = outs
    t = spot[2]
    cols = grads[0].shape[1]
    need(0)
    factor = 1.0 / jnp.sqrt(total[0:1, 0:1] / (FF * D) + 1e-06)
    need(5, 6, 7)
    for m, g in enumerate(grads):
        need(1 + m)
        at = pl.ds(pl.multiple_of((t ^ m) * cols, cols), cols)
        clipped = g[...].astype(F32) * factor
        first = 0.9 * one[:, at] + 0.1 * clipped
        second = 0.95 * two[:, at] + 0.05 * clipped * clipped
        old = master[:, at]
        new = old - 0.003 * (first / (jnp.sqrt(second) + 1e-08) + 0.1 * old)
        one_next[:, at] = first
        two_next[:, at] = second
        master_next[:, at] = new
        shard[:, at] = new.astype(BF16)
        for o in (3, 0, 1, 2):
            done(o, slice(None), at)


def outputs_body(spot, ins, outs, need, done):
    gate, up, *blocks, came = ins
    gate_grad, up_grad = outs
    z, x = spot[0], spot[1]
    tokens, part = came.shape[1:]
    need(*range(7))
    for m, block in enumerate(blocks):
        for side in range(2):
            d_hidden = (came[m] if side else block[:tokens]).astype(F32)
            cols = pl.ds(pl.multiple_of((2 * (z ^ m) + (x ^ side)) * part, part), part)
            gate_f = gate[:, cols].astype(F32)
            sigm = 1.0 / (1.0 + jnp.exp(-gate_f))
            up_grad[:, cols] = (d_hidden * (gate_f * sigm)).astype(BF16)
            gate_grad[:, cols] = (
                d_hidden * up[:, cols].astype(F32) * sigm * (1.0 + gate_f * (1.0 - sigm))
            ).astype(BF16)
    done(0)
    done(1)


def gate_body(*refs):
    del refs


def together(*values):
    return pl.pallas_call(
        gate_body,
        out_shape=tuple(shaped(v.shape, v.dtype) for v in values),
        in_specs=[HBM] * len(values),
        out_specs=(HBM,) * len(values),
        input_output_aliases={i: i for i in range(len(values))},
        compiler_params=pltpu.CompilerParams(vmem_limit_bytes=60 << 20),
    )(*values)


def on_device(n, d_out, gate, up_proj, master, moment_one, moment_two):
    outer = n // CELL
    place = lax.axis_index("dp")
    z, x = place % CELL // 2, place % 2
    t = lax.axis_index("tensor")
    spot = jnp.stack([z, x, t]).astype(jnp.int32)
    tokens, width = gate.shape
    rows = master.shape[0]
    part = width // CELL
    cols = D // 4
    same_pair = [[k + CELL * j for j in range(outer)] for k in range(CELL)]

    def across(value, m):
        return lax.ppermute(value, "dp", [(i, i ^ m) for i in range(n)])

    def swap(value, m):
        return lax.ppermute(value, "tensor", [(i, i ^ m) for i in range(4)])

    def in_order(pieces):
        own, own_x, near, near_x, last, last_x, far, low, high = pieces
        size, half = own.shape[0], low.shape[0]
        out = jnp.zeros((CELL * size,) + own.shape[1:], own.dtype)
        for value, m, shift in (
            (own, 0, 0), (own_x, 1, 0), (near, 2, 0), (near_x, 3, 0), (last, 6, 0),
            (last_x, 7, 0), (far, 4, 0), (low, 5, 0), (high, 5, half),
        ):
            at = (place % CELL ^ m) * size + shift
            out = lax.dynamic_update_slice(out, value, (at, 0))
        return out

    def by_place(value):
        if outer == 1:
            return value
        return value.reshape(tokens, outer, CELL, rows).transpose(0, 2, 1, 3).reshape(tokens, width)

    gate, up_proj = by_place(gate), by_place(up_proj)

    own = lax.dynamic_slice(d_out, (0, t * cols), (tokens, cols))
    half = tokens // 2
    near, own_x, last = across(own, 2), across(own, 1), across(own, 6)
    block = shaped((4, part, tokens), BF16)
    kept, given = call(hidden_body, (block, block), (spot, gate, up_proj), moved=2 << 20)
    near, own_x, given = together(near, own_x, given)
    near_x, came = across(near, 1), across(given, 1)
    last, came = together(last, came)
    far, last_x = across(last, 2), across(last, 1)
    pair = shaped((2, part, tokens), BF16)
    blocks = call(turn_body, (pair,) * 4, (spot, kept, came), moved=1 << 20)
    blocks = [blocks[0]] + [across(blocks[m], 2 * m) for m in (1, 2, 3)]
    far, last_x, *blocks = together(far, last_x, *blocks)
    low, high = across(far[:half], 1), across(last_x[half:], 2)
    hidden = jnp.stack(blocks)
    hidden_y, hidden_c = swap(hidden, 2), swap(hidden, 1)
    hiddens = (hidden, hidden_c, hidden_y, swap(hidden_y, 1))
    weight = master
    if outer > 1:
        weight = lax.all_gather(
            master.astype(BF16), "dp", axis=0, tiled=True, axis_index_groups=same_pair
        )
    weights = [
        lax.dynamic_slice(weight, (0, (t ^ m) * cols), (part, cols)).astype(BF16) for m in range(4)
    ]
    weights = [weights[0]] + [swap(weights[m], m) for m in (1, 2, 3)]
    pieces = (own, own_x, near, near_x, last, last_x, far, low, high)

    flops = 2 * 4 * part * CELL * tokens * cols
    piece, sent = shaped((part, cols), F32), shaped((part, cols), BF16)
    *grads, total = call(
        grad_body,
        (piece, sent, sent, sent, shaped((8, 128), F32)),
        (spot, *pieces, *hiddens),
        flops=flops,
        moved=8 << 20,
    )
    if outer > 1:
        grads = lax.psum_scatter(
            jnp.stack([g.astype(F32) for g in grads]).reshape(4, outer, rows, cols),
            "dp",
            scatter_dimension=1,
            axis_index_groups=same_pair,
        )
        total = jnp.broadcast_to(jnp.sum(grads * grads), (8, 128))
    grad_own = grads[0]
    step = 1
    while step < n:
        total = total + across(total, step)
        step *= 2
    for m in (1, 2):
        total = total + swap(total, m)
    grads = [grads[0]] + [swap(grads[m], m) for m in (1, 2, 3)]

    sums = shaped((2, CELL * tokens, part), F32)
    keep, give = call(
        d_hidden_body,
        (sums, sums),
        (spot, *pieces, *weights),
        flops=flops,
        moved=10 << 20,
        after=(grad_own,),
    )
    give = swap(give, 1)

    state = shaped((rows, D), F32)
    master_next, moment_one_next, moment_two_next, shard_next = call(
        adam_body,
        (state, state, state, shaped((rows, D), BF16)),
        (spot, total, *grads, master, moment_one, moment_two),
        moved=12 << 20,
    )
    if outer > 1:
        shard_next = lax.all_gather(
            shard_next, "dp", axis=0, tiled=True, axis_index_groups=same_pair
        )
    own = shard_next
    half = own.shape[0] // 2
    near, own_x, last = across(own, 2), across(own, 1), across(own, 6)
    mine_sum = shaped((CELL * tokens, part), F32)
    mine, sent = call(add_body, (mine_sum,) * 2, (spot, keep, give), moved=6 << 20)
    came = swap(sent, 2)
    near, own_x = together(near, own_x)
    near_x = across(near, 1)
    last, near_x = together(last, near_x)
    far, last_x = across(last, 2), across(last, 1)
    pair = shaped((2 * tokens, part), BF16)
    blocks = call(back_body, (pair,) * 4, (spot, mine, came), moved=3 << 20)
    blocks = [blocks[0]] + [across(blocks[m], 2 * m) for m in (1, 2, 3)]
    far, last_x, *blocks = together(far, last_x, *blocks)
    low, high = across(far[:half], 1), across(last_x[half:], 2)
    came = across(jnp.stack([b[tokens:] for b in blocks]), 1)
    out = shaped((tokens, width), BF16)
    gate_grad, up_grad = call(
        outputs_body, (out, out), (spot, gate, up_proj, *blocks, came), moved=4 << 20
    )
    weight_next = in_order((own, own_x, near, near_x, last, last_x, far, low, high))
    if outer > 1:
        weight_next = (
            weight_next.reshape(CELL, outer, rows, D).transpose(1, 0, 2, 3).reshape(width, D)
        )

    def from_place(value):
        if outer == 1:
            return value
        return value.reshape(tokens, CELL, outer, rows).transpose(0, 2, 1, 3).reshape(tokens, width)

    return (
        from_place(gate_grad),
        from_place(up_grad),
        master_next,
        moment_one_next,
        moment_two_next,
        weight_next,
    )


def solution(mesh):
    n = mesh.shape["dp"]
    placed = (
        P("dp", None),
        P("dp", "tensor"),
        P("dp", "tensor"),
        P(("tensor", "dp"), None),
        P(("tensor", "dp"), None),
        P(("tensor", "dp"), None),
    )
    return jax.shard_map(
        lambda *args: on_device(n, *args),
        mesh=mesh,
        in_specs=placed,
        out_specs=(
            P("dp", "tensor"),
            P("dp", "tensor"),
            P(("tensor", "dp"), None),
            P(("tensor", "dp"), None),
            P(("tensor", "dp"), None),
            P("tensor", None),
        ),
        check_vma=False,
    )
```

time: 488 us -> 214 us (0.44)
  waiting for transfers between devices: 403 us -> 76.5 us
  starting transfers between devices: 0.12 us -> 55.4 us
  Pallas kernels: 0 us -> 39.6 us
  blocking collectives: 39.6 us -> 0 us
  local copies, waits for them, and re-layouts: 7.3 us -> 36.5 us
  matrix products: 13.6 us -> 0 us
  between operations: 14.5 us -> 0.92 us
  other arithmetic: 9.02 us -> 3.93 us
    reduce_scatter x1 -> x0, waiting for transfers between devices: 210 us -> none  [on_device(): grad = lax.psum_scatter(partial_term, 'dp', scatter_dimension=0, tiled=True)]
    all_gather x2 -> x0, waiting for transfers between devices: 193 us -> none  [the longest x1 98.4 us: on_device(): lax.all_gather(weight, 'dp', axis=0, tiled=True)]
    ppermute x0 -> x40, waiting for transfers between devices: none -> 76.5 us  [the longest x27 56.9 us: across(): return lax.ppermute(value, 'dp', [(i, i ^ m) for i in range(n)])]
    ppermute x0 -> x40, starting transfers between devices: none -> 55.4 us  [the longest x27 46.5 us: across(): return lax.ppermute(value, 'dp', [(i, i ^ m) for i in range(n)])]
    pallas_call x0 -> x14, Pallas kernels: none -> 39.6 us  [the longest x8 39.6 us: call(): pl.pallas_call(kernel, out_shape=tuple(outs), in_specs=[SMEM] + [HBM] * (...]
    psum x1 -> x0, blocking collectives: 39.6 us -> none  [on_device(): total = lax.psum(local_squares, ('dp', 'tensor'))]
    dynamic_update_slice x0 -> x9, local copies, waits for them, and re-layouts: none -> 14.9 us  [in_order(): out = lax.dynamic_update_slice(out, value, (at, 0))]
    dot_general x2 -> x0, matrix products: 13.6 us -> none  [the longest x1 7.69 us: on_device(): lax.dot_general(hidden, d_out, (((0,), (0,)), ((), ())), preferred_elemen...]
  transfers between devices with their start and end apart: 3 -> 40, of which waited for: 3 -> 21; matrix products, arithmetic and copies ran while one was open for 1% -> 12% of each run, Pallas kernels for 0% -> 15%
where the time goes in v2:
time: 214 us; the launch traced here: 213 us
  waiting for transfers between devices  76.5 us (36%)
  starting transfers between devices  55.4 us (26%)
  Pallas kernels  39.6 us (19%)
  local copies, waits for them, and re-layouts  36.5 us (17%)
  other arithmetic  3.93 us (2%)
    ppermute x27, waiting for transfers between devices, across(): return lax.ppermute(value, 'dp', [(i, i ^ m) for i in range(n)])  56.9 us
    ppermute x27, starting transfers between devices, across(): return lax.ppermute(value, 'dp', [(i, i ^ m) for i in range(n)])  46.5 us
    pallas_call x8, Pallas kernels, call(): pl.pallas_call(kernel, out_shape=tuple(outs), in_specs=[SMEM] + [HBM] * (...  39.6 us
    ppermute x13, waiting for transfers between devices, swap(): return lax.ppermute(value, 'tensor', [(i, i ^ m) for i in range(4)])  19.6 us
    dynamic_update_slice x9, local copies, waits for them, and re-layouts, in_order(): out = lax.dynamic_update_slice(out, value, (at, 0))  14.9 us
    unnamed x50, local copies, waits for them, and re-layouts  10.2 us
    ppermute x13, starting transfers between devices, swap(): return lax.ppermute(value, 'tensor', [(i, i ^ m) for i in range(4)])  8.86 us
    slice x4, local copies, waits for them, and re-layouts, on_device(): low, high = (across(far[:half], 1), across(last_x[half:], 2))  4.6 us
  transfers between devices with their start and end apart: 40, of which 21 were waited for; matrix products, arithmetic and copies ran while one was open for 12% of the time, Pallas kernels for 15%

profile of v2, /device:TPU:0, one launch (start us, length us, event | category | flops | bytes accessed | tf_op | source)
XLA Modules:
  0.0 212.9 jit_solution(2109741583317098625)
XLA Ops:
  0.7 1.4 copy-done
  2.8 3.0 %collective-permute-start = (bf16[256,768]{1,0:T(8,128)(2,1)}, bf16[256,768]{1,0:T(8,128)(2,1)}, u32[]{:S(2)}, u32[]{:S(2)}) collective-permute-start(bf16[256,768]{1,0:T(8,128)(2,1)} %constant_dynamic-slice_fusion.refs_0_), channel_id=1, source_target_pairs={{0,8},{4,12},{8,0},{12,4},{16,24},{20,28},{24,16},{28,20},{1,9},{5... | collective-permute-start | bytes 1179656 | tf_op jit(solution)/shard_map/ppermute | solution.py:234
  5.8 1.5 collective-permute-start.1
  7.3 2.5 %collective-permute-start.3 = (bf16[256,768]{1,0:T(8,128)(2,1)}, bf16[256,768]{1,0:T(8,128)(2,1)S(1)}, u32[]{:S(2)}, u32[]{:S(2)}) collective-permute-start(bf16[256,768]{1,0:T(8,128)(2,1)} %constant_dynamic-slice_fusion.refs_0_), channel_id=1, source_target_pairs={{0,24},{4,28},{8,16},{12,20},{16,8},{20,12},{24,0},{28,4},{1,25},{... | collective-permute-start | bytes 1179656 | tf_op jit(solution)/shard_map/ppermute | solution.py:234
  10.5 3.3 %shard_map.109 = (bf16[4,128,256]{2,1,0:T(8,128)(2,1)}, bf16[4,128,256]{2,1,0:T(8,128)(2,1)}) custom-call(s32[3]{0:T(128)} %pad_add_fusion.spot, bf16[256,1024]{1,0:T(8,128)(2,1)} %refs_0_.3, bf16[256,1024]{1,0:T(8,128)(2,1)} %refs_1_.3), custom_call_target="tpu_custom_call" | custom-call | bytes 2097152 | tf_op jit(solution)/shard_map/pallas_call | solution.py:53
  13.8 1.9 collective-permute-done.refs_0_
  15.7 1.1 collective-permute-done.1.refs_1_
  16.7 1.5 collective-permute-start.4
  18.2 7.7 %collective-permute-done.3.refs_0_ = bf16[256,768]{1,0:T(8,128)(2,1)S(1)} collective-permute-done((bf16[256,768]{1,0:T(8,128)(2,1)}, bf16[256,768]{1,0:T(8,128)(2,1)S(1)}, u32[]{:S(2)}, u32[]{:S(2)}) %collective-permute-start.3) | collective-permute-done | bytes 393248 | tf_op jit(solution)/shard_map/ppermute | solution.py:234
  27.3 1.8 collective-permute-start.5
  29.7 2.8 %shard_map.112 = (bf16[2,128,256]{2,1,0:T(8,128)(2,1)}, bf16[2,128,256]{2,1,0:T(8,128)(2,1)}, bf16[2,128,256]{2,1,0:T(8,128)(2,1)}, bf16[2,128,256]{2,1,0:T(8,128)(2,1)}) custom-call(s32[3]{0:T(128)} %pad_add_fusion.spot, bf16[4,128,256]{2,1,0:T(8,128)(2,1)} %get-tuple-element.57.refs_0_, bf16[4,128,256]{2,1,0:T(8,128)(2,1)} %get-tuple-element.58.refs_1_), custom_call_target="tpu_custom_call" | custom-call | bytes 1048576 | tf_op jit(solution)/shard_map/pallas_call | solution.py:53
  32.5 1.2 collective-permute-start.7
  33.7 8.6 %collective-permute-start.8 = (bf16[2,128,256]{2,1,0:T(8,128)(2,1)}, bf16[2,128,256]{2,1,0:T(8,128)(2,1)S(1)}, u32[]{:S(2)}, u32[]{:S(2)}) collective-permute-start(bf16[2,128,256]{2,1,0:T(8,128)(2,1)} %get-tuple-element.61), channel_id=1, source_target_pairs={{0,16},{4,20},{8,24},{12,28},{16,0},{20,4},{24,8},{28,12},{1,17},{... | collective-permute-start | bytes 393224 | tf_op jit(solution)/shard_map/ppermute | solution.py:234
  42.3 1.4 collective-permute-start.9
  43.7 1.8 collective-permute-done.8.refs_4_
  45.5 4.3 %collective-permute-done.9.refs_5_ = bf16[2,128,256]{2,1,0:T(8,128)(2,1)S(1)} collective-permute-done((bf16[2,128,256]{2,1,0:T(8,128)(2,1)}, bf16[2,128,256]{2,1,0:T(8,128)(2,1)S(1)}, u32[]{:S(2)}, u32[]{:S(2)}) %collective-permute-start.9) | collective-permute-done | bytes 131104 | tf_op jit(solution)/shard_map/ppermute | solution.py:234
  51.2 2.0 pad_maximum_fusion.refs_9_
  53.1 1.5 collective-permute-start.13
  54.7 8.0 %collective-permute-done.13.refs_11_ = bf16[4,2,128,256]{3,2,1,0:T(8,128)(2,1)} collective-permute-done((bf16[4,2,128,256]{3,2,1,0:T(8,128)(2,1)}, bf16[4,2,128,256]{3,2,1,0:T(8,128)(2,1)}, u32[]{:S(2)}, u32[]{:S(2)}) %collective-permute-start.13) | collective-permute-done | bytes 524320 | tf_op jit(solution)/shard_map/ppermute | solution.py:237
  62.6 1.6 slice.24
  64.3 2.0 collective-permute-start.10
  66.3 0.9 slice.25
  67.2 1.9 collective-permute-start.11
  70.0 4.9 %collective-permute-done.2.refs_3_ = bf16[256,768]{1,0:T(8,128)(2,1)} collective-permute-done((bf16[256,768]{1,0:T(8,128)(2,1)}, bf16[256,768]{1,0:T(8,128)(2,1)}, u32[]{:S(2)}, u32[]{:S(2)}) %collective-permute-start.2) | collective-permute-done | bytes 393248 | tf_op jit(solution)/shard_map/ppermute | solution.py:234
  74.9 3.8 %collective-permute-done.10.refs_7_ = bf16[128,768]{1,0:T(8,128)(2,1)} collective-permute-done((bf16[128,768]{1,0:T(8,128)(2,1)}, bf16[128,768]{1,0:T(8,128)(2,1)}, u32[]{:S(2)}, u32[]{:S(2)}) %collective-permute-start.10) | collective-permute-done | bytes 196640 | tf_op jit(solution)/shard_map/ppermute | solution.py:234
  78.7 1.5 collective-permute-start.30
  80.2 7.6 %shard_map.114 = (f32[128,768]{1,0:T(8,128)}, bf16[128,768]{1,0:T(8,128)(2,1)}, bf16[128,768]{1,0:T(8,128)(2,1)}, bf16[128,768]{1,0:T(8,128)(2,1)}, f32[8,128]{1,0:T(8,128)}) custom-call(s32[3]{0:T(128)} %pad_add_fusion.spot, bf16[256,768]{1,0:T(8,128)(2,1)} %constant_dynamic-slice_fusion.refs_0_, bf16[256,768]{1,0:T(8,128)(2,1)} %get-tuple-element.53.refs_1_, ...), custom_call_target="tpu_custom_call" | custom-call | flops 1610612736 | bytes 8388608 | tf_op jit(solution)/shard_map/pallas_call | solution.py:53
  89.2 7.2 %shard_map.118 = (f32[2,2048,128]{2,1,0:T(8,128)}, f32[2,2048,128]{2,1,0:T(8,128)}) custom-call(s32[3]{0:T(128)} %pad_add_fusion.spot, bf16[256,768]{1,0:T(8,128)(2,1)} %constant_dynamic-slice_fusion.refs_0_, bf16[256,768]{1,0:T(8,128)(2,1)} %get-tuple-element.53.refs_1_, bf16[256,768]{1,0:T(8,128)(2,1)} %get-tuple-element.54.refs_2_, ...), custom_call_target="tpu_custom_call" | custom-call | flops 1610612736 | bytes 10485760 | tf_op jit(solution)/shard_map/pallas_call | solution.py:53
  97.3 1.5 collective-permute-start.21
  99.6 3.3 %collective-permute-done.15 = f32[8,128]{1,0:T(8,128)S(1)} collective-permute-done((f32[8,128]{1,0:T(8,128)}, f32[8,128]{1,0:T(8,128)S(1)}, u32[]{:S(2)}, u32[]{:S(2)}) %collective-permute-start.15) | collective-permute-done | bytes 4128 | tf_op jit(solution)/shard_map/ppermute | solution.py:234
  103.6 1.9 collective-permute-start.16
  105.5 1.7 collective-permute-done.16
  107.2 2.8 %collective-permute-start.17 = (f32[8,128]{1,0:T(8,128)S(1)}, f32[8,128]{1,0:T(8,128)S(1)}, u32[]{:S(2)}, u32[]{:S(2)}) collective-permute-start(f32[8,128]{1,0:T(8,128)S(1)} %add.81), channel_id=1, source_target_pairs={{0,16},{4,20},{8,24},{12,28},{16,0},{20,4},{24,8},{28,12},{1,17},{... | collective-permute-start | bytes 12296 | tf_op jit(solution)/shard_map/ppermute | solution.py:234
  110.1 1.7 collective-permute-done.17
  111.8 1.2 collective-permute-done.18
  112.9 1.5 collective-permute-start.19
  114.4 2.1 collective-permute-done.19
  118.5 6.6 %shard_map.115 = (f32[128,3072]{1,0:T(8,128)}, f32[128,3072]{1,0:T(8,128)}, f32[128,3072]{1,0:T(8,128)}, bf16[128,3072]{1,0:T(8,128)(2,1)}) custom-call(s32[3]{0:T(128)} %pad_add_fusion.spot, f32[8,128]{1,0:T(8,128)} %add.84.refs_0_, f32[128,768]{1,0:T(8,128)} %get-tuple-element.70.refs_1_.refs_13_, bf16[128,768]{1,0:T(8,128)(2,1)} %copy-done.19, ...), custom_call_target="tpu_custom_call" | custom-call | bytes 12582912 | tf_op jit(solution)/shard_map/pallas_call | solution.py:53
  125.2 1.9 collective-permute-start.24
  127.6 2.4 %collective-permute-start.23 = (bf16[128,3072]{1,0:T(8,128)(2,1)}, bf16[128,3072]{1,0:T(8,128)(2,1)S(1)}, u32[]{:S(2)}, u32[]{:S(2)}) collective-permute-start(bf16[128,3072]{1,0:T(8,128)(2,1)} %get-tuple-element.74), channel_id=1, source_target_pairs={{0,24},{4,28},{8,16},{12,20},{16,8},{20,12},{24,0},{28,4},{1,25},{... | collective-permute-start | bytes 2359304 | tf_op jit(solution)/shard_map/ppermute | solution.py:234
  130.0 15.4 %collective-permute-done.24.refs_0_ = bf16[128,3072]{1,0:T(8,128)(2,1)S(1)} collective-permute-done((bf16[128,3072]{1,0:T(8,128)(2,1)}, bf16[128,3072]{1,0:T(8,128)(2,1)S(1)}, u32[]{:S(2)}, u32[]{:S(2)}) %collective-permute-start.24) | collective-permute-done | bytes 786464 | tf_op jit(solution)/shard_map/ppermute | solution.py:234
  146.9 3.5 %broadcast_in_dim.3 = bf16[1024,3072]{1,0:T(8,128)(2,1)} broadcast(bf16[]{:T(256)} %constant.78.clone.1), dimensions={} | broadcast | bytes 6291458 | tf_op jit(solution)/shard_map/broadcast_in_dim | solution.py:242
  151.3 4.7 %shard_map.119 = (f32[2048,128]{1,0:T(8,128)}, f32[2048,128]{1,0:T(8,128)}) custom-call(s32[3]{0:T(128)} %pad_add_fusion.spot, f32[2,2048,128]{2,1,0:T(8,128)} %get-tuple-element.77.refs_0_, f32[2,2048,128]{2,1,0:T(8,128)} %collective-permute-done.32.refs_1_), custom_call_target="tpu_custom_call" | custom-call | bytes 6291456 | tf_op jit(solution)/shard_map/pallas_call | solution.py:53
  156.0 1.6 collective-permute-start.33
  157.6 2.1 constant_dynamic-update-slice_fusion.7
  159.6 3.4 %collective-permute-done.23.refs_0_ = bf16[128,3072]{1,0:T(8,128)(2,1)S(1)} collective-permute-done((bf16[128,3072]{1,0:T(8,128)(2,1)}, bf16[128,3072]{1,0:T(8,128)(2,1)S(1)}, u32[]{:S(2)}, u32[]{:S(2)}) %collective-permute-start.23) | collective-permute-done | bytes 786464 | tf_op jit(solution)/shard_map/ppermute | solution.py:234
  166.3 2.1 constant_dynamic-update-slice_fusion.6
  168.3 2.1 constant_dynamic-update-slice_fusion.5
  170.4 7.8 %collective-permute-done.33.refs_1_ = f32[2048,128]{1,0:T(8,128)} collective-permute-done((f32[2048,128]{1,0:T(8,128)}, f32[2048,128]{1,0:T(8,128)}, u32[]{:S(2)}, u32[]{:S(2)}) %collective-permute-start.33) | collective-permute-done | bytes 1048608 | tf_op jit(solution)/shard_map/ppermute | solution.py:237
  178.2 3.3 %shard_map.120 = (bf16[512,128]{1,0:T(8,128)(2,1)}, bf16[512,128]{1,0:T(8,128)(2,1)}, bf16[512,128]{1,0:T(8,128)(2,1)}, bf16[512,128]{1,0:T(8,128)(2,1)}) custom-call(s32[3]{0:T(128)} %pad_add_fusion.spot, f32[2048,128]{1,0:T(8,128)} %get-tuple-element.79.refs_0_, f32[2048,128]{1,0:T(8,128)} %collective-permute-done.33.refs_1_), custom_call_target="tpu_custom_call" | custom-call | bytes 3145728 | tf_op jit(solution)/shard_map/pallas_call | solution.py:53
  181.5 1.6 collective-permute-start.34
  183.1 1.5 collective-permute-start.35
  184.5 1.4 collective-permute-start.36
  186.0 2.1 constant_dynamic-update-slice_fusion.4
  188.1 1.2 collective-permute-done.34.refs_3_
  189.2 2.7 %collective-permute-done.35.refs_4_ = bf16[512,128]{1,0:T(8,128)(2,1)S(1)} collective-permute-done((bf16[512,128]{1,0:T(8,128)(2,1)}, bf16[512,128]{1,0:T(8,128)(2,1)S(1)}, u32[]{:S(2)}, u32[]{:S(2)}) %collective-permute-start.35) | collective-permute-done | bytes 131104 | tf_op jit(solution)/shard_map/ppermute | solution.py:234
  192.7 1.0 slice.30
  193.7 1.6 collective-permute-start.38
  195.3 1.0 slice.31
  196.3 2.0 collective-permute-start.39
  200.7 2.1 constant_dynamic-update-slice_fusion.3
  202.7 2.1 constant_dynamic-update-slice_fusion.2
  204.8 1.8 collective-permute-done.37.refs_6_
  207.3 4.1 %shard_map.122 = (bf16[256,1024]{1,0:T(8,128)(2,1)}, bf16[256,1024]{1,0:T(8,128)(2,1)}) custom-call(s32[3]{0:T(128)} %pad_add_fusion.spot, bf16[256,1024]{1,0:T(8,128)(2,1)} %refs_0_.3, bf16[256,1024]{1,0:T(8,128)(2,1)} %refs_1_.3, bf16[512,128]{1,0:T(8,128)(2,1)} %get-tuple-element.85.refs_2_, bf16[512,128]{1,0:T(8,128)(2,1)} %get-tuple-element.86.refs_3_, ...), custom_call_target="tpu_custom_call" | custom-call | bytes 4194304 | tf_op jit(solution)/shard_map/pallas_call | solution.py:53
  (106 shorter events, 22.7 us)
Async XLA Ops:
  0.6 1.4 copy-start
  0.6 68.5 %copy-start.3 = (f32[128,3072]{1,0:T(8,128)S(1)}, f32[128,3072]{1,0:T(8,128)}, u32[]{:S(2)}) copy-start(f32[128,3072]{1,0:T(8,128)} %refs_5_.1) | copy-start | bytes 4718596
  2.8 12.9 %collective-permute-start = (bf16[256,768]{1,0:T(8,128)(2,1)}, bf16[256,768]{1,0:T(8,128)(2,1)}, u32[]{:S(2)}, u32[]{:S(2)}) collective-permute-start(bf16[256,768]{1,0:T(8,128)(2,1)} %constant_dynamic-slice_fusion.refs_0_), channel_id=1, source_target_pairs={{0,8},{4,12},{8,0},{12,4},{16,24},{20,28},{24,16},{28,20},{1,9},{5... | collective-permute-start | bytes 1179656 | tf_op jit(solution)/shard_map/ppermute | solution.py:234
  5.8 10.9 %collective-permute-start.1 = (bf16[256,768]{1,0:T(8,128)(2,1)}, bf16[256,768]{1,0:T(8,128)(2,1)}, u32[]{:S(2)}, u32[]{:S(2)}) collective-permute-start(bf16[256,768]{1,0:T(8,128)(2,1)} %constant_dynamic-slice_fusion.refs_0_), channel_id=1, source_target_pairs={{0,4},{4,0},{8,12},{12,8},{16,20},{20,16},{24,28},{28,24},{1,5},{5... | collective-permute-start | bytes 1179656 | tf_op jit(solution)/shard_map/ppermute | solution.py:234
  7.3 18.6 %collective-permute-start.3 = (bf16[256,768]{1,0:T(8,128)(2,1)}, bf16[256,768]{1,0:T(8,128)(2,1)S(1)}, u32[]{:S(2)}, u32[]{:S(2)}) collective-permute-start(bf16[256,768]{1,0:T(8,128)(2,1)} %constant_dynamic-slice_fusion.refs_0_), channel_id=1, source_target_pairs={{0,24},{4,28},{8,16},{12,20},{16,8},{20,12},{24,0},{28,4},{1,25},{... | collective-permute-start | bytes 1179656 | tf_op jit(solution)/shard_map/ppermute | solution.py:234
  16.7 9.2 %collective-permute-start.4 = (bf16[4,128,256]{2,1,0:T(8,128)(2,1)}, bf16[4,128,256]{2,1,0:T(8,128)(2,1)S(1)}, u32[]{:S(2)}, u32[]{:S(2)}) collective-permute-start(bf16[4,128,256]{2,1,0:T(8,128)(2,1)} %get-tuple-element.55), channel_id=1, source_target_pairs={{0,4},{4,0},{8,12},{12,8},{16,20},{20,16},{24,28},{28,24},{1,5},{5... | collective-permute-start | bytes 786440 | tf_op jit(solution)/shard_map/ppermute | solution.py:234
  25.9 0.7 copy-start.17
  26.6 0.7 copy-start.7
  27.3 22.5 %collective-permute-start.5 = (bf16[256,768]{1,0:T(8,128)(2,1)}, bf16[256,768]{1,0:T(8,128)(2,1)S(1)}, u32[]{:S(2)}, u32[]{:S(2)}) collective-permute-start(bf16[256,768]{1,0:T(8,128)(2,1)} %get-tuple-element.56.refs_4_), channel_id=1, source_target_pairs={{0,8},{4,12},{8,0},{12,4},{16,24},{20,28},{24,16},{28,20},{1,9},{5... | collective-permute-start | bytes 1179656 | tf_op jit(solution)/shard_map/ppermute | solution.py:234
  29.2 20.6 %collective-permute-start.6 = (bf16[256,768]{1,0:T(8,128)(2,1)}, bf16[256,768]{1,0:T(8,128)(2,1)S(1)}, u32[]{:S(2)}, u32[]{:S(2)}) collective-permute-start(bf16[256,768]{1,0:T(8,128)(2,1)} %get-tuple-element.56.refs_4_), channel_id=1, source_target_pairs={{0,4},{4,0},{8,12},{12,8},{16,20},{20,16},{24,28},{28,24},{1,5},{5... | collective-permute-start | bytes 1179656 | tf_op jit(solution)/shard_map/ppermute | solution.py:234
  32.5 11.2 %collective-permute-start.7 = (bf16[2,128,256]{2,1,0:T(8,128)(2,1)}, bf16[2,128,256]{2,1,0:T(8,128)(2,1)S(1)}, u32[]{:S(2)}, u32[]{:S(2)}) collective-permute-start(bf16[2,128,256]{2,1,0:T(8,128)(2,1)} %get-tuple-element.60), channel_id=1, source_target_pairs={{0,8},{4,12},{8,0},{12,4},{16,24},{20,28},{24,16},{28,20},{1,9},{5... | collective-permute-start | bytes 393224 | tf_op jit(solution)/shard_map/ppermute | solution.py:234
  33.7 11.8 %collective-permute-start.8 = (bf16[2,128,256]{2,1,0:T(8,128)(2,1)}, bf16[2,128,256]{2,1,0:T(8,128)(2,1)S(1)}, u32[]{:S(2)}, u32[]{:S(2)}) collective-permute-start(bf16[2,128,256]{2,1,0:T(8,128)(2,1)} %get-tuple-element.61), channel_id=1, source_target_pairs={{0,16},{4,20},{8,24},{12,28},{16,0},{20,4},{24,8},{28,12},{1,17},{... | collective-permute-start | bytes 393224 | tf_op jit(solution)/shard_map/ppermute | solution.py:234
  42.3 7.4 %collective-permute-start.9 = (bf16[2,128,256]{2,1,0:T(8,128)(2,1)}, bf16[2,128,256]{2,1,0:T(8,128)(2,1)S(1)}, u32[]{:S(2)}, u32[]{:S(2)}) collective-permute-start(bf16[2,128,256]{2,1,0:T(8,128)(2,1)} %get-tuple-element.62), channel_id=1, source_target_pairs={{0,24},{4,28},{8,16},{12,20},{16,8},{20,12},{24,0},{28,4},{1,25},{... | collective-permute-start | bytes 393224 | tf_op jit(solution)/shard_map/ppermute | solution.py:234
  43.7 6.7 %copy-start.14 = (bf16[2,128,256]{2,1,0:T(8,128)(2,1)}, bf16[2,128,256]{2,1,0:T(8,128)(2,1)S(1)}, u32[]{:S(2)}) copy-start(bf16[2,128,256]{2,1,0:T(8,128)(2,1)S(1)} %collective-permute-done.7.refs_3_) | copy-start | bytes 393220
  45.5 4.3 %copy-start.15 = (bf16[2,128,256]{2,1,0:T(8,128)(2,1)}, bf16[2,128,256]{2,1,0:T(8,128)(2,1)S(1)}, u32[]{:S(2)}) copy-start(bf16[2,128,256]{2,1,0:T(8,128)(2,1)S(1)} %collective-permute-done.8.refs_4_) | copy-start | bytes 393220
  49.8 0.7 copy-start.16
  49.8 0.8 copy-start.8
  50.4 0.7 copy-start.9
  53.1 9.5 %collective-permute-start.13 = (bf16[4,2,128,256]{3,2,1,0:T(8,128)(2,1)}, bf16[4,2,128,256]{3,2,1,0:T(8,128)(2,1)}, u32[]{:S(2)}, u32[]{:S(2)}) collective-permute-start(bf16[4,2,128,256]{3,2,1,0:T(8,128)(2,1)} %pad_maximum_fusion.refs_9_), channel_id=1, source_target_pairs={{0,2},{1,3},{2,0},{3,1},{4,6},{5,7},{6,4},{7,5},{8,10},{9,11},{10,... | collective-permute-start | bytes 1572872 | tf_op jit(solution)/shard_map/ppermute | solution.py:237
  54.7 25.6 %collective-permute-start.12 = (bf16[4,2,128,256]{3,2,1,0:T(8,128)(2,1)}, bf16[4,2,128,256]{3,2,1,0:T(8,128)(2,1)}, u32[]{:S(2)}, u32[]{:S(2)}) collective-permute-start(bf16[4,2,128,256]{3,2,1,0:T(8,128)(2,1)} %pad_maximum_fusion.refs_9_), channel_id=1, source_target_pairs={{0,1},{1,0},{2,3},{3,2},{4,5},{5,4},{6,7},{7,6},{8,9},{9,8},{10,11... | collective-permute-start | bytes 1572872 | tf_op jit(solution)/shard_map/ppermute | solution.py:237
  62.6 17.6 %collective-permute-start.14 = (bf16[4,2,128,256]{3,2,1,0:T(8,128)(2,1)}, bf16[4,2,128,256]{3,2,1,0:T(8,128)(2,1)}, u32[]{:S(2)}, u32[]{:S(2)}) collective-permute-start(bf16[4,2,128,256]{3,2,1,0:T(8,128)(2,1)} %collective-permute-done.13.refs_11_), channel_id=1, source_target_pairs={{0,1},{1,0},{2,3},{3,2},{4,5},{5,4},{6,7},{7,6},{8,9},{9,8},{10,11... | collective-permute-start | bytes 1572872 | tf_op jit(solution)/shard_map/ppermute | solution.py:237
  62.6 12.2 %collective-permute-start.2 = (bf16[256,768]{1,0:T(8,128)(2,1)}, bf16[256,768]{1,0:T(8,128)(2,1)}, u32[]{:S(2)}, u32[]{:S(2)}) collective-permute-start(bf16[256,768]{1,0:T(8,128)(2,1)} %get-tuple-element.54.refs_2_), channel_id=1, source_target_pairs={{0,4},{4,0},{8,12},{12,8},{16,20},{20,16},{24,28},{28,24},{1,5},{5... | collective-permute-start | bytes 1179656 | tf_op jit(solution)/shard_map/ppermute | solution.py:234
  64.3 14.4 %collective-permute-start.10 = (bf16[128,768]{1,0:T(8,128)(2,1)}, bf16[128,768]{1,0:T(8,128)(2,1)}, u32[]{:S(2)}, u32[]{:S(2)}) collective-permute-start(bf16[128,768]{1,0:T(8,128)(2,1)} %slice.24), channel_id=1, source_target_pairs={{0,4},{4,0},{8,12},{12,8},{16,20},{20,16},{24,28},{28,24},{1,5},{5... | collective-permute-start | bytes 589832 | tf_op jit(solution)/shard_map/ppermute | solution.py:234
  67.2 13.0 %collective-permute-start.11 = (bf16[128,768]{1,0:T(8,128)(2,1)S(1)}, bf16[128,768]{1,0:T(8,128)(2,1)}, u32[]{:S(2)}, u32[]{:S(2)}) collective-permute-start(bf16[128,768]{1,0:T(8,128)(2,1)S(1)} %slice.25), channel_id=1, source_target_pairs={{0,8},{4,12},{8,0},{12,4},{16,24},{20,28},{24,16},{28,20},{1,9},{5... | collective-permute-start | bytes 589832 | tf_op jit(solution)/shard_map/ppermute | solution.py:234
  74.9 13.0 %collective-permute-start.29 = (bf16[128,768]{1,0:T(8,128)(2,1)S(1)}, bf16[128,768]{1,0:T(8,128)(2,1)S(1)}, u32[]{:S(2)}, u32[]{:S(2)}) collective-permute-start(bf16[128,768]{1,0:T(8,128)(2,1)S(1)} %get-tuple-element.99), channel_id=1, source_target_pairs={{0,1},{1,0},{2,3},{3,2},{4,5},{5,4},{6,7},{7,6},{8,9},{9,8},{10,11... | collective-permute-start | bytes 589832 | tf_op jit(solution)/shard_map/ppermute | solution.py:237
  78.7 9.2 %collective-permute-start.30 = (bf16[128,768]{1,0:T(8,128)(2,1)S(1)}, bf16[128,768]{1,0:T(8,128)(2,1)S(1)}, u32[]{:S(2)}, u32[]{:S(2)}) collective-permute-start(bf16[128,768]{1,0:T(8,128)(2,1)S(1)} %get-tuple-element.101), channel_id=1, source_target_pairs={{0,2},{1,3},{2,0},{3,1},{4,6},{5,7},{6,4},{7,5},{8,10},{9,11},{10,... | collective-permute-start | bytes 589832 | tf_op jit(solution)/shard_map/ppermute | solution.py:237
  80.2 8.3 %collective-permute-start.31 = (bf16[128,768]{1,0:T(8,128)(2,1)S(1)}, bf16[128,768]{1,0:T(8,128)(2,1)S(1)}, u32[]{:S(2)}, u32[]{:S(2)}) collective-permute-start(bf16[128,768]{1,0:T(8,128)(2,1)S(1)} %get-tuple-element.98), channel_id=1, source_target_pairs={{0,3},{1,2},{2,1},{3,0},{4,7},{5,6},{6,5},{7,4},{8,11},{9,10},{10,... | collective-permute-start | bytes 589832 | tf_op jit(solution)/shard_map/ppermute | solution.py:237
  87.9 0.7 copy-start.22
  87.9 0.7 copy-start.23
  88.5 0.7 copy-start.24
  96.4 54.9 %collective-permute-start.32 = (f32[2,2048,128]{2,1,0:T(8,128)}, f32[2,2048,128]{2,1,0:T(8,128)}, u32[]{:S(2)}, u32[]{:S(2)}) collective-permute-start(f32[2,2048,128]{2,1,0:T(8,128)} %get-tuple-element.78), channel_id=1, source_target_pairs={{0,1},{1,0},{2,3},{3,2},{4,5},{5,4},{6,7},{7,6},{8,9},{9,8},{10,11... | collective-permute-start | bytes 6291464 | tf_op jit(solution)/shard_map/ppermute | solution.py:237
  97.2 19.9 %collective-permute-start.20 = (bf16[128,768]{1,0:T(8,128)(2,1)}, bf16[128,768]{1,0:T(8,128)(2,1)S(1)}, u32[]{:S(2)}, u32[]{:S(2)}) collective-permute-start(bf16[128,768]{1,0:T(8,128)(2,1)} %get-tuple-element.71), channel_id=1, source_target_pairs={{0,1},{1,0},{2,3},{3,2},{4,5},{5,4},{6,7},{7,6},{8,9},{9,8},{10,11... | collective-permute-start | bytes 589832 | tf_op jit(solution)/shard_map/ppermute | solution.py:237
  97.3 19.8 %collective-permute-start.21 = (bf16[128,768]{1,0:T(8,128)(2,1)}, bf16[128,768]{1,0:T(8,128)(2,1)S(1)}, u32[]{:S(2)}, u32[]{:S(2)}) collective-permute-start(bf16[128,768]{1,0:T(8,128)(2,1)} %get-tuple-element.72), channel_id=1, source_target_pairs={{0,2},{1,3},{2,0},{3,1},{4,6},{5,7},{6,4},{7,5},{8,10},{9,11},{10,... | collective-permute-start | bytes 589832 | tf_op jit(solution)/shard_map/ppermute | solution.py:237
  98.8 18.3 %collective-permute-start.22 = (bf16[128,768]{1,0:T(8,128)(2,1)}, bf16[128,768]{1,0:T(8,128)(2,1)S(1)}, u32[]{:S(2)}, u32[]{:S(2)}) collective-permute-start(bf16[128,768]{1,0:T(8,128)(2,1)} %get-tuple-element.73), channel_id=1, source_target_pairs={{0,3},{1,2},{2,1},{3,0},{4,7},{5,6},{6,5},{7,4},{8,11},{9,10},{10,... | collective-permute-start | bytes 589832 | tf_op jit(solution)/shard_map/ppermute | solution.py:237
  99.1 3.8 %collective-permute-start.15 = (f32[8,128]{1,0:T(8,128)}, f32[8,128]{1,0:T(8,128)S(1)}, u32[]{:S(2)}, u32[]{:S(2)}) collective-permute-start(f32[8,128]{1,0:T(8,128)} %get-tuple-element.69), channel_id=1, source_target_pairs={{0,4},{4,0},{8,12},{12,8},{16,20},{20,16},{24,28},{28,24},{1,5},{5... | collective-permute-start | bytes 12296 | tf_op jit(solution)/shard_map/ppermute | solution.py:234
  103.6 3.6 %collective-permute-start.16 = (f32[8,128]{1,0:T(8,128)S(1)}, f32[8,128]{1,0:T(8,128)S(1)}, u32[]{:S(2)}, u32[]{:S(2)}) collective-permute-start(f32[8,128]{1,0:T(8,128)S(1)} %add.80), channel_id=1, source_target_pairs={{0,8},{4,12},{8,0},{12,4},{16,24},{20,28},{24,16},{28,20},{1,9},{5... | collective-permute-start | bytes 12296 | tf_op jit(solution)/shard_map/ppermute | solution.py:234
  107.2 4.5 %collective-permute-start.17 = (f32[8,128]{1,0:T(8,128)S(1)}, f32[8,128]{1,0:T(8,128)S(1)}, u32[]{:S(2)}, u32[]{:S(2)}) collective-permute-start(f32[8,128]{1,0:T(8,128)S(1)} %add.81), channel_id=1, source_target_pairs={{0,16},{4,20},{8,24},{12,28},{16,0},{20,4},{24,8},{28,12},{1,17},{... | collective-permute-start | bytes 12296 | tf_op jit(solution)/shard_map/ppermute | solution.py:234
  111.7 1.2 collective-permute-start.18
  112.9 3.6 %collective-permute-start.19 = (f32[8,128]{1,0:T(8,128)S(1)}, f32[8,128]{1,0:T(8,128)S(1)}, u32[]{:S(2)}, u32[]{:S(2)}) collective-permute-start(f32[8,128]{1,0:T(8,128)S(1)} %add.83), channel_id=1, source_target_pairs={{0,2},{1,3},{2,0},{3,1},{4,6},{5,7},{6,4},{7,5},{8,10},{9,11},{10,... | collective-permute-start | bytes 12296 | tf_op jit(solution)/shard_map/ppermute | solution.py:237
  117.1 0.7 copy-start.19
  117.1 0.7 copy-start.20
  117.9 0.7 copy-start.21
  125.2 20.2 %collective-permute-start.24 = (bf16[128,3072]{1,0:T(8,128)(2,1)}, bf16[128,3072]{1,0:T(8,128)(2,1)S(1)}, u32[]{:S(2)}, u32[]{:S(2)}) collective-permute-start(bf16[128,3072]{1,0:T(8,128)(2,1)} %get-tuple-element.74), channel_id=1, source_target_pairs={{0,8},{4,12},{8,0},{12,4},{16,24},{20,28},{24,16},{28,20},{1,9},{5... | collective-permute-start | bytes 2359304 | tf_op jit(solution)/shard_map/ppermute | solution.py:234
  127.1 18.5 %collective-permute-start.25 = (bf16[128,3072]{1,0:T(8,128)(2,1)}, bf16[128,3072]{1,0:T(8,128)(2,1)}, u32[]{:S(2)}, u32[]{:S(2)}) collective-permute-start(bf16[128,3072]{1,0:T(8,128)(2,1)} %get-tuple-element.74), channel_id=1, source_target_pairs={{0,4},{4,0},{8,12},{12,8},{16,20},{20,16},{24,28},{28,24},{1,5},{5... | collective-permute-start | bytes 2359304 | tf_op jit(solution)/shard_map/ppermute | solution.py:234
  127.6 35.5 %collective-permute-start.23 = (bf16[128,3072]{1,0:T(8,128)(2,1)}, bf16[128,3072]{1,0:T(8,128)(2,1)S(1)}, u32[]{:S(2)}, u32[]{:S(2)}) collective-permute-start(bf16[128,3072]{1,0:T(8,128)(2,1)} %get-tuple-element.74), channel_id=1, source_target_pairs={{0,24},{4,28},{8,16},{12,20},{16,8},{20,12},{24,0},{28,4},{1,25},{... | collective-permute-start | bytes 2359304 | tf_op jit(solution)/shard_map/ppermute | solution.py:234
  145.4 0.9 copy-start.6
  146.4 16.7 %collective-permute-start.26 = (bf16[128,3072]{1,0:T(8,128)(2,1)}, bf16[128,3072]{1,0:T(8,128)(2,1)S(1)}, u32[]{:S(2)}, u32[]{:S(2)}) collective-permute-start(bf16[128,3072]{1,0:T(8,128)(2,1)} %get-tuple-element.75), channel_id=1, source_target_pairs={{0,4},{4,0},{8,12},{12,8},{16,20},{20,16},{24,28},{28,24},{1,5},{5... | collective-permute-start | bytes 2359304 | tf_op jit(solution)/shard_map/ppermute | solution.py:234
  146.8 3.5 %copy-start.13 = (bf16[128,3072]{1,0:T(8,128)(2,1)S(1)}, bf16[128,3072]{1,0:T(8,128)(2,1)}, u32[]{:S(2)}) copy-start(bf16[128,3072]{1,0:T(8,128)(2,1)} %get-tuple-element.74) | copy-start | bytes 2359300
  156.0 22.2 %collective-permute-start.33 = (f32[2048,128]{1,0:T(8,128)}, f32[2048,128]{1,0:T(8,128)}, u32[]{:S(2)}, u32[]{:S(2)}) collective-permute-start(f32[2048,128]{1,0:T(8,128)} %get-tuple-element.80), channel_id=1, source_target_pairs={{0,2},{1,3},{2,0},{3,1},{4,6},{5,7},{6,4},{7,5},{8,10},{9,11},{10,... | collective-permute-start | bytes 3145736 | tf_op jit(solution)/shard_map/ppermute | solution.py:237
  163.1 0.9 copy-start.4
  163.9 0.9 copy-start.5
  164.9 23.2 %collective-permute-start.27 = (bf16[128,3072]{1,0:T(8,128)(2,1)}, bf16[128,3072]{1,0:T(8,128)(2,1)S(1)}, u32[]{:S(2)}, u32[]{:S(2)}) collective-permute-start(bf16[128,3072]{1,0:T(8,128)(2,1)} %get-tuple-element.76), channel_id=1, source_target_pairs={{0,8},{4,12},{8,0},{12,4},{16,24},{20,28},{24,16},{28,20},{1,9},{5... | collective-permute-start | bytes 2359304 | tf_op jit(solution)/shard_map/ppermute | solution.py:234
  165.5 22.5 %collective-permute-start.28 = (bf16[128,3072]{1,0:T(8,128)(2,1)}, bf16[128,3072]{1,0:T(8,128)(2,1)S(1)}, u32[]{:S(2)}, u32[]{:S(2)}) collective-permute-start(bf16[128,3072]{1,0:T(8,128)(2,1)} %get-tuple-element.76), channel_id=1, source_target_pairs={{0,4},{4,0},{8,12},{12,8},{16,20},{20,16},{24,28},{28,24},{1,5},{5... | collective-permute-start | bytes 2359304 | tf_op jit(solution)/shard_map/ppermute | solution.py:234
  181.5 7.7 %collective-permute-start.34 = (bf16[512,128]{1,0:T(8,128)(2,1)}, bf16[512,128]{1,0:T(8,128)(2,1)S(1)}, u32[]{:S(2)}, u32[]{:S(2)}) collective-permute-start(bf16[512,128]{1,0:T(8,128)(2,1)} %get-tuple-element.82), channel_id=1, source_target_pairs={{0,8},{4,12},{8,0},{12,4},{16,24},{20,28},{24,16},{28,20},{1,9},{5... | collective-permute-start | bytes 393224 | tf_op jit(solution)/shard_map/ppermute | solution.py:234
  183.1 8.9 %collective-permute-start.35 = (bf16[512,128]{1,0:T(8,128)(2,1)}, bf16[512,128]{1,0:T(8,128)(2,1)S(1)}, u32[]{:S(2)}, u32[]{:S(2)}) collective-permute-start(bf16[512,128]{1,0:T(8,128)(2,1)} %get-tuple-element.83), channel_id=1, source_target_pairs={{0,16},{4,20},{8,24},{12,28},{16,0},{20,4},{24,8},{28,12},{1,17},{... | collective-permute-start | bytes 393224 | tf_op jit(solution)/shard_map/ppermute | solution.py:234
  184.5 7.4 %collective-permute-start.36 = (bf16[512,128]{1,0:T(8,128)(2,1)}, bf16[512,128]{1,0:T(8,128)(2,1)S(1)}, u32[]{:S(2)}, u32[]{:S(2)}) collective-permute-start(bf16[512,128]{1,0:T(8,128)(2,1)} %get-tuple-element.84), channel_id=1, source_target_pairs={{0,24},{4,28},{8,16},{12,20},{16,8},{20,12},{24,0},{28,4},{1,25},{... | collective-permute-start | bytes 393224 | tf_op jit(solution)/shard_map/ppermute | solution.py:234
  188.0 3.9 %copy-start.1 = (bf16[128,3072]{1,0:T(8,128)(2,1)}, bf16[128,3072]{1,0:T(8,128)(2,1)S(1)}, u32[]{:S(2)}) copy-start(bf16[128,3072]{1,0:T(8,128)(2,1)S(1)} %collective-permute-done.27.refs_0_) | copy-start | bytes 2359300
  188.0 3.9 %copy-start.2 = (bf16[128,3072]{1,0:T(8,128)(2,1)}, bf16[128,3072]{1,0:T(8,128)(2,1)S(1)}, u32[]{:S(2)}) copy-start(bf16[128,3072]{1,0:T(8,128)(2,1)S(1)} %collective-permute-done.28.refs_1_) | copy-start | bytes 2359300
  189.2 2.8 %copy-start.10 = (bf16[512,128]{1,0:T(8,128)(2,1)}, bf16[512,128]{1,0:T(8,128)(2,1)S(1)}, u32[]{:S(2)}) copy-start(bf16[512,128]{1,0:T(8,128)(2,1)S(1)} %collective-permute-done.34.refs_3_) | copy-start | bytes 393220
  192.0 0.7 copy-start.12
  193.7 17.7 %collective-permute-start.38 = (bf16[64,3072]{1,0:T(8,128)(2,1)S(1)}, bf16[64,3072]{1,0:T(8,128)(2,1)S(1)}, u32[]{:S(2)}, u32[]{:S(2)}) collective-permute-start(bf16[64,3072]{1,0:T(8,128)(2,1)S(1)} %slice.30), channel_id=1, source_target_pairs={{0,4},{4,0},{8,12},{12,8},{16,20},{20,16},{24,28},{28,24},{1,5},{5... | collective-permute-start | bytes 1179656 | tf_op jit(solution)/shard_map/ppermute | solution.py:234
  196.3 15.8 %collective-permute-start.39 = (bf16[64,3072]{1,0:T(8,128)(2,1)S(1)}, bf16[64,3072]{1,0:T(8,128)(2,1)S(1)}, u32[]{:S(2)}, u32[]{:S(2)}) collective-permute-start(bf16[64,3072]{1,0:T(8,128)(2,1)S(1)} %slice.31), channel_id=1, source_target_pairs={{0,8},{4,12},{8,0},{12,4},{16,24},{20,28},{24,16},{28,20},{1,9},{5... | collective-permute-start | bytes 1179656 | tf_op jit(solution)/shard_map/ppermute | solution.py:234
  200.1 6.4 %collective-permute-start.37 = (bf16[4,256,128]{2,1,0:T(8,128)(2,1)S(1)}, bf16[4,256,128]{2,1,0:T(8,128)(2,1)S(1)}, u32[]{:S(2)}, u32[]{:S(2)}) collective-permute-start(bf16[4,256,128]{2,1,0:T(8,128)(2,1)S(1)} %pad_maximum_fusion.1), channel_id=1, source_target_pairs={{0,4},{4,0},{8,12},{12,8},{16,20},{20,16},{24,28},{28,24},{1,5},{5... | collective-permute-start | bytes 786440 | tf_op jit(solution)/shard_map/ppermute | solution.py:234
  206.6 0.7 copy-start.18
  (1 other events, 0.7 us)

commit v3 on v2

--- a/solution.py
+++ b/solution.py
@@ -12,29 +12,78 @@
 F32 = jnp.float32
 SMEM = pl.BlockSpec(memory_space=pltpu.SMEM)
 HBM = pl.BlockSpec(memory_space=pltpu.HBM)
+ANY = pl.BlockSpec(memory_space=pl.ANY)
+NEAR = pl.BlockSpec(memory_space=pltpu.VMEM)
+
+MIDDLE = ((1, 2), (2, 1))
+ROUND = ((0, 3), (3, 0))
+
 
 def shaped(shape, dtype):
     return jax.ShapeDtypeStruct(shape, dtype)
 
 
-def call(body, outs, args, flops=0, moved=0, limit=60, after=()):
-    args, after = tuple(args), tuple(after)
-    n_in, n_out = len(args) - 1, len(outs)
+class Near:
+    def __init__(self, value):
+        self.value = value
+
+
+class Joined:
+    def __init__(self, shape, dtype, parts):
+        self.shape, self.dtype, self.parts = shape, dtype, parts
+
+
+def call(body, outs, args, flops=0, moved=0, limit=24, after=()):
+    spot, *args = args
+    n_in, n_out = len(args), len(outs)
+    flat, specs, scratch, todo = [], [], [], []
+
+    def operand(value, spec):
+        for i, old in enumerate(flat):
+            if old is value and specs[i] is spec:
+                return i
+        flat.append(value)
+        specs.append(spec)
+        return len(flat) - 1
+
+    for i, arg in enumerate(args):
+        if isinstance(arg, Near):
+            todo.append(operand(arg.value, NEAR))
+            continue
+        scratch.append(pltpu.VMEM(arg.shape, arg.dtype))
+        steps = []
+        for value, source, target in arg.parts if isinstance(arg, Joined) else ((arg, None, None),):
+            steps.append((operand(value, ANY), source, target))
+        todo.append(steps)
+    count = sum(len(steps) for steps in todo if not isinstance(steps, int))
 
     def kernel(spot, *refs):
-        given, refs = refs[:n_in], refs[n_in + len(after) :]
+        given, refs = refs[: len(flat)], refs[len(flat) + len(after) :]
         results, refs = refs[:n_out], refs[n_out:]
-        ins, parts, in_sems, out_sems = refs[:n_in], refs[n_in : n_in + n_out], refs[-2], refs[-1]
-        loads = [pltpu.make_async_copy(g, v, in_sems.at[i]) for i, (g, v) in enumerate(zip(given, ins))]
-        for load in loads:
-            load.start()
-        waiting, sent = set(range(n_in)), []
+        slots, parts = list(refs[: len(scratch)]), refs[len(scratch) : len(scratch) + n_out]
+        in_sems, out_sems = refs[-2], refs[-1]
+        ins, loads, used = [], {}, 0
+        for i, steps in enumerate(todo):
+            if isinstance(steps, int):
+                ins.append(given[steps])
+                continue
+            ins.append(slots.pop(0))
+            loads[i] = []
+            for k, source, target in steps:
+                copy = pltpu.make_async_copy(
+                    given[k] if source is None else given[k].at[source],
+                    ins[i] if target is None else ins[i].at[target],
+                    in_sems.at[used],
+                )
+                used += 1
+                copy.start()
+                loads[i].append(copy)
+        sent = []
 
         def need(*which):
             for i in which:
-                if i in waiting:
-                    loads[i].wait()
-                    waiting.remove(i)
+                for load in loads.pop(i, ()):
+                    load.wait()
 
         def done(o, *index):
             copy = pltpu.make_async_copy(
@@ -53,14 +102,14 @@
     return pl.pallas_call(
         kernel,
         out_shape=tuple(outs),
-        in_specs=[SMEM] + [HBM] * (n_in + len(after)),
+        in_specs=[SMEM] + specs + [HBM] * len(after),
         out_specs=(HBM,) * n_out,
-        scratch_shapes=[pltpu.VMEM(a.shape, a.dtype) for a in args[1:]]
+        scratch_shapes=scratch
         + [pltpu.VMEM(o.shape, o.dtype) for o in outs]
-        + [pltpu.SemaphoreType.DMA((n_in,)), pltpu.SemaphoreType.DMA((32,))],
+        + [pltpu.SemaphoreType.DMA((max(1, count),)), pltpu.SemaphoreType.DMA((32,))],
         compiler_params=pltpu.CompilerParams(vmem_limit_bytes=limit << 20),
         cost_estimate=pl.CostEstimate(flops=flops, bytes_accessed=moved, transcendentals=0),
-    )(*args, *after)
+    )(spot, *flat, *after)
 
 
 def hidden_body(spot, ins, outs, need, done):
@@ -88,52 +137,53 @@
         done(m)
 
 
-def in_pairs(pieces):
-    own, own_x, near, near_x, last, last_x, far, low, high = pieces
-    return [((i,), lambda p=p: p[...]) for i, p in enumerate((own, own_x, near, near_x))] + [
-        ((6,), lambda: far[...]),
-        ((7, 8), lambda: jnp.concatenate([low[...], high[...]], axis=0)),
-        ((4,), lambda: last[...]),
-        ((5,), lambda: last_x[...]),
-    ]
+def tokens_in_rows(pieces):
+    size, cols = pieces[0].shape
+    parts = []
+    for m, piece in enumerate(pieces):
+        piece = piece if isinstance(piece, tuple) else (piece,)
+        rows = size // len(piece)
+        parts += [(p, None, (pl.ds(m * size + i * rows, rows),)) for i, p in enumerate(piece)]
+    return Joined((len(pieces) * size, cols), pieces[0].dtype, parts)
+
+
+def tokens_in_columns(hiddens):
+    _, _, part, size = hiddens[0].shape
+    parts = []
+    for i, h in enumerate(hiddens):
+        for m in range(CELL):
+            parts.append((h, (m // 2, m % 2), (pl.ds(i * part, part), pl.ds(m * size, size))))
+    return Joined((4 * part, CELL * size), hiddens[0].dtype, parts)
 
 
 def grad_body(spot, ins, outs, need, done):
     del spot
-    pieces, hidden, squares = ins[:9], ins[9:], outs[4]
+    left, right = ins
     part = outs[0].shape[0]
-    total = None
-    for m, (numbers, right) in enumerate(in_pairs(pieces)):
-        need(*numbers, *range(9, 13))
-        left = jnp.concatenate([h[m // 2, m % 2] for h in hidden], axis=0)
-        term = jnp.dot(left, right(), preferred_element_type=F32)
-        total = term if total is None else total + term
+    need(0, 1)
+    total = jnp.dot(left[...], right[...], preferred_element_type=F32)
     for i in (3, 2, 1, 0):
         outs[i][...] = total[i * part : (i + 1) * part].astype(outs[i].dtype)
         done(i)
-    squares[...] = jnp.broadcast_to(jnp.sum(total * total), squares.shape)
+    outs[4][...] = jnp.broadcast_to(jnp.sum(total * total), outs[4].shape)
     done(4)
 
 
 def d_hidden_body(spot, ins, outs, need, done):
     del spot
-    pieces, weights = ins[:9], ins[9:]
+    pieces, weights = ins
     keep, give = outs
-    part = weights[0].shape[0]
-    tokens = pieces[0].shape[0]
-    need(*range(9, 13))
-    weight = jnp.concatenate([w[...] for w in weights], axis=0)
-    for m, (numbers, side) in enumerate(in_pairs(pieces)):
-        need(*numbers)
-        out = lax.dot_general(side(), weight, (((1,), (1,)), ((), ())), preferred_element_type=F32)
-        rows = slice(m * tokens, (m + 1) * tokens)
-        keep[0, rows] = out[:, :part]
-        give[0, rows] = out[:, part : 2 * part]
-        keep[1, rows] = out[:, 2 * part : 3 * part]
-        give[1, rows] = out[:, 3 * part :]
+    part = weights.shape[0] // 4
+    tokens = pieces.shape[0] // CELL
+    need(0, 1)
+    weight = weights[...].T
+    for m in range(CELL):
         at = pl.ds(m * tokens, tokens)
+        out = jnp.dot(pieces[at, :], weight, preferred_element_type=F32)
+        for i, into in ((1, give), (3, give), (0, keep), (2, keep)):
+            into[i // 2, at] = out[:, i * part : (i + 1) * part]
+        done(1, slice(None), at)
         done(0, slice(None), at)
-        done(1, slice(None), at)
 
 
 def add_body(spot, ins, outs, need, done):
@@ -214,7 +264,7 @@
         in_specs=[HBM] * len(values),
         out_specs=(HBM,) * len(values),
         input_output_aliases={i: i for i in range(len(values))},
-        compiler_params=pltpu.CompilerParams(vmem_limit_bytes=60 << 20),
+        compiler_params=pltpu.CompilerParams(vmem_limit_bytes=8 << 20),
     )(*values)
 
 
@@ -233,6 +283,10 @@
     def across(value, m):
         return lax.ppermute(value, "dp", [(i, i ^ m) for i in range(n)])
 
+    def line(value, pairs):
+        steps = [(i, b) for i in range(n) for a, b in pairs if i % CELL // 2 == a]
+        return lax.ppermute(value, "dp", [(i, i - i % CELL + b * 2 + i % 2) for i, b in steps])
+
     def swap(value, m):
         return lax.ppermute(value, "tensor", [(i, i ^ m) for i in range(4)])
 
@@ -257,12 +311,14 @@
 
     own = lax.dynamic_slice(d_out, (0, t * cols), (tokens, cols))
     half = tokens // 2
-    near, own_x, last = across(own, 2), across(own, 1), across(own, 6)
+    ends = (z == 0) | (z == 3)
+    near, own_x, mid = across(own, 2), across(own, 1), line(own, MIDDLE)
     block = shaped((4, part, tokens), BF16)
     kept, given = call(hidden_body, (block, block), (spot, gate, up_proj), moved=2 << 20)
-    near, own_x, given = together(near, own_x, given)
-    near_x, came = across(near, 1), across(given, 1)
-    last, came = together(last, came)
+    near, own_x, mid, given, own = together(near, own_x, mid, given, own)
+    end, near_x, came = line(own, ROUND), across(near, 1), across(given, 1)
+    end, near_x, came = together(end, near_x, came)
+    last = jnp.where(ends, end, mid)
     far, last_x = across(last, 2), across(last, 1)
     pair = shaped((2, part, tokens), BF16)
     blocks = call(turn_body, (pair,) * 4, (spot, kept, came), moved=1 << 20)
@@ -271,6 +327,7 @@
     low, high = across(far[:half], 1), across(last_x[half:], 2)
     hidden = jnp.stack(blocks)
     hidden_y, hidden_c = swap(hidden, 2), swap(hidden, 1)
+    low, high, hidden_y = together(low, high, hidden_y)
     hiddens = (hidden, hidden_c, hidden_y, swap(hidden_y, 1))
     weight = master
     if outer > 1:
@@ -281,16 +338,17 @@
         lax.dynamic_slice(weight, (0, (t ^ m) * cols), (part, cols)).astype(BF16) for m in range(4)
     ]
     weights = [weights[0]] + [swap(weights[m], m) for m in (1, 2, 3)]
-    pieces = (own, own_x, near, near_x, last, last_x, far, low, high)
+    pieces = tokens_in_rows((own, own_x, near, near_x, far, (low, high), last, last_x))
 
     flops = 2 * 4 * part * CELL * tokens * cols
     piece, sent = shaped((part, cols), F32), shaped((part, cols), BF16)
     *grads, total = call(
         grad_body,
         (piece, sent, sent, sent, shaped((8, 128), F32)),
-        (spot, *pieces, *hiddens),
+        (spot, tokens_in_columns(hiddens), pieces),
         flops=flops,
         moved=8 << 20,
+        limit=52,
     )
     if outer > 1:
         grads = lax.psum_scatter(
@@ -310,12 +368,16 @@
     grads = [grads[0]] + [swap(grads[m], m) for m in (1, 2, 3)]
 
     sums = shaped((2, CELL * tokens, part), F32)
+    weights = Joined(
+        (4 * part, cols), BF16, [(w, None, (pl.ds(m * part, part),)) for m, w in enumerate(weights)]
+    )
     keep, give = call(
         d_hidden_body,
         (sums, sums),
-        (spot, *pieces, *weights),
+        (spot, pieces, weights),
         flops=flops,
         moved=10 << 20,
+        limit=52,
         after=(grad_own,),
     )
     give = swap(give, 1)
@@ -333,13 +395,13 @@
         )
     own = shard_next
     half = own.shape[0] // 2
-    near, own_x, last = across(own, 2), across(own, 1), across(own, 6)
+    near, own_x, mid = across(own, 2), across(own, 1), line(own, MIDDLE)
     mine_sum = shaped((CELL * tokens, part), F32)
     mine, sent = call(add_body, (mine_sum,) * 2, (spot, keep, give), moved=6 << 20)
-    came = swap(sent, 2)
-    near, own_x = together(near, own_x)
-    near_x = across(near, 1)
-    last, near_x = together(last, near_x)
+    near, own_x, mid, sent, own = together(near, own_x, mid, sent, own)
+    end, near_x, came = line(own, ROUND), across(near, 1), swap(sent, 2)
+    end, near_x = together(end, near_x)
+    last = jnp.where(ends, end, mid)
     far, last_x = across(last, 2), across(last, 1)
     pair = shaped((2 * tokens, part), BF16)
     blocks = call(back_body, (pair,) * 4, (spot, mine, came), moved=3 << 20)

time: 214 us -> 197 us (0.921)
  local copies, waits for them, and re-layouts: 36.5 us -> 16.7 us
  waiting for transfers between devices: 76.5 us -> 87.3 us
  Pallas kernels: 39.6 us -> 30.9 us
    ppermute x13, waiting for transfers between devices: 19.6 us -> 5.43 us  [swap(): return lax.ppermute(value, 'tensor', [(i, i ^ m) for i in range(4)])]
    ppermute x0 -> x4, waiting for transfers between devices: none -> 13.5 us  [line(): lax.ppermute(value, 'dp', [(i, i - i % CELL + b * 2 + i % 2) for i, b in...]
    ppermute x27 -> x25, waiting for transfers between devices: 56.9 us -> 68.4 us  [across(): return lax.ppermute(value, 'dp', [(i, i ^ m) for i in range(n)])]
    ppermute x0 -> x4, starting transfers between devices: none -> 11.4 us  [line(): lax.ppermute(value, 'dp', [(i, i - i % CELL + b * 2 + i % 2) for i, b in...]
    dynamic_update_slice x9 -> x8, local copies, waits for them, and re-layouts: 14.9 us -> 4.82 us  [in_order(): out = lax.dynamic_update_slice(out, value, (at, 0))]
    ppermute x27 -> x25, starting transfers between devices: 46.5 us -> 36.6 us  [across(): return lax.ppermute(value, 'dp', [(i, i ^ m) for i in range(n)])]
    pallas_call x8, Pallas kernels: 39.6 us -> 30.9 us  [call(): pl.pallas_call(kernel, out_shape=tuple(outs), in_specs=[SMEM] + specs + [...]
    slice x4, local copies, waits for them, and re-layouts: 4.6 us -> 0.08 us  [on_device(): low, high = (across(far[:half], 1), across(last_x[half:], 2))]
  transfers between devices with their start and end apart: 40 -> 42, of which waited for: 21 -> 19; matrix products, arithmetic and copies ran while one was open for 12% -> 4% of each run, Pallas kernels for 15% -> 13%
where the time goes in v3:
time: 197 us
  waiting for transfers between devices  87.3 us (44%)
  starting transfers between devices  57.2 us (29%)
  Pallas kernels  30.9 us (16%)
  local copies, waits for them, and re-layouts  16.7 us (8%)
  other arithmetic  3.28 us (2%)
    ppermute x25, waiting for transfers between devices, across(): return lax.ppermute(value, 'dp', [(i, i ^ m) for i in range(n)])  68.4 us
    ppermute x25, starting transfers between devices, across(): return lax.ppermute(value, 'dp', [(i, i ^ m) for i in range(n)])  36.6 us
    pallas_call x8, Pallas kernels, call(): pl.pallas_call(kernel, out_shape=tuple(outs), in_specs=[SMEM] + specs + [...  30.9 us
    ppermute x4, waiting for transfers between devices, line(): lax.ppermute(value, 'dp', [(i, i - i % CELL + b * 2 + i % 2) for i, b in...  13.5 us
    ppermute x4, starting transfers between devices, line(): lax.ppermute(value, 'dp', [(i, i - i % CELL + b * 2 + i % 2) for i, b in...  11.4 us
    unnamed x46, local copies, waits for them, and re-layouts  10 us
    ppermute x13, starting transfers between devices, swap(): return lax.ppermute(value, 'tensor', [(i, i ^ m) for i in range(4)])  9.2 us
    ppermute x13, waiting for transfers between devices, swap(): return lax.ppermute(value, 'tensor', [(i, i ^ m) for i in range(4)])  5.43 us
  transfers between devices with their start and end apart: 42, of which 19 were waited for; matrix products, arithmetic and copies ran while one was open for 4% of the time, Pallas kernels for 13%

profile of v3, /device:TPU:0, one launch (start us, length us, event | category | flops | bytes accessed | tf_op | source)
XLA Modules:
  0.0 196.5 jit_solution(12858062151248148515)
XLA Ops:
  0.7 1.4 copy-done
  2.1 3.1 %collective-permute-start = (bf16[256,768]{1,0:T(8,128)(2,1)S(1)}, bf16[256,768]{1,0:T(8,128)(2,1)}, u32[]{:S(2)}, u32[]{:S(2)}) collective-permute-start(bf16[256,768]{1,0:T(8,128)(2,1)S(1)} %constant_dynamic-slice_fusion.refs_4_), channel_id=1, source_target_pairs={{0,8},{4,12},{8,0},{12,4},{16,24},{20,28},{24,16},{28,20},{1,9},{5... | collective-permute-start | bytes 1179656 | tf_op jit(solution)/shard_map/ppermute | solution.py:284
  5.2 1.5 collective-permute-start.1
  6.7 1.4 collective-permute-start.2
  8.2 1.0 copy-done.3
  9.2 1.0 copy-done.5
  10.3 2.0 %shard_map.109 = (bf16[4,128,256]{2,1,0:T(8,128)(2,1)S(1)}, bf16[4,128,256]{2,1,0:T(8,128)(2,1)}) custom-call(s32[3]{0:T(128)S(1)} %pad_add_fusion.spot, bf16[256,1024]{1,0:T(8,128)(2,1)S(1)} %copy-done.3, bf16[256,1024]{1,0:T(8,128)(2,1)S(1)} %copy-done.5), custom_call_target="tpu_custom_call" | custom-call | bytes 2097152 | tf_op jit(solution)/shard_map/pallas_call | solution.py:102
  12.3 2.1 %collective-permute-done.refs_0_ = bf16[256,768]{1,0:T(8,128)(2,1)} collective-permute-done((bf16[256,768]{1,0:T(8,128)(2,1)S(1)}, bf16[256,768]{1,0:T(8,128)(2,1)}, u32[]{:S(2)}, u32[]{:S(2)}) %collective-permute-start) | collective-permute-done | bytes 393248 | tf_op jit(solution)/shard_map/ppermute | solution.py:284
  14.4 1.5 collective-permute-done.1.refs_1_
  15.9 4.4 %collective-permute-start.3 = (bf16[256,768]{1,0:T(8,128)(2,1)S(1)}, bf16[256,768]{1,0:T(8,128)(2,1)}, u32[]{:S(2)}, u32[]{:S(2)}) collective-permute-start(bf16[256,768]{1,0:T(8,128)(2,1)S(1)} %get-tuple-element.62.refs_4_.refs_0_), channel_id=1, source_target_pairs={{0,24},{4,28},{24,0},{28,4},{1,25},{5,29},{25,1},{29,5},{2,26},{6,... | collective-permute-start | bytes 1179656 | tf_op jit(solution)/shard_map/ppermute | solution.py:288
  20.2 1.6 collective-permute-start.4
  22.3 13.5 %collective-permute-done.5.refs_2_ = bf16[4,128,256]{2,1,0:T(8,128)(2,1)} collective-permute-done((bf16[4,128,256]{2,1,0:T(8,128)(2,1)}, bf16[4,128,256]{2,1,0:T(8,128)(2,1)}, u32[]{:S(2)}, u32[]{:S(2)}) %collective-permute-start.5) | collective-permute-done | bytes 262176 | tf_op jit(solution)/shard_map/ppermute | solution.py:284
  35.8 1.0 broadcast_select_fusion.1.refs_11_.refs_7_
  36.9 1.7 collective-permute-start.6
  39.0 0.9 copy-done.14
  40.0 2.5 %shard_map.112 = (bf16[2,128,256]{2,1,0:T(8,128)(2,1)S(1)}, bf16[2,128,256]{2,1,0:T(8,128)(2,1)S(1)}, bf16[2,128,256]{2,1,0:T(8,128)(2,1)S(1)}, bf16[2,128,256]{2,1,0:T(8,128)(2,1)S(1)}) custom-call(s32[3]{0:T(128)S(1)} %pad_add_fusion.spot, bf16[4,128,256]{2,1,0:T(8,128)(2,1)S(1)} %copy-done.14, bf16[4,128,256]{2,1,0:T(8,128)(2,1)} %get-tuple-element.68.refs_1_), custom_call_target="tpu_custom_call" | custom-call | bytes 1048576 | tf_op jit(solution)/shard_map/pallas_call | solution.py:102
  42.5 2.4 %collective-permute-start.10 = (bf16[2,128,256]{2,1,0:T(8,128)(2,1)S(1)}, bf16[2,128,256]{2,1,0:T(8,128)(2,1)S(1)}, u32[]{:S(2)}, u32[]{:S(2)}) collective-permute-start(bf16[2,128,256]{2,1,0:T(8,128)(2,1)S(1)} %get-tuple-element.72), channel_id=1, source_target_pairs={{0,24},{4,28},{8,16},{12,20},{16,8},{20,12},{24,0},{28,4},{1,25},{... | collective-permute-start | bytes 393224 | tf_op jit(solution)/shard_map/ppermute | solution.py:284
  44.9 2.0 %collective-permute-start.9 = (bf16[2,128,256]{2,1,0:T(8,128)(2,1)S(1)}, bf16[2,128,256]{2,1,0:T(8,128)(2,1)S(1)}, u32[]{:S(2)}, u32[]{:S(2)}) collective-permute-start(bf16[2,128,256]{2,1,0:T(8,128)(2,1)S(1)} %get-tuple-element.71), channel_id=1, source_target_pairs={{0,16},{4,20},{8,24},{12,28},{16,0},{20,4},{24,8},{28,12},{1,17},{... | collective-permute-start | bytes 393224 | tf_op jit(solution)/shard_map/ppermute | solution.py:284
  47.0 6.0 %collective-permute-done.10.refs_5_ = bf16[2,128,256]{2,1,0:T(8,128)(2,1)S(1)} collective-permute-done((bf16[2,128,256]{2,1,0:T(8,128)(2,1)S(1)}, bf16[2,128,256]{2,1,0:T(8,128)(2,1)S(1)}, u32[]{:S(2)}, u32[]{:S(2)}) %collective-permute-start.10) | collective-permute-done | bytes 131104 | tf_op jit(solution)/shard_map/ppermute | solution.py:284
  53.0 1.0 collective-permute-done.8.refs_3_
  54.0 1.0 pad_maximum_fusion.refs_0_
  55.0 1.5 collective-permute-start.14
  56.5 1.6 collective-permute-start.12
  58.1 1.4 collective-permute-start.13
  59.5 2.8 %collective-permute-done.12.refs_0_ = bf16[128,768]{1,0:T(8,128)(2,1)S(1)} collective-permute-done((bf16[128,768]{1,0:T(8,128)(2,1)S(1)}, bf16[128,768]{1,0:T(8,128)(2,1)S(1)}, u32[]{:S(2)}, u32[]{:S(2)}) %collective-permute-start.12) | collective-permute-done | bytes 196640 | tf_op jit(solution)/shard_map/ppermute | solution.py:284
  62.3 1.6 collective-permute-done.13.refs_1_
  63.8 2.1 %collective-permute-done.14.refs_2_ = bf16[4,2,128,256]{3,2,1,0:T(8,128)(2,1)} collective-permute-done((bf16[4,2,128,256]{3,2,1,0:T(8,128)(2,1)}, bf16[4,2,128,256]{3,2,1,0:T(8,128)(2,1)}, u32[]{:S(2)}, u32[]{:S(2)}) %collective-permute-start.14) | collective-permute-done | bytes 524320 | tf_op jit(solution)/shard_map/ppermute | solution.py:291
  68.1 1.5 collective-permute-start.28
  71.5 7.1 %shard_map.115 = (f32[128,768]{1,0:T(8,128)S(1)}, bf16[128,768]{1,0:T(8,128)(2,1)S(1)}, bf16[128,768]{1,0:T(8,128)(2,1)S(1)}, bf16[128,768]{1,0:T(8,128)(2,1)S(1)}, f32[8,128]{1,0:T(8,128)S(1)}) custom-call(s32[3]{0:T(128)S(1)} %pad_add_fusion.spot, bf16[4,2,128,256]{3,2,1,0:T(8,128)(2,1)} %pad_maximum_fusion.refs_0_, ...), custom_call_target="tpu_custom_call" | custom-call | flops 1610612736 | bytes 8388608 | tf_op jit(solution)/shard_map/pallas_call | solution.py:102
  79.4 5.5 %shard_map.117 = (f32[2,2048,128]{2,1,0:T(8,128)}, f32[2,2048,128]{2,1,0:T(8,128)}) custom-call(s32[3]{0:T(128)S(1)} %pad_add_fusion.spot, bf16[256,768]{1,0:T(8,128)(2,1)S(1)} %get-tuple-element.62.refs_4_.refs_0_, bf16[256,768]{1,0:T(8,128)(2,1)} %get-tuple-element.80.refs_5_.refs_1_, bf16[256,768]{1,0:T(8,128)(2,1)} %get-tuple-element.63.refs_6_.refs_2_, ...), custom_call_target="tpu_custom_call" | custom-call | flops 1610612736 | bytes 10485760 | tf_op jit(solution)/shard_map/pallas_call | solution.py:102
  85.6 1.5 collective-permute-start.22
  87.4 2.4 %collective-permute-start.16 = (f32[8,128]{1,0:T(8,128)S(1)}, f32[8,128]{1,0:T(8,128)S(1)}, u32[]{:S(2)}, u32[]{:S(2)}) collective-permute-start(f32[8,128]{1,0:T(8,128)S(1)} %get-tuple-element.84), channel_id=1, source_target_pairs={{0,4},{4,0},{8,12},{12,8},{16,20},{20,16},{24,28},{28,24},{1,5},{5... | collective-permute-start | bytes 12296 | tf_op jit(solution)/shard_map/ppermute | solution.py:284
  89.8 1.6 collective-permute-done.16
  91.4 1.9 collective-permute-start.17
  93.3 1.7 collective-permute-done.17
  95.0 2.4 %collective-permute-start.18 = (f32[8,128]{1,0:T(8,128)S(1)}, f32[8,128]{1,0:T(8,128)S(1)}, u32[]{:S(2)}, u32[]{:S(2)}) collective-permute-start(f32[8,128]{1,0:T(8,128)S(1)} %add.81), channel_id=1, source_target_pairs={{0,16},{4,20},{8,24},{12,28},{16,0},{20,4},{24,8},{28,12},{1,17},{... | collective-permute-start | bytes 12296 | tf_op jit(solution)/shard_map/ppermute | solution.py:284
  97.5 2.1 %collective-permute-done.18 = f32[8,128]{1,0:T(8,128)S(1)} collective-permute-done((f32[8,128]{1,0:T(8,128)S(1)}, f32[8,128]{1,0:T(8,128)S(1)}, u32[]{:S(2)}, u32[]{:S(2)}) %collective-permute-start.18) | collective-permute-done | bytes 4128 | tf_op jit(solution)/shard_map/ppermute | solution.py:284
  99.5 1.2 collective-permute-done.19
  100.7 1.5 collective-permute-start.20
  102.2 2.1 %collective-permute-done.20 = f32[8,128]{1,0:T(8,128)S(1)} collective-permute-done((f32[8,128]{1,0:T(8,128)S(1)}, f32[8,128]{1,0:T(8,128)S(1)}, u32[]{:S(2)}, u32[]{:S(2)}) %collective-permute-start.20) | collective-permute-done | bytes 4128 | tf_op jit(solution)/shard_map/ppermute | solution.py:291
  104.4 5.1 %shard_map.116 = (f32[128,3072]{1,0:T(8,128)}, f32[128,3072]{1,0:T(8,128)}, f32[128,3072]{1,0:T(8,128)}, bf16[128,3072]{1,0:T(8,128)(2,1)}) custom-call(s32[3]{0:T(128)S(1)} %pad_add_fusion.spot, f32[8,128]{1,0:T(8,128)S(1)} %add.84.refs_0_, f32[128,768]{1,0:T(8,128)S(1)} %copy-done.12, bf16[128,768]{1,0:T(8,128)(2,1)S(1)} %collective-permute-done.21.refs_2_, ...), custom_call_target="tpu_custom_call" | custom-call | bytes 12582912 | tf_op jit(solution)/shard_map/pallas_call | solution.py:102
  109.5 1.9 collective-permute-start.24
  111.4 1.4 collective-permute-start.25
  112.9 1.5 collective-permute-start.26
  114.4 1.6 copy-done.2
  116.0 3.0 %shard_map.118 = (f32[2048,128]{1,0:T(8,128)S(1)}, f32[2048,128]{1,0:T(8,128)S(1)}) custom-call(s32[3]{0:T(128)S(1)} %pad_add_fusion.spot, f32[2,2048,128]{2,1,0:T(8,128)S(1)} %copy-done.2, f32[2,2048,128]{2,1,0:T(8,128)} %collective-permute-done.30.refs_1_), custom_call_target="tpu_custom_call" | custom-call | bytes 6291456 | tf_op jit(solution)/shard_map/pallas_call | solution.py:102
  118.9 9.4 %collective-permute-done.24.refs_0_ = bf16[128,3072]{1,0:T(8,128)(2,1)S(1)} collective-permute-done((bf16[128,3072]{1,0:T(8,128)(2,1)}, bf16[128,3072]{1,0:T(8,128)(2,1)S(1)}, u32[]{:S(2)}, u32[]{:S(2)}) %collective-permute-start.24) | collective-permute-done | bytes 786464 | tf_op jit(solution)/shard_map/ppermute | solution.py:284
  128.4 1.5 collective-permute-done.25.refs_1_
  129.8 1.5 collective-permute-start.35
  131.3 4.1 %collective-permute-start.31 = (bf16[128,3072]{1,0:T(8,128)(2,1)}, bf16[128,3072]{1,0:T(8,128)(2,1)S(1)}, u32[]{:S(2)}, u32[]{:S(2)}) collective-permute-start(bf16[128,3072]{1,0:T(8,128)(2,1)} %get-tuple-element.93), channel_id=1, source_target_pairs={{0,24},{4,28},{24,0},{28,4},{1,25},{5,29},{25,1},{29,5},{2,26},{6,... | collective-permute-start | bytes 2359304 | tf_op jit(solution)/shard_map/ppermute | solution.py:288
  135.5 1.1 collective-permute-start.32
  137.3 1.2 constant_dynamic-update-slice_fusion.8
  138.7 13.5 %collective-permute-done.31.refs_0_ = bf16[128,3072]{1,0:T(8,128)(2,1)S(1)} collective-permute-done((bf16[128,3072]{1,0:T(8,128)(2,1)}, bf16[128,3072]{1,0:T(8,128)(2,1)S(1)}, u32[]{:S(2)}, u32[]{:S(2)}) %collective-permute-start.31) | collective-permute-done | bytes 786464 | tf_op jit(solution)/shard_map/ppermute | solution.py:288
  152.3 1.1 constant_dynamic-update-slice_fusion.4
  153.4 1.8 collective-permute-start.33
  155.8 1.8 shard_map.121
  157.6 1.2 collective-permute-start.36
  158.8 1.4 collective-permute-start.37
  160.1 1.9 collective-permute-start.38
  162.0 14.7 %collective-permute-done.36.refs_3_ = bf16[512,128]{1,0:T(8,128)(2,1)S(1)} collective-permute-done((bf16[512,128]{1,0:T(8,128)(2,1)}, bf16[512,128]{1,0:T(8,128)(2,1)S(1)}, u32[]{:S(2)}, u32[]{:S(2)}) %collective-permute-start.36) | collective-permute-done | bytes 131104 | tf_op jit(solution)/shard_map/ppermute | solution.py:284
  176.7 2.6 %collective-permute-done.38.refs_5_ = bf16[512,128]{1,0:T(8,128)(2,1)} collective-permute-done((bf16[512,128]{1,0:T(8,128)(2,1)}, bf16[512,128]{1,0:T(8,128)(2,1)}, u32[]{:S(2)}, u32[]{:S(2)}) %collective-permute-start.38) | collective-permute-done | bytes 131104 | tf_op jit(solution)/shard_map/ppermute | solution.py:284
  179.4 2.2 %collective-permute-start.40 = (bf16[64,3072]{1,0:T(8,128)(2,1)S(1)}, bf16[64,3072]{1,0:T(8,128)(2,1)S(1)}, u32[]{:S(2)}, u32[]{:S(2)}) collective-permute-start(bf16[64,3072]{1,0:T(8,128)(2,1)S(1)} %slice.30), channel_id=1, source_target_pairs={{0,4},{4,0},{8,12},{12,8},{16,20},{20,16},{24,28},{28,24},{1,5},{5... | collective-permute-start | bytes 1179656 | tf_op jit(solution)/shard_map/ppermute | solution.py:284
  184.5 6.4 %collective-permute-done.39.refs_6_ = bf16[4,256,128]{2,1,0:T(8,128)(2,1)S(1)} collective-permute-done((bf16[4,256,128]{2,1,0:T(8,128)(2,1)S(1)}, bf16[4,256,128]{2,1,0:T(8,128)(2,1)S(1)}, u32[]{:S(2)}, u32[]{:S(2)}) %collective-permute-start.39) | collective-permute-done | bytes 262176 | tf_op jit(solution)/shard_map/ppermute | solution.py:284
  190.9 4.0 %shard_map.123 = (bf16[256,1024]{1,0:T(8,128)(2,1)}, bf16[256,1024]{1,0:T(8,128)(2,1)}) custom-call(s32[3]{0:T(128)S(1)} %pad_add_fusion.spot, bf16[256,1024]{1,0:T(8,128)(2,1)S(1)} %copy-done.4, bf16[256,1024]{1,0:T(8,128)(2,1)S(1)} %copy-done.6, bf16[512,128]{1,0:T(8,128)(2,1)S(1)} %get-tuple-element.103.refs_2_, ...), custom_call_target="tpu_custom_call" | custom-call | bytes 4194304 | tf_op jit(solution)/shard_map/pallas_call | solution.py:102
  (108 shorter events, 13.1 us)
Async XLA Ops:
  0.6 1.4 copy-start
  0.6 66.7 %copy-start.1 = (f32[128,3072]{1,0:T(8,128)S(1)}, f32[128,3072]{1,0:T(8,128)}, u32[]{:S(2)}) copy-start(f32[128,3072]{1,0:T(8,128)} %refs_5_.1) | copy-start | bytes 4718596
  2.1 12.3 %collective-permute-start = (bf16[256,768]{1,0:T(8,128)(2,1)S(1)}, bf16[256,768]{1,0:T(8,128)(2,1)}, u32[]{:S(2)}, u32[]{:S(2)}) collective-permute-start(bf16[256,768]{1,0:T(8,128)(2,1)S(1)} %constant_dynamic-slice_fusion.refs_4_), channel_id=1, source_target_pairs={{0,8},{4,12},{8,0},{12,4},{16,24},{20,28},{24,16},{28,20},{1,9},{5... | collective-permute-start | bytes 1179656 | tf_op jit(solution)/shard_map/ppermute | solution.py:284
  5.2 10.7 %collective-permute-start.1 = (bf16[256,768]{1,0:T(8,128)(2,1)S(1)}, bf16[256,768]{1,0:T(8,128)(2,1)}, u32[]{:S(2)}, u32[]{:S(2)}) collective-permute-start(bf16[256,768]{1,0:T(8,128)(2,1)S(1)} %constant_dynamic-slice_fusion.refs_4_), channel_id=1, source_target_pairs={{0,4},{4,0},{8,12},{12,8},{16,20},{20,16},{24,28},{28,24},{1,5},{5... | collective-permute-start | bytes 1179656 | tf_op jit(solution)/shard_map/ppermute | solution.py:284
  6.7 9.2 %collective-permute-start.2 = (bf16[256,768]{1,0:T(8,128)(2,1)S(1)}, bf16[256,768]{1,0:T(8,128)(2,1)}, u32[]{:S(2)}, u32[]{:S(2)}) collective-permute-start(bf16[256,768]{1,0:T(8,128)(2,1)S(1)} %constant_dynamic-slice_fusion.refs_4_), channel_id=1, source_target_pairs={{8,16},{12,20},{16,8},{20,12},{9,17},{13,21},{17,9},{21,13},{10,18... | collective-permute-start | bytes 1179656 | tf_op jit(solution)/shard_map/ppermute | solution.py:288
  8.2 1.0 copy-start.3
  9.2 1.0 copy-start.5
  12.2 3.6 %copy-start.13 = (bf16[4,128,256]{2,1,0:T(8,128)(2,1)}, bf16[4,128,256]{2,1,0:T(8,128)(2,1)S(1)}, u32[]{:S(2)}) copy-start(bf16[4,128,256]{2,1,0:T(8,128)(2,1)S(1)} %get-tuple-element.67.refs_0_) | copy-start | bytes 786436
  15.9 19.9 %collective-permute-start.3 = (bf16[256,768]{1,0:T(8,128)(2,1)S(1)}, bf16[256,768]{1,0:T(8,128)(2,1)}, u32[]{:S(2)}, u32[]{:S(2)}) collective-permute-start(bf16[256,768]{1,0:T(8,128)(2,1)S(1)} %get-tuple-element.62.refs_4_.refs_0_), channel_id=1, source_target_pairs={{0,24},{4,28},{24,0},{28,4},{1,25},{5,29},{25,1},{29,5},{2,26},{6,... | collective-permute-start | bytes 1179656 | tf_op jit(solution)/shard_map/ppermute | solution.py:288
  20.2 15.6 %collective-permute-start.4 = (bf16[256,768]{1,0:T(8,128)(2,1)}, bf16[256,768]{1,0:T(8,128)(2,1)}, u32[]{:S(2)}, u32[]{:S(2)}) collective-permute-start(bf16[256,768]{1,0:T(8,128)(2,1)} %get-tuple-element.63.refs_6_.refs_2_), channel_id=1, source_target_pairs={{0,4},{4,0},{8,12},{12,8},{16,20},{20,16},{24,28},{28,24},{1,5},{5... | collective-permute-start | bytes 1179656 | tf_op jit(solution)/shard_map/ppermute | solution.py:284
  21.8 14.0 %collective-permute-start.5 = (bf16[4,128,256]{2,1,0:T(8,128)(2,1)}, bf16[4,128,256]{2,1,0:T(8,128)(2,1)}, u32[]{:S(2)}, u32[]{:S(2)}) collective-permute-start(bf16[4,128,256]{2,1,0:T(8,128)(2,1)} %get-tuple-element.64), channel_id=1, source_target_pairs={{0,4},{4,0},{8,12},{12,8},{16,20},{20,16},{24,28},{28,24},{1,5},{5... | collective-permute-start | bytes 786440 | tf_op jit(solution)/shard_map/ppermute | solution.py:284
  36.8 29.1 %copy-start.22 = (bf16[256,768]{1,0:T(8,128)(2,1)}, bf16[256,768]{1,0:T(8,128)(2,1)S(1)}, u32[]{:S(2)}) copy-start(bf16[256,768]{1,0:T(8,128)(2,1)S(1)} %broadcast_select_fusion.1.refs_11_.refs_7_) | copy-start | bytes 1179652
  36.9 17.1 %collective-permute-start.6 = (bf16[256,768]{1,0:T(8,128)(2,1)S(1)}, bf16[256,768]{1,0:T(8,128)(2,1)S(1)}, u32[]{:S(2)}, u32[]{:S(2)}) collective-permute-start(bf16[256,768]{1,0:T(8,128)(2,1)S(1)} %broadcast_select_fusion.1.refs_11_.refs_7_), channel_id=1, source_target_pairs={{0,8},{4,12},{8,0},{12,4},{16,24},{20,28},{24,16},{28,20},{1,9},{5... | collective-permute-start | bytes 1179656 | tf_op jit(solution)/shard_map/ppermute | solution.py:284
  38.5 15.5 %collective-permute-start.7 = (bf16[256,768]{1,0:T(8,128)(2,1)S(1)}, bf16[256,768]{1,0:T(8,128)(2,1)S(1)}, u32[]{:S(2)}, u32[]{:S(2)}) collective-permute-start(bf16[256,768]{1,0:T(8,128)(2,1)S(1)} %broadcast_select_fusion.1.refs_11_.refs_7_), channel_id=1, source_target_pairs={{0,4},{4,0},{8,12},{12,8},{16,20},{20,16},{24,28},{28,24},{1,5},{5... | collective-permute-start | bytes 1179656 | tf_op jit(solution)/shard_map/ppermute | solution.py:284
  39.0 0.9 copy-start.14
  42.5 10.5 %collective-permute-start.10 = (bf16[2,128,256]{2,1,0:T(8,128)(2,1)S(1)}, bf16[2,128,256]{2,1,0:T(8,128)(2,1)S(1)}, u32[]{:S(2)}, u32[]{:S(2)}) collective-permute-start(bf16[2,128,256]{2,1,0:T(8,128)(2,1)S(1)} %get-tuple-element.72), channel_id=1, source_target_pairs={{0,24},{4,28},{8,16},{12,20},{16,8},{20,12},{24,0},{28,4},{1,25},{... | collective-permute-start | bytes 393224 | tf_op jit(solution)/shard_map/ppermute | solution.py:284
  44.9 9.1 %collective-permute-start.8 = (bf16[2,128,256]{2,1,0:T(8,128)(2,1)S(1)}, bf16[2,128,256]{2,1,0:T(8,128)(2,1)S(1)}, u32[]{:S(2)}, u32[]{:S(2)}) collective-permute-start(bf16[2,128,256]{2,1,0:T(8,128)(2,1)S(1)} %get-tuple-element.70), channel_id=1, source_target_pairs={{0,8},{4,12},{8,0},{12,4},{16,24},{20,28},{24,16},{28,20},{1,9},{5... | collective-permute-start | bytes 393224 | tf_op jit(solution)/shard_map/ppermute | solution.py:284
  44.9 9.1 %collective-permute-start.9 = (bf16[2,128,256]{2,1,0:T(8,128)(2,1)S(1)}, bf16[2,128,256]{2,1,0:T(8,128)(2,1)S(1)}, u32[]{:S(2)}, u32[]{:S(2)}) collective-permute-start(bf16[2,128,256]{2,1,0:T(8,128)(2,1)S(1)} %get-tuple-element.71), channel_id=1, source_target_pairs={{0,16},{4,20},{8,24},{12,28},{16,0},{20,4},{24,8},{28,12},{1,17},{... | collective-permute-start | bytes 393224 | tf_op jit(solution)/shard_map/ppermute | solution.py:284
  54.0 2.5 %copy-start.9 = (bf16[256,768]{1,0:T(8,128)(2,1)}, bf16[256,768]{1,0:T(8,128)(2,1)S(1)}, u32[]{:S(2)}) copy-start(bf16[256,768]{1,0:T(8,128)(2,1)S(1)} %get-tuple-element.77.refs_8_.refs_4_) | copy-start | bytes 1179652
  54.0 4.1 %copy-start.10 = (bf16[256,768]{1,0:T(8,128)(2,1)}, bf16[256,768]{1,0:T(8,128)(2,1)S(1)}, u32[]{:S(2)}) copy-start(bf16[256,768]{1,0:T(8,128)(2,1)S(1)} %get-tuple-element.78.refs_12_.refs_8_) | copy-start | bytes 1179652
  55.0 11.0 %collective-permute-start.14 = (bf16[4,2,128,256]{3,2,1,0:T(8,128)(2,1)}, bf16[4,2,128,256]{3,2,1,0:T(8,128)(2,1)}, u32[]{:S(2)}, u32[]{:S(2)}) collective-permute-start(bf16[4,2,128,256]{3,2,1,0:T(8,128)(2,1)} %pad_maximum_fusion.refs_0_), channel_id=1, source_target_pairs={{0,2},{1,3},{2,0},{3,1},{4,6},{5,7},{6,4},{7,5},{8,10},{9,11},{10,... | collective-permute-start | bytes 1572872 | tf_op jit(solution)/shard_map/ppermute | solution.py:291
  56.5 5.7 %collective-permute-start.12 = (bf16[128,768]{1,0:T(8,128)(2,1)S(1)}, bf16[128,768]{1,0:T(8,128)(2,1)S(1)}, u32[]{:S(2)}, u32[]{:S(2)}) collective-permute-start(bf16[128,768]{1,0:T(8,128)(2,1)S(1)} %slice.24), channel_id=1, source_target_pairs={{0,4},{4,0},{8,12},{12,8},{16,20},{20,16},{24,28},{28,24},{1,5},{5... | collective-permute-start | bytes 589832 | tf_op jit(solution)/shard_map/ppermute | solution.py:284
  58.1 5.7 %collective-permute-start.13 = (bf16[128,768]{1,0:T(8,128)(2,1)S(1)}, bf16[128,768]{1,0:T(8,128)(2,1)S(1)}, u32[]{:S(2)}, u32[]{:S(2)}) collective-permute-start(bf16[128,768]{1,0:T(8,128)(2,1)S(1)} %slice.25), channel_id=1, source_target_pairs={{0,8},{4,12},{8,0},{12,4},{16,24},{20,28},{24,16},{28,20},{1,9},{5... | collective-permute-start | bytes 589832 | tf_op jit(solution)/shard_map/ppermute | solution.py:284
  59.5 10.1 %collective-permute-start.11 = (bf16[4,2,128,256]{3,2,1,0:T(8,128)(2,1)}, bf16[4,2,128,256]{3,2,1,0:T(8,128)(2,1)}, u32[]{:S(2)}, u32[]{:S(2)}) collective-permute-start(bf16[4,2,128,256]{3,2,1,0:T(8,128)(2,1)} %pad_maximum_fusion.refs_0_), channel_id=1, source_target_pairs={{0,1},{1,0},{2,3},{3,2},{4,5},{5,4},{6,7},{7,6},{8,9},{9,8},{10,11... | collective-permute-start | bytes 1572872 | tf_op jit(solution)/shard_map/ppermute | solution.py:291
  66.0 0.7 copy-start.15
  67.4 2.3 %collective-permute-start.15 = (bf16[4,2,128,256]{3,2,1,0:T(8,128)(2,1)}, bf16[4,2,128,256]{3,2,1,0:T(8,128)(2,1)}, u32[]{:S(2)}, u32[]{:S(2)}) collective-permute-start(bf16[4,2,128,256]{3,2,1,0:T(8,128)(2,1)} %get-tuple-element.79.refs_2_), channel_id=1, source_target_pairs={{0,1},{1,0},{2,3},{3,2},{4,5},{5,4},{6,7},{7,6},{8,9},{9,8},{10,11... | collective-permute-start | bytes 1572872 | tf_op jit(solution)/shard_map/ppermute | solution.py:291
  67.4 12.0 %copy-start.17 = (bf16[128,768]{1,0:T(8,128)(2,1)S(1)}, bf16[128,768]{1,0:T(8,128)(2,1)}, u32[]{:S(2)}) copy-start(bf16[128,768]{1,0:T(8,128)(2,1)} %copy-done.15) | copy-start | bytes 589828
  67.4 12.0 %copy-start.20 = (bf16[128,768]{1,0:T(8,128)(2,1)S(1)}, bf16[128,768]{1,0:T(8,128)(2,1)}, u32[]{:S(2)}) copy-start(bf16[128,768]{1,0:T(8,128)(2,1)} %copy-done.18) | copy-start | bytes 589828
  67.5 36.8 %copy-start.7 = (f32[128,3072]{1,0:T(8,128)S(1)}, f32[128,3072]{1,0:T(8,128)}, u32[]{:S(2)}) copy-start(f32[128,3072]{1,0:T(8,128)} %refs_6_.1) | copy-start | bytes 4718596
  67.5 36.8 %copy-start.8 = (f32[128,3072]{1,0:T(8,128)S(1)}, f32[128,3072]{1,0:T(8,128)}, u32[]{:S(2)}) copy-start(f32[128,3072]{1,0:T(8,128)} %refs_7_.1) | copy-start | bytes 4718596
  67.5 11.8 %collective-permute-start.27 = (bf16[128,768]{1,0:T(8,128)(2,1)S(1)}, bf16[128,768]{1,0:T(8,128)(2,1)S(1)}, u32[]{:S(2)}, u32[]{:S(2)}) collective-permute-start(bf16[128,768]{1,0:T(8,128)(2,1)S(1)} %get-tuple-element.119), channel_id=1, source_target_pairs={{0,1},{1,0},{2,3},{3,2},{4,5},{5,4},{6,7},{7,6},{8,9},{9,8},{10,11... | collective-permute-start | bytes 589832 | tf_op jit(solution)/shard_map/ppermute | solution.py:291
  68.1 11.3 %collective-permute-start.28 = (bf16[128,768]{1,0:T(8,128)(2,1)S(1)}, bf16[128,768]{1,0:T(8,128)(2,1)S(1)}, u32[]{:S(2)}, u32[]{:S(2)}) collective-permute-start(bf16[128,768]{1,0:T(8,128)(2,1)S(1)} %get-tuple-element.121), channel_id=1, source_target_pairs={{0,2},{1,3},{2,0},{3,1},{4,6},{5,7},{6,4},{7,5},{8,10},{9,11},{10,... | collective-permute-start | bytes 589832 | tf_op jit(solution)/shard_map/ppermute | solution.py:291
  69.6 9.7 %collective-permute-start.29 = (bf16[128,768]{1,0:T(8,128)(2,1)S(1)}, bf16[128,768]{1,0:T(8,128)(2,1)S(1)}, u32[]{:S(2)}, u32[]{:S(2)}) collective-permute-start(bf16[128,768]{1,0:T(8,128)(2,1)S(1)} %get-tuple-element.118), channel_id=1, source_target_pairs={{0,3},{1,2},{2,1},{3,0},{4,7},{5,6},{6,5},{7,4},{8,11},{9,10},{10,... | collective-permute-start | bytes 589832 | tf_op jit(solution)/shard_map/ppermute | solution.py:291
  69.6 0.9 copy-start.16
  70.5 0.9 copy-start.19
  78.6 0.7 copy-start.11
  79.3 25.0 %copy-start.12 = (f32[128,768]{1,0:T(8,128)S(1)}, f32[128,768]{1,0:T(8,128)}, u32[]{:S(2)}) copy-start(f32[128,768]{1,0:T(8,128)} %copy-done.11) | copy-start | bytes 1179652
  84.9 29.5 %collective-permute-start.30 = (f32[2,2048,128]{2,1,0:T(8,128)}, f32[2,2048,128]{2,1,0:T(8,128)}, u32[]{:S(2)}, u32[]{:S(2)}) collective-permute-start(f32[2,2048,128]{2,1,0:T(8,128)} %get-tuple-element.91), channel_id=1, source_target_pairs={{0,1},{1,0},{2,3},{3,2},{4,5},{5,4},{6,7},{7,6},{8,9},{9,8},{10,11... | collective-permute-start | bytes 6291464 | tf_op jit(solution)/shard_map/ppermute | solution.py:291
  85.5 18.8 %collective-permute-start.21 = (bf16[128,768]{1,0:T(8,128)(2,1)S(1)}, bf16[128,768]{1,0:T(8,128)(2,1)S(1)}, u32[]{:S(2)}, u32[]{:S(2)}) collective-permute-start(bf16[128,768]{1,0:T(8,128)(2,1)S(1)} %get-tuple-element.86), channel_id=1, source_target_pairs={{0,1},{1,0},{2,3},{3,2},{4,5},{5,4},{6,7},{7,6},{8,9},{9,8},{10,11... | collective-permute-start | bytes 589832 | tf_op jit(solution)/shard_map/ppermute | solution.py:291
  85.6 18.7 %collective-permute-start.22 = (bf16[128,768]{1,0:T(8,128)(2,1)S(1)}, bf16[128,768]{1,0:T(8,128)(2,1)S(1)}, u32[]{:S(2)}, u32[]{:S(2)}) collective-permute-start(bf16[128,768]{1,0:T(8,128)(2,1)S(1)} %get-tuple-element.87), channel_id=1, source_target_pairs={{0,2},{1,3},{2,0},{3,1},{4,6},{5,7},{6,4},{7,5},{8,10},{9,11},{10,... | collective-permute-start | bytes 589832 | tf_op jit(solution)/shard_map/ppermute | solution.py:291
  87.1 17.2 %collective-permute-start.23 = (bf16[128,768]{1,0:T(8,128)(2,1)S(1)}, bf16[128,768]{1,0:T(8,128)(2,1)S(1)}, u32[]{:S(2)}, u32[]{:S(2)}) collective-permute-start(bf16[128,768]{1,0:T(8,128)(2,1)S(1)} %get-tuple-element.88), channel_id=1, source_target_pairs={{0,3},{1,2},{2,1},{3,0},{4,7},{5,6},{6,5},{7,4},{8,11},{9,10},{10,... | collective-permute-start | bytes 589832 | tf_op jit(solution)/shard_map/ppermute | solution.py:291
  87.4 4.0 %collective-permute-start.16 = (f32[8,128]{1,0:T(8,128)S(1)}, f32[8,128]{1,0:T(8,128)S(1)}, u32[]{:S(2)}, u32[]{:S(2)}) collective-permute-start(f32[8,128]{1,0:T(8,128)S(1)} %get-tuple-element.84), channel_id=1, source_target_pairs={{0,4},{4,0},{8,12},{12,8},{16,20},{20,16},{24,28},{28,24},{1,5},{5... | collective-permute-start | bytes 12296 | tf_op jit(solution)/shard_map/ppermute | solution.py:284
  91.4 3.6 %collective-permute-start.17 = (f32[8,128]{1,0:T(8,128)S(1)}, f32[8,128]{1,0:T(8,128)S(1)}, u32[]{:S(2)}, u32[]{:S(2)}) collective-permute-start(f32[8,128]{1,0:T(8,128)S(1)} %add.80), channel_id=1, source_target_pairs={{0,8},{4,12},{8,0},{12,4},{16,24},{20,28},{24,16},{28,20},{1,9},{5... | collective-permute-start | bytes 12296 | tf_op jit(solution)/shard_map/ppermute | solution.py:284
  95.0 4.5 %collective-permute-start.18 = (f32[8,128]{1,0:T(8,128)S(1)}, f32[8,128]{1,0:T(8,128)S(1)}, u32[]{:S(2)}, u32[]{:S(2)}) collective-permute-start(f32[8,128]{1,0:T(8,128)S(1)} %add.81), channel_id=1, source_target_pairs={{0,16},{4,20},{8,24},{12,28},{16,0},{20,4},{24,8},{28,12},{1,17},{... | collective-permute-start | bytes 12296 | tf_op jit(solution)/shard_map/ppermute | solution.py:284
  99.5 1.2 collective-permute-start.19
  100.7 3.6 %collective-permute-start.20 = (f32[8,128]{1,0:T(8,128)S(1)}, f32[8,128]{1,0:T(8,128)S(1)}, u32[]{:S(2)}, u32[]{:S(2)}) collective-permute-start(f32[8,128]{1,0:T(8,128)S(1)} %add.83), channel_id=1, source_target_pairs={{0,2},{1,3},{2,0},{3,1},{4,6},{5,7},{6,4},{7,5},{8,10},{9,11},{10,... | collective-permute-start | bytes 12296 | tf_op jit(solution)/shard_map/ppermute | solution.py:291
  109.5 18.9 %collective-permute-start.24 = (bf16[128,3072]{1,0:T(8,128)(2,1)}, bf16[128,3072]{1,0:T(8,128)(2,1)S(1)}, u32[]{:S(2)}, u32[]{:S(2)}) collective-permute-start(bf16[128,3072]{1,0:T(8,128)(2,1)} %get-tuple-element.89.refs_4_), channel_id=1, source_target_pairs={{0,8},{4,12},{8,0},{12,4},{16,24},{20,28},{24,16},{28,20},{1,9},{5... | collective-permute-start | bytes 2359304 | tf_op jit(solution)/shard_map/ppermute | solution.py:284
  111.4 18.4 %collective-permute-start.25 = (bf16[128,3072]{1,0:T(8,128)(2,1)}, bf16[128,3072]{1,0:T(8,128)(2,1)S(1)}, u32[]{:S(2)}, u32[]{:S(2)}) collective-permute-start(bf16[128,3072]{1,0:T(8,128)(2,1)} %get-tuple-element.89.refs_4_), channel_id=1, source_target_pairs={{0,4},{4,0},{8,12},{12,8},{16,20},{20,16},{24,28},{28,24},{1,5},{5... | collective-permute-start | bytes 2359304 | tf_op jit(solution)/shard_map/ppermute | solution.py:284
  112.9 17.0 %collective-permute-start.26 = (bf16[128,3072]{1,0:T(8,128)(2,1)}, bf16[128,3072]{1,0:T(8,128)(2,1)}, u32[]{:S(2)}, u32[]{:S(2)}) collective-permute-start(bf16[128,3072]{1,0:T(8,128)(2,1)} %get-tuple-element.89.refs_4_), channel_id=1, source_target_pairs={{8,16},{12,20},{16,8},{20,12},{9,17},{13,21},{17,9},{21,13},{10,18... | collective-permute-start | bytes 2359304 | tf_op jit(solution)/shard_map/ppermute | solution.py:288
  114.4 1.6 copy-start.2
  129.8 26.0 %collective-permute-start.35 = (f32[2048,128]{1,0:T(8,128)S(1)}, f32[2048,128]{1,0:T(8,128)S(1)}, u32[]{:S(2)}, u32[]{:S(2)}) collective-permute-start(f32[2048,128]{1,0:T(8,128)S(1)} %get-tuple-element.98), channel_id=1, source_target_pairs={{0,2},{1,3},{2,0},{3,1},{4,6},{5,7},{6,4},{7,5},{8,10},{9,11},{10,... | collective-permute-start | bytes 3145736 | tf_op jit(solution)/shard_map/ppermute | solution.py:291
  131.3 20.9 %collective-permute-start.31 = (bf16[128,3072]{1,0:T(8,128)(2,1)}, bf16[128,3072]{1,0:T(8,128)(2,1)S(1)}, u32[]{:S(2)}, u32[]{:S(2)}) collective-permute-start(bf16[128,3072]{1,0:T(8,128)(2,1)} %get-tuple-element.93), channel_id=1, source_target_pairs={{0,24},{4,28},{24,0},{28,4},{1,25},{5,29},{25,1},{29,5},{2,26},{6,... | collective-permute-start | bytes 2359304 | tf_op jit(solution)/shard_map/ppermute | solution.py:288
  135.5 16.8 %collective-permute-start.32 = (bf16[128,3072]{1,0:T(8,128)(2,1)S(1)}, bf16[128,3072]{1,0:T(8,128)(2,1)S(1)}, u32[]{:S(2)}, u32[]{:S(2)}) collective-permute-start(bf16[128,3072]{1,0:T(8,128)(2,1)S(1)} %get-tuple-element.94), channel_id=1, source_target_pairs={{0,4},{4,0},{8,12},{12,8},{16,20},{20,16},{24,28},{28,24},{1,5},{5... | collective-permute-start | bytes 2359304 | tf_op jit(solution)/shard_map/ppermute | solution.py:284
  153.4 5.3 %copy-start.21 = (bf16[1024,3072]{1,0:T(8,128)(2,1)}, bf16[1024,3072]{1,0:T(8,128)(2,1)S(1)}, u32[]{:S(2)}) copy-start(bf16[1024,3072]{1,0:T(8,128)(2,1)S(1)} %get-tuple-element.116) | copy-start | bytes 18874372
  153.4 25.9 %collective-permute-start.33 = (bf16[128,3072]{1,0:T(8,128)(2,1)}, bf16[128,3072]{1,0:T(8,128)(2,1)S(1)}, u32[]{:S(2)}, u32[]{:S(2)}) collective-permute-start(bf16[128,3072]{1,0:T(8,128)(2,1)} %get-tuple-element.117), channel_id=1, source_target_pairs={{0,8},{4,12},{8,0},{12,4},{16,24},{20,28},{24,16},{28,20},{1,9},{5... | collective-permute-start | bytes 2359304 | tf_op jit(solution)/shard_map/ppermute | solution.py:284
  155.2 24.1 %collective-permute-start.34 = (bf16[128,3072]{1,0:T(8,128)(2,1)}, bf16[128,3072]{1,0:T(8,128)(2,1)S(1)}, u32[]{:S(2)}, u32[]{:S(2)}) collective-permute-start(bf16[128,3072]{1,0:T(8,128)(2,1)} %get-tuple-element.117), channel_id=1, source_target_pairs={{0,4},{4,0},{8,12},{12,8},{16,20},{20,16},{24,28},{28,24},{1,5},{5... | collective-permute-start | bytes 2359304 | tf_op jit(solution)/shard_map/ppermute | solution.py:284
  157.6 19.2 %collective-permute-start.36 = (bf16[512,128]{1,0:T(8,128)(2,1)}, bf16[512,128]{1,0:T(8,128)(2,1)S(1)}, u32[]{:S(2)}, u32[]{:S(2)}) collective-permute-start(bf16[512,128]{1,0:T(8,128)(2,1)} %get-tuple-element.100), channel_id=1, source_target_pairs={{0,8},{4,12},{8,0},{12,4},{16,24},{20,28},{24,16},{28,20},{1,9},{5... | collective-permute-start | bytes 393224 | tf_op jit(solution)/shard_map/ppermute | solution.py:284
  158.8 18.0 %collective-permute-start.37 = (bf16[512,128]{1,0:T(8,128)(2,1)}, bf16[512,128]{1,0:T(8,128)(2,1)S(1)}, u32[]{:S(2)}, u32[]{:S(2)}) collective-permute-start(bf16[512,128]{1,0:T(8,128)(2,1)} %get-tuple-element.101), channel_id=1, source_target_pairs={{0,16},{4,20},{8,24},{12,28},{16,0},{20,4},{24,8},{28,12},{1,17},{... | collective-permute-start | bytes 393224 | tf_op jit(solution)/shard_map/ppermute | solution.py:284
  160.1 19.2 %collective-permute-start.38 = (bf16[512,128]{1,0:T(8,128)(2,1)}, bf16[512,128]{1,0:T(8,128)(2,1)}, u32[]{:S(2)}, u32[]{:S(2)}) collective-permute-start(bf16[512,128]{1,0:T(8,128)(2,1)} %get-tuple-element.102), channel_id=1, source_target_pairs={{0,24},{4,28},{8,16},{12,20},{16,8},{20,12},{24,0},{28,4},{1,25},{... | collective-permute-start | bytes 393224 | tf_op jit(solution)/shard_map/ppermute | solution.py:284
  162.0 28.9 %copy-start.4 = (bf16[256,1024]{1,0:T(8,128)(2,1)S(1)}, bf16[256,1024]{1,0:T(8,128)(2,1)}, u32[]{:S(2)}) copy-start(bf16[256,1024]{1,0:T(8,128)(2,1)} %refs_0_.3) | copy-start | bytes 1572868
  162.0 28.9 %copy-start.6 = (bf16[256,1024]{1,0:T(8,128)(2,1)S(1)}, bf16[256,1024]{1,0:T(8,128)(2,1)}, u32[]{:S(2)}) copy-start(bf16[256,1024]{1,0:T(8,128)(2,1)} %refs_1_.3) | copy-start | bytes 1572868
  179.4 15.6 %collective-permute-start.40 = (bf16[64,3072]{1,0:T(8,128)(2,1)S(1)}, bf16[64,3072]{1,0:T(8,128)(2,1)S(1)}, u32[]{:S(2)}, u32[]{:S(2)}) collective-permute-start(bf16[64,3072]{1,0:T(8,128)(2,1)S(1)} %slice.30), channel_id=1, source_target_pairs={{0,4},{4,0},{8,12},{12,8},{16,20},{20,16},{24,28},{28,24},{1,5},{5... | collective-permute-start | bytes 1179656 | tf_op jit(solution)/shard_map/ppermute | solution.py:284
  181.6 14.2 %collective-permute-start.41 = (bf16[64,3072]{1,0:T(8,128)(2,1)S(1)}, bf16[64,3072]{1,0:T(8,128)(2,1)S(1)}, u32[]{:S(2)}, u32[]{:S(2)}) collective-permute-start(bf16[64,3072]{1,0:T(8,128)(2,1)S(1)} %slice.31), channel_id=1, source_target_pairs={{0,8},{4,12},{8,0},{12,4},{16,24},{20,28},{24,16},{28,20},{1,9},{5... | collective-permute-start | bytes 1179656 | tf_op jit(solution)/shard_map/ppermute | solution.py:284
  182.6 8.4 %collective-permute-start.39 = (bf16[4,256,128]{2,1,0:T(8,128)(2,1)S(1)}, bf16[4,256,128]{2,1,0:T(8,128)(2,1)S(1)}, u32[]{:S(2)}, u32[]{:S(2)}) collective-permute-start(bf16[4,256,128]{2,1,0:T(8,128)(2,1)S(1)} %pad_maximum_fusion.1), channel_id=1, source_target_pairs={{0,4},{4,0},{8,12},{12,8},{16,20},{20,16},{24,28},{28,24},{1,5},{5... | collective-permute-start | bytes 786440 | tf_op jit(solution)/shard_map/ppermute | solution.py:284
  (1 other events, 0.7 us)

commit v4 on v3

--- a/solution.py
+++ b/solution.py
@@ -147,21 +147,23 @@
     return Joined((len(pieces) * size, cols), pieces[0].dtype, parts)
 
 
-def tokens_in_columns(hiddens):
-    _, _, part, size = hiddens[0].shape
-    parts = []
-    for i, h in enumerate(hiddens):
-        for m in range(CELL):
-            parts.append((h, (m // 2, m % 2), (pl.ds(i * part, part), pl.ds(m * size, size))))
-    return Joined((4 * part, CELL * size), hiddens[0].dtype, parts)
+def hidden_blocks(hiddens):
+    shape = hiddens[0].shape
+    parts = [(h, None, (i,)) for i, h in enumerate(hiddens)]
+    return Joined((4,) + shape, hiddens[0].dtype, parts)
 
 
 def grad_body(spot, ins, outs, need, done):
     del spot
-    left, right = ins
-    part = outs[0].shape[0]
-    need(0, 1)
-    total = jnp.dot(left[...], right[...], preferred_element_type=F32)
+    hidden, pieces = ins
+    part, size = hidden.shape[-2:]
+    need(0, 1)
+    total = None
+    for m in range(CELL):
+        left = jnp.concatenate([hidden[i, m // 2, m % 2] for i in range(4)], axis=0)
+        right = pieces[m * size : (m + 1) * size, :]
+        term = jnp.dot(left, right, preferred_element_type=F32)
+        total = term if total is None else total + term
     for i in (3, 2, 1, 0):
         outs[i][...] = total[i * part : (i + 1) * part].astype(outs[i].dtype)
         done(i)
@@ -257,15 +259,15 @@
     del refs
 
 
-def together(*values):
+def together(*values, after=()):
     return pl.pallas_call(
         gate_body,
         out_shape=tuple(shaped(v.shape, v.dtype) for v in values),
-        in_specs=[HBM] * len(values),
+        in_specs=[HBM] * len(values) + [ANY] * len(after),
         out_specs=(HBM,) * len(values),
         input_output_aliases={i: i for i in range(len(values))},
         compiler_params=pltpu.CompilerParams(vmem_limit_bytes=8 << 20),
-    )(*values)
+    )(*values, *after)
 
 
 def on_device(n, d_out, gate, up_proj, master, moment_one, moment_two):
@@ -317,7 +319,7 @@
     kept, given = call(hidden_body, (block, block), (spot, gate, up_proj), moved=2 << 20)
     near, own_x, mid, given, own = together(near, own_x, mid, given, own)
     end, near_x, came = line(own, ROUND), across(near, 1), across(given, 1)
-    end, near_x, came = together(end, near_x, came)
+    end, came = together(end, came, after=(near_x,))
     last = jnp.where(ends, end, mid)
     far, last_x = across(last, 2), across(last, 1)
     pair = shaped((2, part, tokens), BF16)
@@ -327,7 +329,7 @@
     low, high = across(far[:half], 1), across(last_x[half:], 2)
     hidden = jnp.stack(blocks)
     hidden_y, hidden_c = swap(hidden, 2), swap(hidden, 1)
-    low, high, hidden_y = together(low, high, hidden_y)
+    (hidden_y,) = together(hidden_y, after=(low, high))
     hiddens = (hidden, hidden_c, hidden_y, swap(hidden_y, 1))
     weight = master
     if outer > 1:
@@ -345,7 +347,7 @@
     *grads, total = call(
         grad_body,
         (piece, sent, sent, sent, shaped((8, 128), F32)),
-        (spot, tokens_in_columns(hiddens), pieces),
+        (spot, hidden_blocks(hiddens), pieces),
         flops=flops,
         moved=8 << 20,
         limit=52,

time: 197 us -> 196 us (level)
  no operation moved by 1% of the time
where the time goes in v4:
time: 196 us; the launch traced here: 195 us
  waiting for transfers between devices  87.2 us (44%)
  starting transfers between devices  57.3 us (29%)
  Pallas kernels  30.5 us (16%)
  local copies, waits for them, and re-layouts  16.1 us (8%)
  other arithmetic  3.28 us (2%)
    ppermute x25, waiting for transfers between devices, across(): return lax.ppermute(value, 'dp', [(i, i ^ m) for i in range(n)])  68.3 us
    ppermute x25, starting transfers between devices, across(): return lax.ppermute(value, 'dp', [(i, i ^ m) for i in range(n)])  36.6 us
    pallas_call x8, Pallas kernels, call(): pl.pallas_call(kernel, out_shape=tuple(outs), in_specs=[SMEM] + specs + [...  30.5 us
    ppermute x4, waiting for transfers between devices, line(): lax.ppermute(value, 'dp', [(i, i - i % CELL + b * 2 + i % 2) for i, b in...  13.5 us
    ppermute x4, starting transfers between devices, line(): lax.ppermute(value, 'dp', [(i, i - i % CELL + b * 2 + i % 2) for i, b in...  11.5 us
    unnamed x46, local copies, waits for them, and re-layouts  9.35 us
    ppermute x13, starting transfers between devices, swap(): return lax.ppermute(value, 'tensor', [(i, i ^ m) for i in range(4)])  9.2 us
    ppermute x13, waiting for transfers between devices, swap(): return lax.ppermute(value, 'tensor', [(i, i ^ m) for i in range(4)])  5.42 us
  transfers between devices with their start and end apart: 42, of which 19 were waited for; matrix products, arithmetic and copies ran while one was open for 4% of the time, Pallas kernels for 13%

profile of v4, /device:TPU:0, one launch (start us, length us, event | category | flops | bytes accessed | tf_op | source)
XLA Modules:
  0.0 195.2 jit_solution(8785205864271625282)
XLA Ops:
  0.7 1.4 copy-done
  2.1 3.1 %collective-permute-start = (bf16[256,768]{1,0:T(8,128)(2,1)S(1)}, bf16[256,768]{1,0:T(8,128)(2,1)}, u32[]{:S(2)}, u32[]{:S(2)}) collective-permute-start(bf16[256,768]{1,0:T(8,128)(2,1)S(1)} %constant_dynamic-slice_fusion.refs_4_), channel_id=1, source_target_pairs={{0,8},{4,12},{8,0},{12,4},{16,24},{20,28},{24,16},{28,20},{1,9},{5... | collective-permute-start | bytes 1179656 | tf_op jit(solution)/shard_map/ppermute | solution.py:286
  5.2 1.5 collective-permute-start.1
  6.7 1.4 collective-permute-start.2
  8.2 1.0 copy-done.3
  9.2 1.0 copy-done.5
  10.3 2.0 %shard_map.109 = (bf16[4,128,256]{2,1,0:T(8,128)(2,1)S(1)}, bf16[4,128,256]{2,1,0:T(8,128)(2,1)}) custom-call(s32[3]{0:T(128)S(1)} %pad_add_fusion.spot, bf16[256,1024]{1,0:T(8,128)(2,1)S(1)} %copy-done.3, bf16[256,1024]{1,0:T(8,128)(2,1)S(1)} %copy-done.5), custom_call_target="tpu_custom_call" | custom-call | bytes 2097152 | tf_op jit(solution)/shard_map/pallas_call | solution.py:102
  12.3 2.1 %collective-permute-done.refs_0_ = bf16[256,768]{1,0:T(8,128)(2,1)} collective-permute-done((bf16[256,768]{1,0:T(8,128)(2,1)S(1)}, bf16[256,768]{1,0:T(8,128)(2,1)}, u32[]{:S(2)}, u32[]{:S(2)}) %collective-permute-start) | collective-permute-done | bytes 393248 | tf_op jit(solution)/shard_map/ppermute | solution.py:286
  14.4 1.5 collective-permute-done.1.refs_1_
  15.9 4.4 %collective-permute-start.3 = (bf16[256,768]{1,0:T(8,128)(2,1)S(1)}, bf16[256,768]{1,0:T(8,128)(2,1)}, u32[]{:S(2)}, u32[]{:S(2)}) collective-permute-start(bf16[256,768]{1,0:T(8,128)(2,1)S(1)} %get-tuple-element.58.refs_4_.refs_0_), channel_id=1, source_target_pairs={{0,24},{4,28},{24,0},{28,4},{1,25},{5,29},{25,1},{29,5},{2,26},{6,... | collective-permute-start | bytes 1179656 | tf_op jit(solution)/shard_map/ppermute | solution.py:290
  20.2 1.6 collective-permute-start.5
  22.3 13.5 %collective-permute-done.4.refs_1_ = bf16[4,128,256]{2,1,0:T(8,128)(2,1)} collective-permute-done((bf16[4,128,256]{2,1,0:T(8,128)(2,1)}, bf16[4,128,256]{2,1,0:T(8,128)(2,1)}, u32[]{:S(2)}, u32[]{:S(2)}) %collective-permute-start.4) | collective-permute-done | bytes 262176 | tf_op jit(solution)/shard_map/ppermute | solution.py:286
  35.8 1.0 broadcast_select_fusion.1.refs_11_.refs_7_
  36.9 1.6 collective-permute-start.6
  39.0 0.9 copy-done.14
  40.0 2.5 %shard_map.112 = (bf16[2,128,256]{2,1,0:T(8,128)(2,1)S(1)}, bf16[2,128,256]{2,1,0:T(8,128)(2,1)S(1)}, bf16[2,128,256]{2,1,0:T(8,128)(2,1)S(1)}, bf16[2,128,256]{2,1,0:T(8,128)(2,1)S(1)}) custom-call(s32[3]{0:T(128)S(1)} %pad_add_fusion.spot, bf16[4,128,256]{2,1,0:T(8,128)(2,1)S(1)} %copy-done.14, bf16[4,128,256]{2,1,0:T(8,128)(2,1)} %get-tuple-element.64.refs_1_), custom_call_target="tpu_custom_call" | custom-call | bytes 1048576 | tf_op jit(solution)/shard_map/pallas_call | solution.py:102
  42.5 2.4 %collective-permute-start.10 = (bf16[2,128,256]{2,1,0:T(8,128)(2,1)S(1)}, bf16[2,128,256]{2,1,0:T(8,128)(2,1)S(1)}, u32[]{:S(2)}, u32[]{:S(2)}) collective-permute-start(bf16[2,128,256]{2,1,0:T(8,128)(2,1)S(1)} %get-tuple-element.68), channel_id=1, source_target_pairs={{0,24},{4,28},{8,16},{12,20},{16,8},{20,12},{24,0},{28,4},{1,25},{... | collective-permute-start | bytes 393224 | tf_op jit(solution)/shard_map/ppermute | solution.py:286
  44.9 2.0 %collective-permute-start.9 = (bf16[2,128,256]{2,1,0:T(8,128)(2,1)S(1)}, bf16[2,128,256]{2,1,0:T(8,128)(2,1)S(1)}, u32[]{:S(2)}, u32[]{:S(2)}) collective-permute-start(bf16[2,128,256]{2,1,0:T(8,128)(2,1)S(1)} %get-tuple-element.67), channel_id=1, source_target_pairs={{0,16},{4,20},{8,24},{12,28},{16,0},{20,4},{24,8},{28,12},{1,17},{... | collective-permute-start | bytes 393224 | tf_op jit(solution)/shard_map/ppermute | solution.py:286
  47.0 6.0 %collective-permute-done.10.refs_5_ = bf16[2,128,256]{2,1,0:T(8,128)(2,1)S(1)} collective-permute-done((bf16[2,128,256]{2,1,0:T(8,128)(2,1)S(1)}, bf16[2,128,256]{2,1,0:T(8,128)(2,1)S(1)}, u32[]{:S(2)}, u32[]{:S(2)}) %collective-permute-start.10) | collective-permute-done | bytes 131104 | tf_op jit(solution)/shard_map/ppermute | solution.py:286
  53.0 1.0 collective-permute-done.8.refs_3_
  54.0 1.0 pad_maximum_fusion.refs_0_
  55.0 1.5 collective-permute-start.12
  56.5 1.6 collective-permute-start.13
  58.1 1.4 collective-permute-start.14
  59.5 2.8 %collective-permute-done.13.refs_1_.refs_9_.refs_5_ = bf16[128,768]{1,0:T(8,128)(2,1)S(1)} collective-permute-done((bf16[128,768]{1,0:T(8,128)(2,1)S(1)}, bf16[128,768]{1,0:T(8,128)(2,1)S(1)}, u32[]{:S(2)}, u32[]{:S(2)}) %collective-permute-start.13) | collective-permute-done | bytes 196640 | tf_op jit(solution)/shard_map/ppermute | solution.py:286
  62.3 1.6 collective-permute-done.14.refs_2_.refs_10_.refs_6_
  63.8 2.1 %collective-permute-done.12.refs_0_ = bf16[4,2,128,256]{3,2,1,0:T(8,128)(2,1)} collective-permute-done((bf16[4,2,128,256]{3,2,1,0:T(8,128)(2,1)}, bf16[4,2,128,256]{3,2,1,0:T(8,128)(2,1)}, u32[]{:S(2)}, u32[]{:S(2)}) %collective-permute-start.12) | collective-permute-done | bytes 524320 | tf_op jit(solution)/shard_map/ppermute | solution.py:293
  67.4 1.5 collective-permute-start.28
  70.8 6.7 %shard_map.115 = (f32[128,768]{1,0:T(8,128)S(1)}, bf16[128,768]{1,0:T(8,128)(2,1)S(1)}, bf16[128,768]{1,0:T(8,128)(2,1)S(1)}, bf16[128,768]{1,0:T(8,128)(2,1)S(1)}, f32[8,128]{1,0:T(8,128)S(1)}) custom-call(s32[3]{0:T(128)S(1)} %pad_add_fusion.spot, bf16[4,2,128,256]{3,2,1,0:T(8,128)(2,1)} %pad_maximum_fusion.refs_0_, ...), custom_call_target="tpu_custom_call" | custom-call | flops 1610612736 | bytes 8388608 | tf_op jit(solution)/shard_map/pallas_call | solution.py:102
  78.2 5.5 %shard_map.117 = (f32[2,2048,128]{2,1,0:T(8,128)}, f32[2,2048,128]{2,1,0:T(8,128)}) custom-call(s32[3]{0:T(128)S(1)} %pad_add_fusion.spot, bf16[256,768]{1,0:T(8,128)(2,1)S(1)} %get-tuple-element.58.refs_4_.refs_0_, bf16[256,768]{1,0:T(8,128)(2,1)} %get-tuple-element.75.refs_5_.refs_1_, bf16[256,768]{1,0:T(8,128)(2,1)} %get-tuple-element.60.refs_6_.refs_2_, ...), custom_call_target="tpu_custom_call" | custom-call | flops 1610612736 | bytes 10485760 | tf_op jit(solution)/shard_map/pallas_call | solution.py:102
  84.5 1.5 collective-permute-start.22
  86.3 2.4 %collective-permute-start.16 = (f32[8,128]{1,0:T(8,128)S(1)}, f32[8,128]{1,0:T(8,128)S(1)}, u32[]{:S(2)}, u32[]{:S(2)}) collective-permute-start(f32[8,128]{1,0:T(8,128)S(1)} %get-tuple-element.76), channel_id=1, source_target_pairs={{0,4},{4,0},{8,12},{12,8},{16,20},{20,16},{24,28},{28,24},{1,5},{5... | collective-permute-start | bytes 12296 | tf_op jit(solution)/shard_map/ppermute | solution.py:286
  88.7 1.6 collective-permute-done.16
  90.3 1.9 collective-permute-start.17
  92.2 1.7 collective-permute-done.17
  93.9 2.5 %collective-permute-start.18 = (f32[8,128]{1,0:T(8,128)S(1)}, f32[8,128]{1,0:T(8,128)S(1)}, u32[]{:S(2)}, u32[]{:S(2)}) collective-permute-start(f32[8,128]{1,0:T(8,128)S(1)} %add.81), channel_id=1, source_target_pairs={{0,16},{4,20},{8,24},{12,28},{16,0},{20,4},{24,8},{28,12},{1,17},{... | collective-permute-start | bytes 12296 | tf_op jit(solution)/shard_map/ppermute | solution.py:286
  96.4 2.1 %collective-permute-done.18 = f32[8,128]{1,0:T(8,128)S(1)} collective-permute-done((f32[8,128]{1,0:T(8,128)S(1)}, f32[8,128]{1,0:T(8,128)S(1)}, u32[]{:S(2)}, u32[]{:S(2)}) %collective-permute-start.18) | collective-permute-done | bytes 4128 | tf_op jit(solution)/shard_map/ppermute | solution.py:286
  98.4 1.2 collective-permute-done.19
  99.6 1.5 collective-permute-start.20
  101.1 2.1 %collective-permute-done.20 = f32[8,128]{1,0:T(8,128)S(1)} collective-permute-done((f32[8,128]{1,0:T(8,128)S(1)}, f32[8,128]{1,0:T(8,128)S(1)}, u32[]{:S(2)}, u32[]{:S(2)}) %collective-permute-start.20) | collective-permute-done | bytes 4128 | tf_op jit(solution)/shard_map/ppermute | solution.py:293
  103.2 5.1 %shard_map.116 = (f32[128,3072]{1,0:T(8,128)}, f32[128,3072]{1,0:T(8,128)}, f32[128,3072]{1,0:T(8,128)}, bf16[128,3072]{1,0:T(8,128)(2,1)}) custom-call(s32[3]{0:T(128)S(1)} %pad_add_fusion.spot, f32[8,128]{1,0:T(8,128)S(1)} %add.84.refs_0_, f32[128,768]{1,0:T(8,128)S(1)} %copy-done.12, bf16[128,768]{1,0:T(8,128)(2,1)S(1)} %collective-permute-done.21.refs_2_, ...), custom_call_target="tpu_custom_call" | custom-call | bytes 12582912 | tf_op jit(solution)/shard_map/pallas_call | solution.py:102
  108.4 1.9 collective-permute-start.24
  110.3 1.4 collective-permute-start.25
  111.7 1.5 collective-permute-start.26
  113.3 1.6 copy-done.2
  114.9 3.0 %shard_map.118 = (f32[2048,128]{1,0:T(8,128)S(1)}, f32[2048,128]{1,0:T(8,128)S(1)}) custom-call(s32[3]{0:T(128)S(1)} %pad_add_fusion.spot, f32[2,2048,128]{2,1,0:T(8,128)S(1)} %copy-done.2, f32[2,2048,128]{2,1,0:T(8,128)} %collective-permute-done.30.refs_1_), custom_call_target="tpu_custom_call" | custom-call | bytes 6291456 | tf_op jit(solution)/shard_map/pallas_call | solution.py:102
  117.8 9.4 %collective-permute-done.24.refs_0_ = bf16[128,3072]{1,0:T(8,128)(2,1)S(1)} collective-permute-done((bf16[128,3072]{1,0:T(8,128)(2,1)}, bf16[128,3072]{1,0:T(8,128)(2,1)S(1)}, u32[]{:S(2)}, u32[]{:S(2)}) %collective-permute-start.24) | collective-permute-done | bytes 786464 | tf_op jit(solution)/shard_map/ppermute | solution.py:286
  127.2 1.5 collective-permute-done.25.refs_1_
  128.7 1.5 collective-permute-start.35
  130.2 4.1 %collective-permute-start.31 = (bf16[128,3072]{1,0:T(8,128)(2,1)}, bf16[128,3072]{1,0:T(8,128)(2,1)S(1)}, u32[]{:S(2)}, u32[]{:S(2)}) collective-permute-start(bf16[128,3072]{1,0:T(8,128)(2,1)} %get-tuple-element.85), channel_id=1, source_target_pairs={{0,24},{4,28},{24,0},{28,4},{1,25},{5,29},{25,1},{29,5},{2,26},{6,... | collective-permute-start | bytes 2359304 | tf_op jit(solution)/shard_map/ppermute | solution.py:290
  134.3 1.1 collective-permute-start.32
  136.2 1.2 constant_dynamic-update-slice_fusion.8
  137.6 13.5 %collective-permute-done.31.refs_0_ = bf16[128,3072]{1,0:T(8,128)(2,1)S(1)} collective-permute-done((bf16[128,3072]{1,0:T(8,128)(2,1)}, bf16[128,3072]{1,0:T(8,128)(2,1)S(1)}, u32[]{:S(2)}, u32[]{:S(2)}) %collective-permute-start.31) | collective-permute-done | bytes 786464 | tf_op jit(solution)/shard_map/ppermute | solution.py:290
  151.1 1.1 constant_dynamic-update-slice_fusion.4
  152.3 1.8 collective-permute-start.33
  154.6 1.8 shard_map.121
  156.4 1.2 collective-permute-start.36
  157.6 1.4 collective-permute-start.37
  159.0 1.9 collective-permute-start.38
  160.8 14.7 %collective-permute-done.36.refs_3_ = bf16[512,128]{1,0:T(8,128)(2,1)S(1)} collective-permute-done((bf16[512,128]{1,0:T(8,128)(2,1)}, bf16[512,128]{1,0:T(8,128)(2,1)S(1)}, u32[]{:S(2)}, u32[]{:S(2)}) %collective-permute-start.36) | collective-permute-done | bytes 131104 | tf_op jit(solution)/shard_map/ppermute | solution.py:286
  175.5 2.6 %collective-permute-done.38.refs_5_ = bf16[512,128]{1,0:T(8,128)(2,1)} collective-permute-done((bf16[512,128]{1,0:T(8,128)(2,1)}, bf16[512,128]{1,0:T(8,128)(2,1)}, u32[]{:S(2)}, u32[]{:S(2)}) %collective-permute-start.38) | collective-permute-done | bytes 131104 | tf_op jit(solution)/shard_map/ppermute | solution.py:286
  178.2 2.2 %collective-permute-start.40 = (bf16[64,3072]{1,0:T(8,128)(2,1)S(1)}, bf16[64,3072]{1,0:T(8,128)(2,1)S(1)}, u32[]{:S(2)}, u32[]{:S(2)}) collective-permute-start(bf16[64,3072]{1,0:T(8,128)(2,1)S(1)} %slice.30), channel_id=1, source_target_pairs={{0,4},{4,0},{8,12},{12,8},{16,20},{20,16},{24,28},{28,24},{1,5},{5... | collective-permute-start | bytes 1179656 | tf_op jit(solution)/shard_map/ppermute | solution.py:286
  183.3 6.3 %collective-permute-done.39.refs_6_ = bf16[4,256,128]{2,1,0:T(8,128)(2,1)S(1)} collective-permute-done((bf16[4,256,128]{2,1,0:T(8,128)(2,1)S(1)}, bf16[4,256,128]{2,1,0:T(8,128)(2,1)S(1)}, u32[]{:S(2)}, u32[]{:S(2)}) %collective-permute-start.39) | collective-permute-done | bytes 262176 | tf_op jit(solution)/shard_map/ppermute | solution.py:286
  189.7 4.0 %shard_map.123 = (bf16[256,1024]{1,0:T(8,128)(2,1)}, bf16[256,1024]{1,0:T(8,128)(2,1)}) custom-call(s32[3]{0:T(128)S(1)} %pad_add_fusion.spot, bf16[256,1024]{1,0:T(8,128)(2,1)S(1)} %copy-done.4, bf16[256,1024]{1,0:T(8,128)(2,1)S(1)} %copy-done.6, bf16[512,128]{1,0:T(8,128)(2,1)S(1)} %get-tuple-element.95.refs_2_, ...), custom_call_target="tpu_custom_call" | custom-call | bytes 4194304 | tf_op jit(solution)/shard_map/pallas_call | solution.py:102
  (108 shorter events, 12.5 us)
Async XLA Ops:
  0.6 1.4 copy-start
  0.6 66.0 %copy-start.1 = (f32[128,3072]{1,0:T(8,128)S(1)}, f32[128,3072]{1,0:T(8,128)}, u32[]{:S(2)}) copy-start(f32[128,3072]{1,0:T(8,128)} %refs_5_.1) | copy-start | bytes 4718596
  2.1 12.3 %collective-permute-start = (bf16[256,768]{1,0:T(8,128)(2,1)S(1)}, bf16[256,768]{1,0:T(8,128)(2,1)}, u32[]{:S(2)}, u32[]{:S(2)}) collective-permute-start(bf16[256,768]{1,0:T(8,128)(2,1)S(1)} %constant_dynamic-slice_fusion.refs_4_), channel_id=1, source_target_pairs={{0,8},{4,12},{8,0},{12,4},{16,24},{20,28},{24,16},{28,20},{1,9},{5... | collective-permute-start | bytes 1179656 | tf_op jit(solution)/shard_map/ppermute | solution.py:286
  5.2 10.7 %collective-permute-start.1 = (bf16[256,768]{1,0:T(8,128)(2,1)S(1)}, bf16[256,768]{1,0:T(8,128)(2,1)}, u32[]{:S(2)}, u32[]{:S(2)}) collective-permute-start(bf16[256,768]{1,0:T(8,128)(2,1)S(1)} %constant_dynamic-slice_fusion.refs_4_), channel_id=1, source_target_pairs={{0,4},{4,0},{8,12},{12,8},{16,20},{20,16},{24,28},{28,24},{1,5},{5... | collective-permute-start | bytes 1179656 | tf_op jit(solution)/shard_map/ppermute | solution.py:286
  6.7 9.2 %collective-permute-start.2 = (bf16[256,768]{1,0:T(8,128)(2,1)S(1)}, bf16[256,768]{1,0:T(8,128)(2,1)}, u32[]{:S(2)}, u32[]{:S(2)}) collective-permute-start(bf16[256,768]{1,0:T(8,128)(2,1)S(1)} %constant_dynamic-slice_fusion.refs_4_), channel_id=1, source_target_pairs={{8,16},{12,20},{16,8},{20,12},{9,17},{13,21},{17,9},{21,13},{10,18... | collective-permute-start | bytes 1179656 | tf_op jit(solution)/shard_map/ppermute | solution.py:290
  8.2 1.0 copy-start.3
  9.2 1.0 copy-start.5
  12.3 3.6 %copy-start.13 = (bf16[4,128,256]{2,1,0:T(8,128)(2,1)}, bf16[4,128,256]{2,1,0:T(8,128)(2,1)S(1)}, u32[]{:S(2)}) copy-start(bf16[4,128,256]{2,1,0:T(8,128)(2,1)S(1)} %get-tuple-element.63.refs_0_) | copy-start | bytes 786436
  15.9 19.9 %collective-permute-start.3 = (bf16[256,768]{1,0:T(8,128)(2,1)S(1)}, bf16[256,768]{1,0:T(8,128)(2,1)}, u32[]{:S(2)}, u32[]{:S(2)}) collective-permute-start(bf16[256,768]{1,0:T(8,128)(2,1)S(1)} %get-tuple-element.58.refs_4_.refs_0_), channel_id=1, source_target_pairs={{0,24},{4,28},{24,0},{28,4},{1,25},{5,29},{25,1},{29,5},{2,26},{6,... | collective-permute-start | bytes 1179656 | tf_op jit(solution)/shard_map/ppermute | solution.py:290
  20.2 15.6 %collective-permute-start.5 = (bf16[256,768]{1,0:T(8,128)(2,1)}, bf16[256,768]{1,0:T(8,128)(2,1)}, u32[]{:S(2)}, u32[]{:S(2)}) collective-permute-start(bf16[256,768]{1,0:T(8,128)(2,1)} %get-tuple-element.60.refs_6_.refs_2_), channel_id=1, source_target_pairs={{0,4},{4,0},{8,12},{12,8},{16,20},{20,16},{24,28},{28,24},{1,5},{5... | collective-permute-start | bytes 1179656 | tf_op jit(solution)/shard_map/ppermute | solution.py:286
  21.8 14.0 %collective-permute-start.4 = (bf16[4,128,256]{2,1,0:T(8,128)(2,1)}, bf16[4,128,256]{2,1,0:T(8,128)(2,1)}, u32[]{:S(2)}, u32[]{:S(2)}) collective-permute-start(bf16[4,128,256]{2,1,0:T(8,128)(2,1)} %get-tuple-element.59), channel_id=1, source_target_pairs={{0,4},{4,0},{8,12},{12,8},{16,20},{20,16},{24,28},{28,24},{1,5},{5... | collective-permute-start | bytes 786440 | tf_op jit(solution)/shard_map/ppermute | solution.py:286
  36.8 29.1 %copy-start.22 = (bf16[256,768]{1,0:T(8,128)(2,1)}, bf16[256,768]{1,0:T(8,128)(2,1)S(1)}, u32[]{:S(2)}) copy-start(bf16[256,768]{1,0:T(8,128)(2,1)S(1)} %broadcast_select_fusion.1.refs_11_.refs_7_) | copy-start | bytes 1179652
  36.9 17.1 %collective-permute-start.6 = (bf16[256,768]{1,0:T(8,128)(2,1)S(1)}, bf16[256,768]{1,0:T(8,128)(2,1)S(1)}, u32[]{:S(2)}, u32[]{:S(2)}) collective-permute-start(bf16[256,768]{1,0:T(8,128)(2,1)S(1)} %broadcast_select_fusion.1.refs_11_.refs_7_), channel_id=1, source_target_pairs={{0,8},{4,12},{8,0},{12,4},{16,24},{20,28},{24,16},{28,20},{1,9},{5... | collective-permute-start | bytes 1179656 | tf_op jit(solution)/shard_map/ppermute | solution.py:286
  38.5 15.5 %collective-permute-start.7 = (bf16[256,768]{1,0:T(8,128)(2,1)S(1)}, bf16[256,768]{1,0:T(8,128)(2,1)S(1)}, u32[]{:S(2)}, u32[]{:S(2)}) collective-permute-start(bf16[256,768]{1,0:T(8,128)(2,1)S(1)} %broadcast_select_fusion.1.refs_11_.refs_7_), channel_id=1, source_target_pairs={{0,4},{4,0},{8,12},{12,8},{16,20},{20,16},{24,28},{28,24},{1,5},{5... | collective-permute-start | bytes 1179656 | tf_op jit(solution)/shard_map/ppermute | solution.py:286
  39.0 0.9 copy-start.14
  42.5 10.5 %collective-permute-start.10 = (bf16[2,128,256]{2,1,0:T(8,128)(2,1)S(1)}, bf16[2,128,256]{2,1,0:T(8,128)(2,1)S(1)}, u32[]{:S(2)}, u32[]{:S(2)}) collective-permute-start(bf16[2,128,256]{2,1,0:T(8,128)(2,1)S(1)} %get-tuple-element.68), channel_id=1, source_target_pairs={{0,24},{4,28},{8,16},{12,20},{16,8},{20,12},{24,0},{28,4},{1,25},{... | collective-permute-start | bytes 393224 | tf_op jit(solution)/shard_map/ppermute | solution.py:286
  44.9 9.1 %collective-permute-start.8 = (bf16[2,128,256]{2,1,0:T(8,128)(2,1)S(1)}, bf16[2,128,256]{2,1,0:T(8,128)(2,1)S(1)}, u32[]{:S(2)}, u32[]{:S(2)}) collective-permute-start(bf16[2,128,256]{2,1,0:T(8,128)(2,1)S(1)} %get-tuple-element.66), channel_id=1, source_target_pairs={{0,8},{4,12},{8,0},{12,4},{16,24},{20,28},{24,16},{28,20},{1,9},{5... | collective-permute-start | bytes 393224 | tf_op jit(solution)/shard_map/ppermute | solution.py:286
  44.9 9.1 %collective-permute-start.9 = (bf16[2,128,256]{2,1,0:T(8,128)(2,1)S(1)}, bf16[2,128,256]{2,1,0:T(8,128)(2,1)S(1)}, u32[]{:S(2)}, u32[]{:S(2)}) collective-permute-start(bf16[2,128,256]{2,1,0:T(8,128)(2,1)S(1)} %get-tuple-element.67), channel_id=1, source_target_pairs={{0,16},{4,20},{8,24},{12,28},{16,0},{20,4},{24,8},{28,12},{1,17},{... | collective-permute-start | bytes 393224 | tf_op jit(solution)/shard_map/ppermute | solution.py:286
  54.0 2.5 %copy-start.9 = (bf16[256,768]{1,0:T(8,128)(2,1)}, bf16[256,768]{1,0:T(8,128)(2,1)S(1)}, u32[]{:S(2)}) copy-start(bf16[256,768]{1,0:T(8,128)(2,1)S(1)} %get-tuple-element.73.refs_8_.refs_4_) | copy-start | bytes 1179652
  54.0 4.1 %copy-start.10 = (bf16[256,768]{1,0:T(8,128)(2,1)}, bf16[256,768]{1,0:T(8,128)(2,1)S(1)}, u32[]{:S(2)}) copy-start(bf16[256,768]{1,0:T(8,128)(2,1)S(1)} %get-tuple-element.74.refs_12_.refs_8_) | copy-start | bytes 1179652
  55.0 11.0 %collective-permute-start.12 = (bf16[4,2,128,256]{3,2,1,0:T(8,128)(2,1)}, bf16[4,2,128,256]{3,2,1,0:T(8,128)(2,1)}, u32[]{:S(2)}, u32[]{:S(2)}) collective-permute-start(bf16[4,2,128,256]{3,2,1,0:T(8,128)(2,1)} %pad_maximum_fusion.refs_0_), channel_id=1, source_target_pairs={{0,2},{1,3},{2,0},{3,1},{4,6},{5,7},{6,4},{7,5},{8,10},{9,11},{10,... | collective-permute-start | bytes 1572872 | tf_op jit(solution)/shard_map/ppermute | solution.py:293
  56.5 5.7 %collective-permute-start.13 = (bf16[128,768]{1,0:T(8,128)(2,1)S(1)}, bf16[128,768]{1,0:T(8,128)(2,1)S(1)}, u32[]{:S(2)}, u32[]{:S(2)}) collective-permute-start(bf16[128,768]{1,0:T(8,128)(2,1)S(1)} %slice.24), channel_id=1, source_target_pairs={{0,4},{4,0},{8,12},{12,8},{16,20},{20,16},{24,28},{28,24},{1,5},{5... | collective-permute-start | bytes 589832 | tf_op jit(solution)/shard_map/ppermute | solution.py:286
  58.1 5.7 %collective-permute-start.14 = (bf16[128,768]{1,0:T(8,128)(2,1)S(1)}, bf16[128,768]{1,0:T(8,128)(2,1)S(1)}, u32[]{:S(2)}, u32[]{:S(2)}) collective-permute-start(bf16[128,768]{1,0:T(8,128)(2,1)S(1)} %slice.25), channel_id=1, source_target_pairs={{0,8},{4,12},{8,0},{12,4},{16,24},{20,28},{24,16},{28,20},{1,9},{5... | collective-permute-start | bytes 589832 | tf_op jit(solution)/shard_map/ppermute | solution.py:286
  59.5 9.4 %collective-permute-start.11 = (bf16[4,2,128,256]{3,2,1,0:T(8,128)(2,1)}, bf16[4,2,128,256]{3,2,1,0:T(8,128)(2,1)}, u32[]{:S(2)}, u32[]{:S(2)}) collective-permute-start(bf16[4,2,128,256]{3,2,1,0:T(8,128)(2,1)} %pad_maximum_fusion.refs_0_), channel_id=1, source_target_pairs={{0,1},{1,0},{2,3},{3,2},{4,5},{5,4},{6,7},{7,6},{8,9},{9,8},{10,11... | collective-permute-start | bytes 1572872 | tf_op jit(solution)/shard_map/ppermute | solution.py:293
  63.8 2.1 %copy-start.18 = (bf16[128,768]{1,0:T(8,128)(2,1)}, bf16[128,768]{1,0:T(8,128)(2,1)S(1)}, u32[]{:S(2)}) copy-start(bf16[128,768]{1,0:T(8,128)(2,1)S(1)} %collective-permute-done.14.refs_2_.refs_10_.refs_6_) | copy-start | bytes 589828
  66.7 2.3 %collective-permute-start.15 = (bf16[4,2,128,256]{3,2,1,0:T(8,128)(2,1)}, bf16[4,2,128,256]{3,2,1,0:T(8,128)(2,1)}, u32[]{:S(2)}, u32[]{:S(2)}) collective-permute-start(bf16[4,2,128,256]{3,2,1,0:T(8,128)(2,1)} %shard_map.114.refs_2_), channel_id=1, source_target_pairs={{0,1},{1,0},{2,3},{3,2},{4,5},{5,4},{6,7},{7,6},{8,9},{9,8},{10,11... | collective-permute-start | bytes 1572872 | tf_op jit(solution)/shard_map/ppermute | solution.py:293
  66.7 11.5 %copy-start.17 = (bf16[128,768]{1,0:T(8,128)(2,1)S(1)}, bf16[128,768]{1,0:T(8,128)(2,1)}, u32[]{:S(2)}) copy-start(bf16[128,768]{1,0:T(8,128)(2,1)} %copy-done.15) | copy-start | bytes 589828
  66.7 11.5 %copy-start.20 = (bf16[128,768]{1,0:T(8,128)(2,1)S(1)}, bf16[128,768]{1,0:T(8,128)(2,1)}, u32[]{:S(2)}) copy-start(bf16[128,768]{1,0:T(8,128)(2,1)} %copy-done.18) | copy-start | bytes 589828
  66.8 36.4 %copy-start.7 = (f32[128,3072]{1,0:T(8,128)S(1)}, f32[128,3072]{1,0:T(8,128)}, u32[]{:S(2)}) copy-start(f32[128,3072]{1,0:T(8,128)} %refs_6_.1) | copy-start | bytes 4718596
  66.8 36.4 %copy-start.8 = (f32[128,3072]{1,0:T(8,128)S(1)}, f32[128,3072]{1,0:T(8,128)}, u32[]{:S(2)}) copy-start(f32[128,3072]{1,0:T(8,128)} %refs_7_.1) | copy-start | bytes 4718596
  66.8 11.4 %collective-permute-start.27 = (bf16[128,768]{1,0:T(8,128)(2,1)S(1)}, bf16[128,768]{1,0:T(8,128)(2,1)S(1)}, u32[]{:S(2)}, u32[]{:S(2)}) collective-permute-start(bf16[128,768]{1,0:T(8,128)(2,1)S(1)} %get-tuple-element.111), channel_id=1, source_target_pairs={{0,1},{1,0},{2,3},{3,2},{4,5},{5,4},{6,7},{7,6},{8,9},{9,8},{10,11... | collective-permute-start | bytes 589832 | tf_op jit(solution)/shard_map/ppermute | solution.py:293
  67.4 10.8 %collective-permute-start.28 = (bf16[128,768]{1,0:T(8,128)(2,1)S(1)}, bf16[128,768]{1,0:T(8,128)(2,1)S(1)}, u32[]{:S(2)}, u32[]{:S(2)}) collective-permute-start(bf16[128,768]{1,0:T(8,128)(2,1)S(1)} %get-tuple-element.113), channel_id=1, source_target_pairs={{0,2},{1,3},{2,0},{3,1},{4,6},{5,7},{6,4},{7,5},{8,10},{9,11},{10,... | collective-permute-start | bytes 589832 | tf_op jit(solution)/shard_map/ppermute | solution.py:293
  68.9 9.3 %collective-permute-start.29 = (bf16[128,768]{1,0:T(8,128)(2,1)S(1)}, bf16[128,768]{1,0:T(8,128)(2,1)S(1)}, u32[]{:S(2)}, u32[]{:S(2)}) collective-permute-start(bf16[128,768]{1,0:T(8,128)(2,1)S(1)} %get-tuple-element.110), channel_id=1, source_target_pairs={{0,3},{1,2},{2,1},{3,0},{4,7},{5,6},{6,5},{7,4},{8,11},{9,10},{10,... | collective-permute-start | bytes 589832 | tf_op jit(solution)/shard_map/ppermute | solution.py:293
  68.9 0.9 copy-start.16
  69.9 0.9 copy-start.19
  77.4 0.7 copy-start.11
  78.2 25.0 %copy-start.12 = (f32[128,768]{1,0:T(8,128)S(1)}, f32[128,768]{1,0:T(8,128)}, u32[]{:S(2)}) copy-start(f32[128,768]{1,0:T(8,128)} %copy-done.11) | copy-start | bytes 1179652
  83.7 29.5 %collective-permute-start.30 = (f32[2,2048,128]{2,1,0:T(8,128)}, f32[2,2048,128]{2,1,0:T(8,128)}, u32[]{:S(2)}, u32[]{:S(2)}) collective-permute-start(f32[2,2048,128]{2,1,0:T(8,128)} %get-tuple-element.83), channel_id=1, source_target_pairs={{0,1},{1,0},{2,3},{3,2},{4,5},{5,4},{6,7},{7,6},{8,9},{9,8},{10,11... | collective-permute-start | bytes 6291464 | tf_op jit(solution)/shard_map/ppermute | solution.py:293
  84.4 18.8 %collective-permute-start.21 = (bf16[128,768]{1,0:T(8,128)(2,1)S(1)}, bf16[128,768]{1,0:T(8,128)(2,1)S(1)}, u32[]{:S(2)}, u32[]{:S(2)}) collective-permute-start(bf16[128,768]{1,0:T(8,128)(2,1)S(1)} %get-tuple-element.78), channel_id=1, source_target_pairs={{0,1},{1,0},{2,3},{3,2},{4,5},{5,4},{6,7},{7,6},{8,9},{9,8},{10,11... | collective-permute-start | bytes 589832 | tf_op jit(solution)/shard_map/ppermute | solution.py:293
  84.5 18.7 %collective-permute-start.22 = (bf16[128,768]{1,0:T(8,128)(2,1)S(1)}, bf16[128,768]{1,0:T(8,128)(2,1)S(1)}, u32[]{:S(2)}, u32[]{:S(2)}) collective-permute-start(bf16[128,768]{1,0:T(8,128)(2,1)S(1)} %get-tuple-element.79), channel_id=1, source_target_pairs={{0,2},{1,3},{2,0},{3,1},{4,6},{5,7},{6,4},{7,5},{8,10},{9,11},{10,... | collective-permute-start | bytes 589832 | tf_op jit(solution)/shard_map/ppermute | solution.py:293
  86.0 17.2 %collective-permute-start.23 = (bf16[128,768]{1,0:T(8,128)(2,1)S(1)}, bf16[128,768]{1,0:T(8,128)(2,1)S(1)}, u32[]{:S(2)}, u32[]{:S(2)}) collective-permute-start(bf16[128,768]{1,0:T(8,128)(2,1)S(1)} %get-tuple-element.80), channel_id=1, source_target_pairs={{0,3},{1,2},{2,1},{3,0},{4,7},{5,6},{6,5},{7,4},{8,11},{9,10},{10,... | collective-permute-start | bytes 589832 | tf_op jit(solution)/shard_map/ppermute | solution.py:293
  86.3 4.0 %collective-permute-start.16 = (f32[8,128]{1,0:T(8,128)S(1)}, f32[8,128]{1,0:T(8,128)S(1)}, u32[]{:S(2)}, u32[]{:S(2)}) collective-permute-start(f32[8,128]{1,0:T(8,128)S(1)} %get-tuple-element.76), channel_id=1, source_target_pairs={{0,4},{4,0},{8,12},{12,8},{16,20},{20,16},{24,28},{28,24},{1,5},{5... | collective-permute-start | bytes 12296 | tf_op jit(solution)/shard_map/ppermute | solution.py:286
  90.3 3.6 %collective-permute-start.17 = (f32[8,128]{1,0:T(8,128)S(1)}, f32[8,128]{1,0:T(8,128)S(1)}, u32[]{:S(2)}, u32[]{:S(2)}) collective-permute-start(f32[8,128]{1,0:T(8,128)S(1)} %add.80), channel_id=1, source_target_pairs={{0,8},{4,12},{8,0},{12,4},{16,24},{20,28},{24,16},{28,20},{1,9},{5... | collective-permute-start | bytes 12296 | tf_op jit(solution)/shard_map/ppermute | solution.py:286
  93.9 4.5 %collective-permute-start.18 = (f32[8,128]{1,0:T(8,128)S(1)}, f32[8,128]{1,0:T(8,128)S(1)}, u32[]{:S(2)}, u32[]{:S(2)}) collective-permute-start(f32[8,128]{1,0:T(8,128)S(1)} %add.81), channel_id=1, source_target_pairs={{0,16},{4,20},{8,24},{12,28},{16,0},{20,4},{24,8},{28,12},{1,17},{... | collective-permute-start | bytes 12296 | tf_op jit(solution)/shard_map/ppermute | solution.py:286
  98.4 1.2 collective-permute-start.19
  99.6 3.6 %collective-permute-start.20 = (f32[8,128]{1,0:T(8,128)S(1)}, f32[8,128]{1,0:T(8,128)S(1)}, u32[]{:S(2)}, u32[]{:S(2)}) collective-permute-start(f32[8,128]{1,0:T(8,128)S(1)} %add.83), channel_id=1, source_target_pairs={{0,2},{1,3},{2,0},{3,1},{4,6},{5,7},{6,4},{7,5},{8,10},{9,11},{10,... | collective-permute-start | bytes 12296 | tf_op jit(solution)/shard_map/ppermute | solution.py:293
  108.4 18.8 %collective-permute-start.24 = (bf16[128,3072]{1,0:T(8,128)(2,1)}, bf16[128,3072]{1,0:T(8,128)(2,1)S(1)}, u32[]{:S(2)}, u32[]{:S(2)}) collective-permute-start(bf16[128,3072]{1,0:T(8,128)(2,1)} %get-tuple-element.81.refs_4_), channel_id=1, source_target_pairs={{0,8},{4,12},{8,0},{12,4},{16,24},{20,28},{24,16},{28,20},{1,9},{5... | collective-permute-start | bytes 2359304 | tf_op jit(solution)/shard_map/ppermute | solution.py:286
  110.3 18.4 %collective-permute-start.25 = (bf16[128,3072]{1,0:T(8,128)(2,1)}, bf16[128,3072]{1,0:T(8,128)(2,1)S(1)}, u32[]{:S(2)}, u32[]{:S(2)}) collective-permute-start(bf16[128,3072]{1,0:T(8,128)(2,1)} %get-tuple-element.81.refs_4_), channel_id=1, source_target_pairs={{0,4},{4,0},{8,12},{12,8},{16,20},{20,16},{24,28},{28,24},{1,5},{5... | collective-permute-start | bytes 2359304 | tf_op jit(solution)/shard_map/ppermute | solution.py:286
  111.7 16.9 %collective-permute-start.26 = (bf16[128,3072]{1,0:T(8,128)(2,1)}, bf16[128,3072]{1,0:T(8,128)(2,1)}, u32[]{:S(2)}, u32[]{:S(2)}) collective-permute-start(bf16[128,3072]{1,0:T(8,128)(2,1)} %get-tuple-element.81.refs_4_), channel_id=1, source_target_pairs={{8,16},{12,20},{16,8},{20,12},{9,17},{13,21},{17,9},{21,13},{10,18... | collective-permute-start | bytes 2359304 | tf_op jit(solution)/shard_map/ppermute | solution.py:290
  113.3 1.6 copy-start.2
  128.7 25.9 %collective-permute-start.35 = (f32[2048,128]{1,0:T(8,128)S(1)}, f32[2048,128]{1,0:T(8,128)S(1)}, u32[]{:S(2)}, u32[]{:S(2)}) collective-permute-start(f32[2048,128]{1,0:T(8,128)S(1)} %get-tuple-element.90), channel_id=1, source_target_pairs={{0,2},{1,3},{2,0},{3,1},{4,6},{5,7},{6,4},{7,5},{8,10},{9,11},{10,... | collective-permute-start | bytes 3145736 | tf_op jit(solution)/shard_map/ppermute | solution.py:293
  130.2 20.8 %collective-permute-start.31 = (bf16[128,3072]{1,0:T(8,128)(2,1)}, bf16[128,3072]{1,0:T(8,128)(2,1)S(1)}, u32[]{:S(2)}, u32[]{:S(2)}) collective-permute-start(bf16[128,3072]{1,0:T(8,128)(2,1)} %get-tuple-element.85), channel_id=1, source_target_pairs={{0,24},{4,28},{24,0},{28,4},{1,25},{5,29},{25,1},{29,5},{2,26},{6,... | collective-permute-start | bytes 2359304 | tf_op jit(solution)/shard_map/ppermute | solution.py:290
  134.3 16.7 %collective-permute-start.32 = (bf16[128,3072]{1,0:T(8,128)(2,1)S(1)}, bf16[128,3072]{1,0:T(8,128)(2,1)S(1)}, u32[]{:S(2)}, u32[]{:S(2)}) collective-permute-start(bf16[128,3072]{1,0:T(8,128)(2,1)S(1)} %get-tuple-element.86), channel_id=1, source_target_pairs={{0,4},{4,0},{8,12},{12,8},{16,20},{20,16},{24,28},{28,24},{1,5},{5... | collective-permute-start | bytes 2359304 | tf_op jit(solution)/shard_map/ppermute | solution.py:286
  152.3 5.3 %copy-start.21 = (bf16[1024,3072]{1,0:T(8,128)(2,1)}, bf16[1024,3072]{1,0:T(8,128)(2,1)S(1)}, u32[]{:S(2)}) copy-start(bf16[1024,3072]{1,0:T(8,128)(2,1)S(1)} %get-tuple-element.108) | copy-start | bytes 18874372
  152.3 25.9 %collective-permute-start.33 = (bf16[128,3072]{1,0:T(8,128)(2,1)}, bf16[128,3072]{1,0:T(8,128)(2,1)S(1)}, u32[]{:S(2)}, u32[]{:S(2)}) collective-permute-start(bf16[128,3072]{1,0:T(8,128)(2,1)} %get-tuple-element.109), channel_id=1, source_target_pairs={{0,8},{4,12},{8,0},{12,4},{16,24},{20,28},{24,16},{28,20},{1,9},{5... | collective-permute-start | bytes 2359304 | tf_op jit(solution)/shard_map/ppermute | solution.py:286
  154.0 24.1 %collective-permute-start.34 = (bf16[128,3072]{1,0:T(8,128)(2,1)}, bf16[128,3072]{1,0:T(8,128)(2,1)S(1)}, u32[]{:S(2)}, u32[]{:S(2)}) collective-permute-start(bf16[128,3072]{1,0:T(8,128)(2,1)} %get-tuple-element.109), channel_id=1, source_target_pairs={{0,4},{4,0},{8,12},{12,8},{16,20},{20,16},{24,28},{28,24},{1,5},{5... | collective-permute-start | bytes 2359304 | tf_op jit(solution)/shard_map/ppermute | solution.py:286
  156.4 19.1 %collective-permute-start.36 = (bf16[512,128]{1,0:T(8,128)(2,1)}, bf16[512,128]{1,0:T(8,128)(2,1)S(1)}, u32[]{:S(2)}, u32[]{:S(2)}) collective-permute-start(bf16[512,128]{1,0:T(8,128)(2,1)} %get-tuple-element.92), channel_id=1, source_target_pairs={{0,8},{4,12},{8,0},{12,4},{16,24},{20,28},{24,16},{28,20},{1,9},{5... | collective-permute-start | bytes 393224 | tf_op jit(solution)/shard_map/ppermute | solution.py:286
  157.6 17.9 %collective-permute-start.37 = (bf16[512,128]{1,0:T(8,128)(2,1)}, bf16[512,128]{1,0:T(8,128)(2,1)S(1)}, u32[]{:S(2)}, u32[]{:S(2)}) collective-permute-start(bf16[512,128]{1,0:T(8,128)(2,1)} %get-tuple-element.93), channel_id=1, source_target_pairs={{0,16},{4,20},{8,24},{12,28},{16,0},{20,4},{24,8},{28,12},{1,17},{... | collective-permute-start | bytes 393224 | tf_op jit(solution)/shard_map/ppermute | solution.py:286
  159.0 19.2 %collective-permute-start.38 = (bf16[512,128]{1,0:T(8,128)(2,1)}, bf16[512,128]{1,0:T(8,128)(2,1)}, u32[]{:S(2)}, u32[]{:S(2)}) collective-permute-start(bf16[512,128]{1,0:T(8,128)(2,1)} %get-tuple-element.94), channel_id=1, source_target_pairs={{0,24},{4,28},{8,16},{12,20},{16,8},{20,12},{24,0},{28,4},{1,25},{... | collective-permute-start | bytes 393224 | tf_op jit(solution)/shard_map/ppermute | solution.py:286
  160.8 28.9 %copy-start.4 = (bf16[256,1024]{1,0:T(8,128)(2,1)S(1)}, bf16[256,1024]{1,0:T(8,128)(2,1)}, u32[]{:S(2)}) copy-start(bf16[256,1024]{1,0:T(8,128)(2,1)} %refs_0_.3) | copy-start | bytes 1572868
  160.8 28.9 %copy-start.6 = (bf16[256,1024]{1,0:T(8,128)(2,1)S(1)}, bf16[256,1024]{1,0:T(8,128)(2,1)}, u32[]{:S(2)}) copy-start(bf16[256,1024]{1,0:T(8,128)(2,1)} %refs_1_.3) | copy-start | bytes 1572868
  178.2 15.5 %collective-permute-start.40 = (bf16[64,3072]{1,0:T(8,128)(2,1)S(1)}, bf16[64,3072]{1,0:T(8,128)(2,1)S(1)}, u32[]{:S(2)}, u32[]{:S(2)}) collective-permute-start(bf16[64,3072]{1,0:T(8,128)(2,1)S(1)} %slice.30), channel_id=1, source_target_pairs={{0,4},{4,0},{8,12},{12,8},{16,20},{20,16},{24,28},{28,24},{1,5},{5... | collective-permute-start | bytes 1179656 | tf_op jit(solution)/shard_map/ppermute | solution.py:286
  180.4 14.1 %collective-permute-start.41 = (bf16[64,3072]{1,0:T(8,128)(2,1)S(1)}, bf16[64,3072]{1,0:T(8,128)(2,1)S(1)}, u32[]{:S(2)}, u32[]{:S(2)}) collective-permute-start(bf16[64,3072]{1,0:T(8,128)(2,1)S(1)} %slice.31), channel_id=1, source_target_pairs={{0,8},{4,12},{8,0},{12,4},{16,24},{20,28},{24,16},{28,20},{1,9},{5... | collective-permute-start | bytes 1179656 | tf_op jit(solution)/shard_map/ppermute | solution.py:286
  181.4 8.3 %collective-permute-start.39 = (bf16[4,256,128]{2,1,0:T(8,128)(2,1)S(1)}, bf16[4,256,128]{2,1,0:T(8,128)(2,1)S(1)}, u32[]{:S(2)}, u32[]{:S(2)}) collective-permute-start(bf16[4,256,128]{2,1,0:T(8,128)(2,1)S(1)} %pad_maximum_fusion.1), channel_id=1, source_target_pairs={{0,4},{4,0},{8,12},{12,8},{16,20},{20,16},{24,28},{28,24},{1,5},{5... | collective-permute-start | bytes 786440 | tf_op jit(solution)/shard_map/ppermute | solution.py:286
  (1 other events, 0.7 us)

commit v5 on v4

--- a/solution.py
+++ b/solution.py
@@ -409,8 +409,10 @@
     blocks = call(back_body, (pair,) * 4, (spot, mine, came), moved=3 << 20)
     blocks = [blocks[0]] + [across(blocks[m], 2 * m) for m in (1, 2, 3)]
     far, last_x, *blocks = together(far, last_x, *blocks)
+    given = jnp.stack([b[tokens:] for b in blocks])
+    far, last_x = together(far, last_x, after=(given,))
+    came = across(given, 1)
     low, high = across(far[:half], 1), across(last_x[half:], 2)
-    came = across(jnp.stack([b[tokens:] for b in blocks]), 1)
     out = shaped((tokens, width), BF16)
     gate_grad, up_grad = call(
         outputs_body, (out, out), (spot, gate, up_proj, *blocks, came), moved=4 << 20

time: 196 us -> 193 us (0.985)
  waiting for transfers between devices: 87.2 us -> 84.1 us
    ppermute x25, waiting for transfers between devices: 68.3 us -> 65.2 us  [across(): return lax.ppermute(value, 'dp', [(i, i ^ m) for i in range(n)])]
  transfers between devices with their start and end apart: 42 -> 42, of which waited for: 19 -> 20; matrix products, arithmetic and copies ran while one was open for 4% -> 3% of each run, Pallas kernels for 13% -> 13%
where the time goes in v5:
time: 193 us; the launch traced here: 192 us
  waiting for transfers between devices  84.1 us (44%)
  starting transfers between devices  57.1 us (30%)
  Pallas kernels  30.5 us (16%)
  local copies, waits for them, and re-layouts  16 us (8%)
  other arithmetic  3.27 us (2%)
    ppermute x25, waiting for transfers between devices, across(): return lax.ppermute(value, 'dp', [(i, i ^ m) for i in range(n)])  65.2 us
    ppermute x25, starting transfers between devices, across(): return lax.ppermute(value, 'dp', [(i, i ^ m) for i in range(n)])  36.5 us
    pallas_call x8, Pallas kernels, call(): pl.pallas_call(kernel, out_shape=tuple(outs), in_specs=[SMEM] + specs + [...  30.5 us
    ppermute x4, waiting for transfers between devices, line(): lax.ppermute(value, 'dp', [(i, i - i % CELL + b * 2 + i % 2) for i, b in...  13.5 us
    ppermute x4, starting transfers between devices, line(): lax.ppermute(value, 'dp', [(i, i - i % CELL + b * 2 + i % 2) for i, b in...  11.4 us
    unnamed x46, local copies, waits for them, and re-layouts  9.35 us
    ppermute x13, starting transfers between devices, swap(): return lax.ppermute(value, 'tensor', [(i, i ^ m) for i in range(4)])  9.2 us
    ppermute x13, waiting for transfers between devices, swap(): return lax.ppermute(value, 'tensor', [(i, i ^ m) for i in range(4)])  5.43 us
  transfers between devices with their start and end apart: 42, of which 20 were waited for; matrix products, arithmetic and copies ran while one was open for 3% of the time, Pallas kernels for 13%

profile of v5, /device:TPU:0, one launch (start us, length us, event | category | flops | bytes accessed | tf_op | source)
XLA Modules:
  0.0 192.1 jit_solution(4925929627573673392)
XLA Ops:
  0.7 1.4 copy-done
  2.1 3.1 %collective-permute-start = (bf16[256,768]{1,0:T(8,128)(2,1)S(1)}, bf16[256,768]{1,0:T(8,128)(2,1)}, u32[]{:S(2)}, u32[]{:S(2)}) collective-permute-start(bf16[256,768]{1,0:T(8,128)(2,1)S(1)} %constant_dynamic-slice_fusion.refs_4_), channel_id=1, source_target_pairs={{0,8},{4,12},{8,0},{12,4},{16,24},{20,28},{24,16},{28,20},{1,9},{5... | collective-permute-start | bytes 1179656 | tf_op jit(solution)/shard_map/ppermute | solution.py:286
  5.2 1.5 collective-permute-start.1
  6.7 1.4 collective-permute-start.2
  8.2 1.0 copy-done.3
  9.2 1.0 copy-done.5
  10.3 2.0 %shard_map.109 = (bf16[4,128,256]{2,1,0:T(8,128)(2,1)S(1)}, bf16[4,128,256]{2,1,0:T(8,128)(2,1)}) custom-call(s32[3]{0:T(128)S(1)} %pad_add_fusion.spot, bf16[256,1024]{1,0:T(8,128)(2,1)S(1)} %copy-done.3, bf16[256,1024]{1,0:T(8,128)(2,1)S(1)} %copy-done.5), custom_call_target="tpu_custom_call" | custom-call | bytes 2097152 | tf_op jit(solution)/shard_map/pallas_call | solution.py:102
  12.3 2.1 %collective-permute-done.refs_0_ = bf16[256,768]{1,0:T(8,128)(2,1)} collective-permute-done((bf16[256,768]{1,0:T(8,128)(2,1)S(1)}, bf16[256,768]{1,0:T(8,128)(2,1)}, u32[]{:S(2)}, u32[]{:S(2)}) %collective-permute-start) | collective-permute-done | bytes 393248 | tf_op jit(solution)/shard_map/ppermute | solution.py:286
  14.4 1.5 collective-permute-done.1.refs_1_
  15.9 4.4 %collective-permute-start.3 = (bf16[256,768]{1,0:T(8,128)(2,1)S(1)}, bf16[256,768]{1,0:T(8,128)(2,1)}, u32[]{:S(2)}, u32[]{:S(2)}) collective-permute-start(bf16[256,768]{1,0:T(8,128)(2,1)S(1)} %get-tuple-element.60.refs_4_.refs_0_), channel_id=1, source_target_pairs={{0,24},{4,28},{24,0},{28,4},{1,25},{5,29},{25,1},{29,5},{2,26},{6,... | collective-permute-start | bytes 1179656 | tf_op jit(solution)/shard_map/ppermute | solution.py:290
  20.2 1.6 collective-permute-start.5
  22.3 13.5 %collective-permute-done.4.refs_1_ = bf16[4,128,256]{2,1,0:T(8,128)(2,1)} collective-permute-done((bf16[4,128,256]{2,1,0:T(8,128)(2,1)}, bf16[4,128,256]{2,1,0:T(8,128)(2,1)}, u32[]{:S(2)}, u32[]{:S(2)}) %collective-permute-start.4) | collective-permute-done | bytes 262176 | tf_op jit(solution)/shard_map/ppermute | solution.py:286
  35.8 1.0 broadcast_select_fusion.1.refs_11_.refs_7_
  36.9 1.7 collective-permute-start.6
  39.0 0.9 copy-done.14
  40.0 2.5 %shard_map.112 = (bf16[2,128,256]{2,1,0:T(8,128)(2,1)S(1)}, bf16[2,128,256]{2,1,0:T(8,128)(2,1)S(1)}, bf16[2,128,256]{2,1,0:T(8,128)(2,1)S(1)}, bf16[2,128,256]{2,1,0:T(8,128)(2,1)S(1)}) custom-call(s32[3]{0:T(128)S(1)} %pad_add_fusion.spot, bf16[4,128,256]{2,1,0:T(8,128)(2,1)S(1)} %copy-done.14, bf16[4,128,256]{2,1,0:T(8,128)(2,1)} %get-tuple-element.66.refs_1_), custom_call_target="tpu_custom_call" | custom-call | bytes 1048576 | tf_op jit(solution)/shard_map/pallas_call | solution.py:102
  42.5 2.4 %collective-permute-start.10 = (bf16[2,128,256]{2,1,0:T(8,128)(2,1)S(1)}, bf16[2,128,256]{2,1,0:T(8,128)(2,1)S(1)}, u32[]{:S(2)}, u32[]{:S(2)}) collective-permute-start(bf16[2,128,256]{2,1,0:T(8,128)(2,1)S(1)} %get-tuple-element.70), channel_id=1, source_target_pairs={{0,24},{4,28},{8,16},{12,20},{16,8},{20,12},{24,0},{28,4},{1,25},{... | collective-permute-start | bytes 393224 | tf_op jit(solution)/shard_map/ppermute | solution.py:286
  44.9 2.0 %collective-permute-start.9 = (bf16[2,128,256]{2,1,0:T(8,128)(2,1)S(1)}, bf16[2,128,256]{2,1,0:T(8,128)(2,1)S(1)}, u32[]{:S(2)}, u32[]{:S(2)}) collective-permute-start(bf16[2,128,256]{2,1,0:T(8,128)(2,1)S(1)} %get-tuple-element.69), channel_id=1, source_target_pairs={{0,16},{4,20},{8,24},{12,28},{16,0},{20,4},{24,8},{28,12},{1,17},{... | collective-permute-start | bytes 393224 | tf_op jit(solution)/shard_map/ppermute | solution.py:286
  47.0 6.0 %collective-permute-done.10.refs_5_ = bf16[2,128,256]{2,1,0:T(8,128)(2,1)S(1)} collective-permute-done((bf16[2,128,256]{2,1,0:T(8,128)(2,1)S(1)}, bf16[2,128,256]{2,1,0:T(8,128)(2,1)S(1)}, u32[]{:S(2)}, u32[]{:S(2)}) %collective-permute-start.10) | collective-permute-done | bytes 131104 | tf_op jit(solution)/shard_map/ppermute | solution.py:286
  53.0 1.0 collective-permute-done.8.refs_3_
  54.0 1.0 pad_maximum_fusion.refs_0_
  55.0 1.5 collective-permute-start.12
  56.5 1.6 collective-permute-start.13
  58.1 1.4 collective-permute-start.14
  59.5 2.8 %collective-permute-done.13.refs_1_.refs_9_.refs_5_ = bf16[128,768]{1,0:T(8,128)(2,1)S(1)} collective-permute-done((bf16[128,768]{1,0:T(8,128)(2,1)S(1)}, bf16[128,768]{1,0:T(8,128)(2,1)S(1)}, u32[]{:S(2)}, u32[]{:S(2)}) %collective-permute-start.13) | collective-permute-done | bytes 196640 | tf_op jit(solution)/shard_map/ppermute | solution.py:286
  62.3 1.6 collective-permute-done.14.refs_2_.refs_10_.refs_6_
  63.8 2.1 %collective-permute-done.12.refs_0_ = bf16[4,2,128,256]{3,2,1,0:T(8,128)(2,1)} collective-permute-done((bf16[4,2,128,256]{3,2,1,0:T(8,128)(2,1)}, bf16[4,2,128,256]{3,2,1,0:T(8,128)(2,1)}, u32[]{:S(2)}, u32[]{:S(2)}) %collective-permute-start.12) | collective-permute-done | bytes 524320 | tf_op jit(solution)/shard_map/ppermute | solution.py:293
  67.4 1.5 collective-permute-start.28
  70.8 6.7 %shard_map.115 = (f32[128,768]{1,0:T(8,128)S(1)}, bf16[128,768]{1,0:T(8,128)(2,1)S(1)}, bf16[128,768]{1,0:T(8,128)(2,1)S(1)}, bf16[128,768]{1,0:T(8,128)(2,1)S(1)}, f32[8,128]{1,0:T(8,128)S(1)}) custom-call(s32[3]{0:T(128)S(1)} %pad_add_fusion.spot, bf16[4,2,128,256]{3,2,1,0:T(8,128)(2,1)} %pad_maximum_fusion.refs_0_, ...), custom_call_target="tpu_custom_call" | custom-call | flops 1610612736 | bytes 8388608 | tf_op jit(solution)/shard_map/pallas_call | solution.py:102
  78.2 5.5 %shard_map.117 = (f32[2,2048,128]{2,1,0:T(8,128)}, f32[2,2048,128]{2,1,0:T(8,128)}) custom-call(s32[3]{0:T(128)S(1)} %pad_add_fusion.spot, bf16[256,768]{1,0:T(8,128)(2,1)S(1)} %get-tuple-element.60.refs_4_.refs_0_, bf16[256,768]{1,0:T(8,128)(2,1)} %get-tuple-element.77.refs_5_.refs_1_, bf16[256,768]{1,0:T(8,128)(2,1)} %get-tuple-element.62.refs_6_.refs_2_, ...), custom_call_target="tpu_custom_call" | custom-call | flops 1610612736 | bytes 10485760 | tf_op jit(solution)/shard_map/pallas_call | solution.py:102
  84.5 1.5 collective-permute-start.22
  86.3 2.4 %collective-permute-start.16 = (f32[8,128]{1,0:T(8,128)S(1)}, f32[8,128]{1,0:T(8,128)S(1)}, u32[]{:S(2)}, u32[]{:S(2)}) collective-permute-start(f32[8,128]{1,0:T(8,128)S(1)} %get-tuple-element.78), channel_id=1, source_target_pairs={{0,4},{4,0},{8,12},{12,8},{16,20},{20,16},{24,28},{28,24},{1,5},{5... | collective-permute-start | bytes 12296 | tf_op jit(solution)/shard_map/ppermute | solution.py:286
  88.7 1.6 collective-permute-done.16
  90.3 1.9 collective-permute-start.17
  92.2 1.7 collective-permute-done.17
  93.9 2.4 %collective-permute-start.18 = (f32[8,128]{1,0:T(8,128)S(1)}, f32[8,128]{1,0:T(8,128)S(1)}, u32[]{:S(2)}, u32[]{:S(2)}) collective-permute-start(f32[8,128]{1,0:T(8,128)S(1)} %add.81), channel_id=1, source_target_pairs={{0,16},{4,20},{8,24},{12,28},{16,0},{20,4},{24,8},{28,12},{1,17},{... | collective-permute-start | bytes 12296 | tf_op jit(solution)/shard_map/ppermute | solution.py:286
  96.4 2.1 %collective-permute-done.18 = f32[8,128]{1,0:T(8,128)S(1)} collective-permute-done((f32[8,128]{1,0:T(8,128)S(1)}, f32[8,128]{1,0:T(8,128)S(1)}, u32[]{:S(2)}, u32[]{:S(2)}) %collective-permute-start.18) | collective-permute-done | bytes 4128 | tf_op jit(solution)/shard_map/ppermute | solution.py:286
  98.4 1.2 collective-permute-done.19
  99.6 1.5 collective-permute-start.20
  101.1 2.1 %collective-permute-done.20 = f32[8,128]{1,0:T(8,128)S(1)} collective-permute-done((f32[8,128]{1,0:T(8,128)S(1)}, f32[8,128]{1,0:T(8,128)S(1)}, u32[]{:S(2)}, u32[]{:S(2)}) %collective-permute-start.20) | collective-permute-done | bytes 4128 | tf_op jit(solution)/shard_map/ppermute | solution.py:293
  103.3 5.1 %shard_map.116 = (f32[128,3072]{1,0:T(8,128)}, f32[128,3072]{1,0:T(8,128)}, f32[128,3072]{1,0:T(8,128)}, bf16[128,3072]{1,0:T(8,128)(2,1)}) custom-call(s32[3]{0:T(128)S(1)} %pad_add_fusion.spot, f32[8,128]{1,0:T(8,128)S(1)} %add.84.refs_0_, f32[128,768]{1,0:T(8,128)S(1)} %copy-done.12, bf16[128,768]{1,0:T(8,128)(2,1)S(1)} %collective-permute-done.21.refs_2_, ...), custom_call_target="tpu_custom_call" | custom-call | bytes 12582912 | tf_op jit(solution)/shard_map/pallas_call | solution.py:102
  108.4 1.9 %collective-permute-start.24 = (bf16[128,3072]{1,0:T(8,128)(2,1)}, bf16[128,3072]{1,0:T(8,128)(2,1)S(1)}, u32[]{:S(2)}, u32[]{:S(2)}) collective-permute-start(bf16[128,3072]{1,0:T(8,128)(2,1)} %get-tuple-element.83.refs_4_), channel_id=1, source_target_pairs={{0,8},{4,12},{8,0},{12,4},{16,24},{20,28},{24,16},{28,20},{1,9},{5... | collective-permute-start | bytes 2359304 | tf_op jit(solution)/shard_map/ppermute | solution.py:286
  110.3 1.4 collective-permute-start.25
  111.7 1.5 collective-permute-start.26
  113.3 1.6 copy-done.2
  114.9 3.0 %shard_map.118 = (f32[2048,128]{1,0:T(8,128)S(1)}, f32[2048,128]{1,0:T(8,128)S(1)}) custom-call(s32[3]{0:T(128)S(1)} %pad_add_fusion.spot, f32[2,2048,128]{2,1,0:T(8,128)S(1)} %copy-done.2, f32[2,2048,128]{2,1,0:T(8,128)} %collective-permute-done.30.refs_1_), custom_call_target="tpu_custom_call" | custom-call | bytes 6291456 | tf_op jit(solution)/shard_map/pallas_call | solution.py:102
  117.8 9.4 %collective-permute-done.24.refs_0_ = bf16[128,3072]{1,0:T(8,128)(2,1)S(1)} collective-permute-done((bf16[128,3072]{1,0:T(8,128)(2,1)}, bf16[128,3072]{1,0:T(8,128)(2,1)S(1)}, u32[]{:S(2)}, u32[]{:S(2)}) %collective-permute-start.24) | collective-permute-done | bytes 786464 | tf_op jit(solution)/shard_map/ppermute | solution.py:286
  127.2 1.5 collective-permute-done.25.refs_1_
  128.7 1.5 collective-permute-start.35
  130.2 4.1 %collective-permute-start.31 = (bf16[128,3072]{1,0:T(8,128)(2,1)}, bf16[128,3072]{1,0:T(8,128)(2,1)S(1)}, u32[]{:S(2)}, u32[]{:S(2)}) collective-permute-start(bf16[128,3072]{1,0:T(8,128)(2,1)} %get-tuple-element.87), channel_id=1, source_target_pairs={{0,24},{4,28},{24,0},{28,4},{1,25},{5,29},{25,1},{29,5},{2,26},{6,... | collective-permute-start | bytes 2359304 | tf_op jit(solution)/shard_map/ppermute | solution.py:290
  134.3 1.1 collective-permute-start.32
  136.2 1.2 constant_dynamic-update-slice_fusion.8
  137.6 13.5 %collective-permute-done.31.refs_0_ = bf16[128,3072]{1,0:T(8,128)(2,1)S(1)} collective-permute-done((bf16[128,3072]{1,0:T(8,128)(2,1)}, bf16[128,3072]{1,0:T(8,128)(2,1)S(1)}, u32[]{:S(2)}, u32[]{:S(2)}) %collective-permute-start.31) | collective-permute-done | bytes 786464 | tf_op jit(solution)/shard_map/ppermute | solution.py:290
  151.1 1.1 constant_dynamic-update-slice_fusion.4
  152.2 1.8 collective-permute-start.33
  154.6 1.8 shard_map.121
  156.4 1.2 collective-permute-start.36
  157.6 1.4 collective-permute-start.37
  158.9 1.9 collective-permute-start.38
  160.8 14.7 %collective-permute-done.36.refs_3_ = bf16[512,128]{1,0:T(8,128)(2,1)S(1)} collective-permute-done((bf16[512,128]{1,0:T(8,128)(2,1)}, bf16[512,128]{1,0:T(8,128)(2,1)S(1)}, u32[]{:S(2)}, u32[]{:S(2)}) %collective-permute-start.36) | collective-permute-done | bytes 131104 | tf_op jit(solution)/shard_map/ppermute | solution.py:286
  175.5 2.3 %collective-permute-done.38.refs_5_ = bf16[512,128]{1,0:T(8,128)(2,1)} collective-permute-done((bf16[512,128]{1,0:T(8,128)(2,1)}, bf16[512,128]{1,0:T(8,128)(2,1)}, u32[]{:S(2)}, u32[]{:S(2)}) %collective-permute-start.38) | collective-permute-done | bytes 131104 | tf_op jit(solution)/shard_map/ppermute | solution.py:286
  178.7 1.6 collective-permute-start.39
  182.9 3.4 %collective-permute-done.39.refs_6_ = bf16[4,256,128]{2,1,0:T(8,128)(2,1)S(1)} collective-permute-done((bf16[4,256,128]{2,1,0:T(8,128)(2,1)S(1)}, bf16[4,256,128]{2,1,0:T(8,128)(2,1)S(1)}, u32[]{:S(2)}, u32[]{:S(2)}) %collective-permute-start.39) | collective-permute-done | bytes 262176 | tf_op jit(solution)/shard_map/ppermute | solution.py:286
  186.3 4.0 %shard_map.123 = (bf16[256,1024]{1,0:T(8,128)(2,1)}, bf16[256,1024]{1,0:T(8,128)(2,1)}) custom-call(s32[3]{0:T(128)S(1)} %pad_add_fusion.spot, bf16[256,1024]{1,0:T(8,128)(2,1)S(1)} %copy-done.4, bf16[256,1024]{1,0:T(8,128)(2,1)S(1)} %copy-done.6, bf16[512,128]{1,0:T(8,128)(2,1)S(1)} %get-tuple-element.97.refs_2_, ...), custom_call_target="tpu_custom_call" | custom-call | bytes 4194304 | tf_op jit(solution)/shard_map/pallas_call | solution.py:102
  (109 shorter events, 13.2 us)
Async XLA Ops:
  0.6 1.4 copy-start
  0.6 66.0 %copy-start.1 = (f32[128,3072]{1,0:T(8,128)S(1)}, f32[128,3072]{1,0:T(8,128)}, u32[]{:S(2)}) copy-start(f32[128,3072]{1,0:T(8,128)} %refs_5_.1) | copy-start | bytes 4718596
  2.1 12.3 %collective-permute-start = (bf16[256,768]{1,0:T(8,128)(2,1)S(1)}, bf16[256,768]{1,0:T(8,128)(2,1)}, u32[]{:S(2)}, u32[]{:S(2)}) collective-permute-start(bf16[256,768]{1,0:T(8,128)(2,1)S(1)} %constant_dynamic-slice_fusion.refs_4_), channel_id=1, source_target_pairs={{0,8},{4,12},{8,0},{12,4},{16,24},{20,28},{24,16},{28,20},{1,9},{5... | collective-permute-start | bytes 1179656 | tf_op jit(solution)/shard_map/ppermute | solution.py:286
  5.2 10.7 %collective-permute-start.1 = (bf16[256,768]{1,0:T(8,128)(2,1)S(1)}, bf16[256,768]{1,0:T(8,128)(2,1)}, u32[]{:S(2)}, u32[]{:S(2)}) collective-permute-start(bf16[256,768]{1,0:T(8,128)(2,1)S(1)} %constant_dynamic-slice_fusion.refs_4_), channel_id=1, source_target_pairs={{0,4},{4,0},{8,12},{12,8},{16,20},{20,16},{24,28},{28,24},{1,5},{5... | collective-permute-start | bytes 1179656 | tf_op jit(solution)/shard_map/ppermute | solution.py:286
  6.7 9.2 %collective-permute-start.2 = (bf16[256,768]{1,0:T(8,128)(2,1)S(1)}, bf16[256,768]{1,0:T(8,128)(2,1)}, u32[]{:S(2)}, u32[]{:S(2)}) collective-permute-start(bf16[256,768]{1,0:T(8,128)(2,1)S(1)} %constant_dynamic-slice_fusion.refs_4_), channel_id=1, source_target_pairs={{8,16},{12,20},{16,8},{20,12},{9,17},{13,21},{17,9},{21,13},{10,18... | collective-permute-start | bytes 1179656 | tf_op jit(solution)/shard_map/ppermute | solution.py:290
  8.2 1.0 copy-start.3
  9.2 1.0 copy-start.5
  12.2 3.6 %copy-start.13 = (bf16[4,128,256]{2,1,0:T(8,128)(2,1)}, bf16[4,128,256]{2,1,0:T(8,128)(2,1)S(1)}, u32[]{:S(2)}) copy-start(bf16[4,128,256]{2,1,0:T(8,128)(2,1)S(1)} %get-tuple-element.65.refs_0_) | copy-start | bytes 786436
  15.9 19.9 %collective-permute-start.3 = (bf16[256,768]{1,0:T(8,128)(2,1)S(1)}, bf16[256,768]{1,0:T(8,128)(2,1)}, u32[]{:S(2)}, u32[]{:S(2)}) collective-permute-start(bf16[256,768]{1,0:T(8,128)(2,1)S(1)} %get-tuple-element.60.refs_4_.refs_0_), channel_id=1, source_target_pairs={{0,24},{4,28},{24,0},{28,4},{1,25},{5,29},{25,1},{29,5},{2,26},{6,... | collective-permute-start | bytes 1179656 | tf_op jit(solution)/shard_map/ppermute | solution.py:290
  20.2 15.6 %collective-permute-start.5 = (bf16[256,768]{1,0:T(8,128)(2,1)}, bf16[256,768]{1,0:T(8,128)(2,1)}, u32[]{:S(2)}, u32[]{:S(2)}) collective-permute-start(bf16[256,768]{1,0:T(8,128)(2,1)} %get-tuple-element.62.refs_6_.refs_2_), channel_id=1, source_target_pairs={{0,4},{4,0},{8,12},{12,8},{16,20},{20,16},{24,28},{28,24},{1,5},{5... | collective-permute-start | bytes 1179656 | tf_op jit(solution)/shard_map/ppermute | solution.py:286
  21.8 14.0 %collective-permute-start.4 = (bf16[4,128,256]{2,1,0:T(8,128)(2,1)}, bf16[4,128,256]{2,1,0:T(8,128)(2,1)}, u32[]{:S(2)}, u32[]{:S(2)}) collective-permute-start(bf16[4,128,256]{2,1,0:T(8,128)(2,1)} %get-tuple-element.61), channel_id=1, source_target_pairs={{0,4},{4,0},{8,12},{12,8},{16,20},{20,16},{24,28},{28,24},{1,5},{5... | collective-permute-start | bytes 786440 | tf_op jit(solution)/shard_map/ppermute | solution.py:286
  36.8 29.1 %copy-start.22 = (bf16[256,768]{1,0:T(8,128)(2,1)}, bf16[256,768]{1,0:T(8,128)(2,1)S(1)}, u32[]{:S(2)}) copy-start(bf16[256,768]{1,0:T(8,128)(2,1)S(1)} %broadcast_select_fusion.1.refs_11_.refs_7_) | copy-start | bytes 1179652
  36.9 17.1 %collective-permute-start.6 = (bf16[256,768]{1,0:T(8,128)(2,1)S(1)}, bf16[256,768]{1,0:T(8,128)(2,1)S(1)}, u32[]{:S(2)}, u32[]{:S(2)}) collective-permute-start(bf16[256,768]{1,0:T(8,128)(2,1)S(1)} %broadcast_select_fusion.1.refs_11_.refs_7_), channel_id=1, source_target_pairs={{0,8},{4,12},{8,0},{12,4},{16,24},{20,28},{24,16},{28,20},{1,9},{5... | collective-permute-start | bytes 1179656 | tf_op jit(solution)/shard_map/ppermute | solution.py:286
  38.5 15.5 %collective-permute-start.7 = (bf16[256,768]{1,0:T(8,128)(2,1)S(1)}, bf16[256,768]{1,0:T(8,128)(2,1)S(1)}, u32[]{:S(2)}, u32[]{:S(2)}) collective-permute-start(bf16[256,768]{1,0:T(8,128)(2,1)S(1)} %broadcast_select_fusion.1.refs_11_.refs_7_), channel_id=1, source_target_pairs={{0,4},{4,0},{8,12},{12,8},{16,20},{20,16},{24,28},{28,24},{1,5},{5... | collective-permute-start | bytes 1179656 | tf_op jit(solution)/shard_map/ppermute | solution.py:286
  39.0 0.9 copy-start.14
  42.5 10.5 %collective-permute-start.10 = (bf16[2,128,256]{2,1,0:T(8,128)(2,1)S(1)}, bf16[2,128,256]{2,1,0:T(8,128)(2,1)S(1)}, u32[]{:S(2)}, u32[]{:S(2)}) collective-permute-start(bf16[2,128,256]{2,1,0:T(8,128)(2,1)S(1)} %get-tuple-element.70), channel_id=1, source_target_pairs={{0,24},{4,28},{8,16},{12,20},{16,8},{20,12},{24,0},{28,4},{1,25},{... | collective-permute-start | bytes 393224 | tf_op jit(solution)/shard_map/ppermute | solution.py:286
  44.9 9.1 %collective-permute-start.8 = (bf16[2,128,256]{2,1,0:T(8,128)(2,1)S(1)}, bf16[2,128,256]{2,1,0:T(8,128)(2,1)S(1)}, u32[]{:S(2)}, u32[]{:S(2)}) collective-permute-start(bf16[2,128,256]{2,1,0:T(8,128)(2,1)S(1)} %get-tuple-element.68), channel_id=1, source_target_pairs={{0,8},{4,12},{8,0},{12,4},{16,24},{20,28},{24,16},{28,20},{1,9},{5... | collective-permute-start | bytes 393224 | tf_op jit(solution)/shard_map/ppermute | solution.py:286
  44.9 9.1 %collective-permute-start.9 = (bf16[2,128,256]{2,1,0:T(8,128)(2,1)S(1)}, bf16[2,128,256]{2,1,0:T(8,128)(2,1)S(1)}, u32[]{:S(2)}, u32[]{:S(2)}) collective-permute-start(bf16[2,128,256]{2,1,0:T(8,128)(2,1)S(1)} %get-tuple-element.69), channel_id=1, source_target_pairs={{0,16},{4,20},{8,24},{12,28},{16,0},{20,4},{24,8},{28,12},{1,17},{... | collective-permute-start | bytes 393224 | tf_op jit(solution)/shard_map/ppermute | solution.py:286
  54.0 2.5 %copy-start.9 = (bf16[256,768]{1,0:T(8,128)(2,1)}, bf16[256,768]{1,0:T(8,128)(2,1)S(1)}, u32[]{:S(2)}) copy-start(bf16[256,768]{1,0:T(8,128)(2,1)S(1)} %get-tuple-element.75.refs_8_.refs_4_) | copy-start | bytes 1179652
  54.0 4.1 %copy-start.10 = (bf16[256,768]{1,0:T(8,128)(2,1)}, bf16[256,768]{1,0:T(8,128)(2,1)S(1)}, u32[]{:S(2)}) copy-start(bf16[256,768]{1,0:T(8,128)(2,1)S(1)} %get-tuple-element.76.refs_12_.refs_8_) | copy-start | bytes 1179652
  55.0 11.0 %collective-permute-start.12 = (bf16[4,2,128,256]{3,2,1,0:T(8,128)(2,1)}, bf16[4,2,128,256]{3,2,1,0:T(8,128)(2,1)}, u32[]{:S(2)}, u32[]{:S(2)}) collective-permute-start(bf16[4,2,128,256]{3,2,1,0:T(8,128)(2,1)} %pad_maximum_fusion.refs_0_), channel_id=1, source_target_pairs={{0,2},{1,3},{2,0},{3,1},{4,6},{5,7},{6,4},{7,5},{8,10},{9,11},{10,... | collective-permute-start | bytes 1572872 | tf_op jit(solution)/shard_map/ppermute | solution.py:293
  56.5 5.7 %collective-permute-start.13 = (bf16[128,768]{1,0:T(8,128)(2,1)S(1)}, bf16[128,768]{1,0:T(8,128)(2,1)S(1)}, u32[]{:S(2)}, u32[]{:S(2)}) collective-permute-start(bf16[128,768]{1,0:T(8,128)(2,1)S(1)} %slice.24), channel_id=1, source_target_pairs={{0,4},{4,0},{8,12},{12,8},{16,20},{20,16},{24,28},{28,24},{1,5},{5... | collective-permute-start | bytes 589832 | tf_op jit(solution)/shard_map/ppermute | solution.py:286
  58.1 5.7 %collective-permute-start.14 = (bf16[128,768]{1,0:T(8,128)(2,1)S(1)}, bf16[128,768]{1,0:T(8,128)(2,1)S(1)}, u32[]{:S(2)}, u32[]{:S(2)}) collective-permute-start(bf16[128,768]{1,0:T(8,128)(2,1)S(1)} %slice.25), channel_id=1, source_target_pairs={{0,8},{4,12},{8,0},{12,4},{16,24},{20,28},{24,16},{28,20},{1,9},{5... | collective-permute-start | bytes 589832 | tf_op jit(solution)/shard_map/ppermute | solution.py:286
  59.5 9.4 %collective-permute-start.11 = (bf16[4,2,128,256]{3,2,1,0:T(8,128)(2,1)}, bf16[4,2,128,256]{3,2,1,0:T(8,128)(2,1)}, u32[]{:S(2)}, u32[]{:S(2)}) collective-permute-start(bf16[4,2,128,256]{3,2,1,0:T(8,128)(2,1)} %pad_maximum_fusion.refs_0_), channel_id=1, source_target_pairs={{0,1},{1,0},{2,3},{3,2},{4,5},{5,4},{6,7},{7,6},{8,9},{9,8},{10,11... | collective-permute-start | bytes 1572872 | tf_op jit(solution)/shard_map/ppermute | solution.py:293
  63.8 2.2 %copy-start.18 = (bf16[128,768]{1,0:T(8,128)(2,1)}, bf16[128,768]{1,0:T(8,128)(2,1)S(1)}, u32[]{:S(2)}) copy-start(bf16[128,768]{1,0:T(8,128)(2,1)S(1)} %collective-permute-done.14.refs_2_.refs_10_.refs_6_) | copy-start | bytes 589828
  66.7 2.3 %collective-permute-start.15 = (bf16[4,2,128,256]{3,2,1,0:T(8,128)(2,1)}, bf16[4,2,128,256]{3,2,1,0:T(8,128)(2,1)}, u32[]{:S(2)}, u32[]{:S(2)}) collective-permute-start(bf16[4,2,128,256]{3,2,1,0:T(8,128)(2,1)} %shard_map.114.refs_2_), channel_id=1, source_target_pairs={{0,1},{1,0},{2,3},{3,2},{4,5},{5,4},{6,7},{7,6},{8,9},{9,8},{10,11... | collective-permute-start | bytes 1572872 | tf_op jit(solution)/shard_map/ppermute | solution.py:293
  66.7 11.5 %copy-start.17 = (bf16[128,768]{1,0:T(8,128)(2,1)S(1)}, bf16[128,768]{1,0:T(8,128)(2,1)}, u32[]{:S(2)}) copy-start(bf16[128,768]{1,0:T(8,128)(2,1)} %copy-done.15) | copy-start | bytes 589828
  66.7 11.5 %copy-start.20 = (bf16[128,768]{1,0:T(8,128)(2,1)S(1)}, bf16[128,768]{1,0:T(8,128)(2,1)}, u32[]{:S(2)}) copy-start(bf16[128,768]{1,0:T(8,128)(2,1)} %copy-done.18) | copy-start | bytes 589828
  66.8 36.4 %copy-start.7 = (f32[128,3072]{1,0:T(8,128)S(1)}, f32[128,3072]{1,0:T(8,128)}, u32[]{:S(2)}) copy-start(f32[128,3072]{1,0:T(8,128)} %refs_6_.1) | copy-start | bytes 4718596
  66.8 36.4 %copy-start.8 = (f32[128,3072]{1,0:T(8,128)S(1)}, f32[128,3072]{1,0:T(8,128)}, u32[]{:S(2)}) copy-start(f32[128,3072]{1,0:T(8,128)} %refs_7_.1) | copy-start | bytes 4718596
  66.8 11.4 %collective-permute-start.27 = (bf16[128,768]{1,0:T(8,128)(2,1)S(1)}, bf16[128,768]{1,0:T(8,128)(2,1)S(1)}, u32[]{:S(2)}, u32[]{:S(2)}) collective-permute-start(bf16[128,768]{1,0:T(8,128)(2,1)S(1)} %get-tuple-element.115), channel_id=1, source_target_pairs={{0,1},{1,0},{2,3},{3,2},{4,5},{5,4},{6,7},{7,6},{8,9},{9,8},{10,11... | collective-permute-start | bytes 589832 | tf_op jit(solution)/shard_map/ppermute | solution.py:293
  67.4 10.8 %collective-permute-start.28 = (bf16[128,768]{1,0:T(8,128)(2,1)S(1)}, bf16[128,768]{1,0:T(8,128)(2,1)S(1)}, u32[]{:S(2)}, u32[]{:S(2)}) collective-permute-start(bf16[128,768]{1,0:T(8,128)(2,1)S(1)} %get-tuple-element.117), channel_id=1, source_target_pairs={{0,2},{1,3},{2,0},{3,1},{4,6},{5,7},{6,4},{7,5},{8,10},{9,11},{10,... | collective-permute-start | bytes 589832 | tf_op jit(solution)/shard_map/ppermute | solution.py:293
  68.9 9.3 %collective-permute-start.29 = (bf16[128,768]{1,0:T(8,128)(2,1)S(1)}, bf16[128,768]{1,0:T(8,128)(2,1)S(1)}, u32[]{:S(2)}, u32[]{:S(2)}) collective-permute-start(bf16[128,768]{1,0:T(8,128)(2,1)S(1)} %get-tuple-element.114), channel_id=1, source_target_pairs={{0,3},{1,2},{2,1},{3,0},{4,7},{5,6},{6,5},{7,4},{8,11},{9,10},{10,... | collective-permute-start | bytes 589832 | tf_op jit(solution)/shard_map/ppermute | solution.py:293
  68.9 0.9 copy-start.16
  69.9 0.9 copy-start.19
  77.5 0.7 copy-start.11
  78.2 25.0 %copy-start.12 = (f32[128,768]{1,0:T(8,128)S(1)}, f32[128,768]{1,0:T(8,128)}, u32[]{:S(2)}) copy-start(f32[128,768]{1,0:T(8,128)} %copy-done.11) | copy-start | bytes 1179652
  83.8 29.5 %collective-permute-start.30 = (f32[2,2048,128]{2,1,0:T(8,128)}, f32[2,2048,128]{2,1,0:T(8,128)}, u32[]{:S(2)}, u32[]{:S(2)}) collective-permute-start(f32[2,2048,128]{2,1,0:T(8,128)} %get-tuple-element.85), channel_id=1, source_target_pairs={{0,1},{1,0},{2,3},{3,2},{4,5},{5,4},{6,7},{7,6},{8,9},{9,8},{10,11... | collective-permute-start | bytes 6291464 | tf_op jit(solution)/shard_map/ppermute | solution.py:293
  84.4 18.8 %collective-permute-start.21 = (bf16[128,768]{1,0:T(8,128)(2,1)S(1)}, bf16[128,768]{1,0:T(8,128)(2,1)S(1)}, u32[]{:S(2)}, u32[]{:S(2)}) collective-permute-start(bf16[128,768]{1,0:T(8,128)(2,1)S(1)} %get-tuple-element.80), channel_id=1, source_target_pairs={{0,1},{1,0},{2,3},{3,2},{4,5},{5,4},{6,7},{7,6},{8,9},{9,8},{10,11... | collective-permute-start | bytes 589832 | tf_op jit(solution)/shard_map/ppermute | solution.py:293
  84.5 18.7 %collective-permute-start.22 = (bf16[128,768]{1,0:T(8,128)(2,1)S(1)}, bf16[128,768]{1,0:T(8,128)(2,1)S(1)}, u32[]{:S(2)}, u32[]{:S(2)}) collective-permute-start(bf16[128,768]{1,0:T(8,128)(2,1)S(1)} %get-tuple-element.81), channel_id=1, source_target_pairs={{0,2},{1,3},{2,0},{3,1},{4,6},{5,7},{6,4},{7,5},{8,10},{9,11},{10,... | collective-permute-start | bytes 589832 | tf_op jit(solution)/shard_map/ppermute | solution.py:293
  86.0 17.2 %collective-permute-start.23 = (bf16[128,768]{1,0:T(8,128)(2,1)S(1)}, bf16[128,768]{1,0:T(8,128)(2,1)S(1)}, u32[]{:S(2)}, u32[]{:S(2)}) collective-permute-start(bf16[128,768]{1,0:T(8,128)(2,1)S(1)} %get-tuple-element.82), channel_id=1, source_target_pairs={{0,3},{1,2},{2,1},{3,0},{4,7},{5,6},{6,5},{7,4},{8,11},{9,10},{10,... | collective-permute-start | bytes 589832 | tf_op jit(solution)/shard_map/ppermute | solution.py:293
  86.3 4.0 %collective-permute-start.16 = (f32[8,128]{1,0:T(8,128)S(1)}, f32[8,128]{1,0:T(8,128)S(1)}, u32[]{:S(2)}, u32[]{:S(2)}) collective-permute-start(f32[8,128]{1,0:T(8,128)S(1)} %get-tuple-element.78), channel_id=1, source_target_pairs={{0,4},{4,0},{8,12},{12,8},{16,20},{20,16},{24,28},{28,24},{1,5},{5... | collective-permute-start | bytes 12296 | tf_op jit(solution)/shard_map/ppermute | solution.py:286
  90.3 3.6 %collective-permute-start.17 = (f32[8,128]{1,0:T(8,128)S(1)}, f32[8,128]{1,0:T(8,128)S(1)}, u32[]{:S(2)}, u32[]{:S(2)}) collective-permute-start(f32[8,128]{1,0:T(8,128)S(1)} %add.80), channel_id=1, source_target_pairs={{0,8},{4,12},{8,0},{12,4},{16,24},{20,28},{24,16},{28,20},{1,9},{5... | collective-permute-start | bytes 12296 | tf_op jit(solution)/shard_map/ppermute | solution.py:286
  93.9 4.5 %collective-permute-start.18 = (f32[8,128]{1,0:T(8,128)S(1)}, f32[8,128]{1,0:T(8,128)S(1)}, u32[]{:S(2)}, u32[]{:S(2)}) collective-permute-start(f32[8,128]{1,0:T(8,128)S(1)} %add.81), channel_id=1, source_target_pairs={{0,16},{4,20},{8,24},{12,28},{16,0},{20,4},{24,8},{28,12},{1,17},{... | collective-permute-start | bytes 12296 | tf_op jit(solution)/shard_map/ppermute | solution.py:286
  98.4 1.2 collective-permute-start.19
  99.6 3.6 %collective-permute-start.20 = (f32[8,128]{1,0:T(8,128)S(1)}, f32[8,128]{1,0:T(8,128)S(1)}, u32[]{:S(2)}, u32[]{:S(2)}) collective-permute-start(f32[8,128]{1,0:T(8,128)S(1)} %add.83), channel_id=1, source_target_pairs={{0,2},{1,3},{2,0},{3,1},{4,6},{5,7},{6,4},{7,5},{8,10},{9,11},{10,... | collective-permute-start | bytes 12296 | tf_op jit(solution)/shard_map/ppermute | solution.py:293
  108.4 18.8 %collective-permute-start.24 = (bf16[128,3072]{1,0:T(8,128)(2,1)}, bf16[128,3072]{1,0:T(8,128)(2,1)S(1)}, u32[]{:S(2)}, u32[]{:S(2)}) collective-permute-start(bf16[128,3072]{1,0:T(8,128)(2,1)} %get-tuple-element.83.refs_4_), channel_id=1, source_target_pairs={{0,8},{4,12},{8,0},{12,4},{16,24},{20,28},{24,16},{28,20},{1,9},{5... | collective-permute-start | bytes 2359304 | tf_op jit(solution)/shard_map/ppermute | solution.py:286
  110.3 18.4 %collective-permute-start.25 = (bf16[128,3072]{1,0:T(8,128)(2,1)}, bf16[128,3072]{1,0:T(8,128)(2,1)S(1)}, u32[]{:S(2)}, u32[]{:S(2)}) collective-permute-start(bf16[128,3072]{1,0:T(8,128)(2,1)} %get-tuple-element.83.refs_4_), channel_id=1, source_target_pairs={{0,4},{4,0},{8,12},{12,8},{16,20},{20,16},{24,28},{28,24},{1,5},{5... | collective-permute-start | bytes 2359304 | tf_op jit(solution)/shard_map/ppermute | solution.py:286
  111.7 16.9 %collective-permute-start.26 = (bf16[128,3072]{1,0:T(8,128)(2,1)}, bf16[128,3072]{1,0:T(8,128)(2,1)}, u32[]{:S(2)}, u32[]{:S(2)}) collective-permute-start(bf16[128,3072]{1,0:T(8,128)(2,1)} %get-tuple-element.83.refs_4_), channel_id=1, source_target_pairs={{8,16},{12,20},{16,8},{20,12},{9,17},{13,21},{17,9},{21,13},{10,18... | collective-permute-start | bytes 2359304 | tf_op jit(solution)/shard_map/ppermute | solution.py:290
  113.3 1.6 copy-start.2
  128.7 25.9 %collective-permute-start.35 = (f32[2048,128]{1,0:T(8,128)S(1)}, f32[2048,128]{1,0:T(8,128)S(1)}, u32[]{:S(2)}, u32[]{:S(2)}) collective-permute-start(f32[2048,128]{1,0:T(8,128)S(1)} %get-tuple-element.92), channel_id=1, source_target_pairs={{0,2},{1,3},{2,0},{3,1},{4,6},{5,7},{6,4},{7,5},{8,10},{9,11},{10,... | collective-permute-start | bytes 3145736 | tf_op jit(solution)/shard_map/ppermute | solution.py:293
  130.2 20.8 %collective-permute-start.31 = (bf16[128,3072]{1,0:T(8,128)(2,1)}, bf16[128,3072]{1,0:T(8,128)(2,1)S(1)}, u32[]{:S(2)}, u32[]{:S(2)}) collective-permute-start(bf16[128,3072]{1,0:T(8,128)(2,1)} %get-tuple-element.87), channel_id=1, source_target_pairs={{0,24},{4,28},{24,0},{28,4},{1,25},{5,29},{25,1},{29,5},{2,26},{6,... | collective-permute-start | bytes 2359304 | tf_op jit(solution)/shard_map/ppermute | solution.py:290
  134.3 16.7 %collective-permute-start.32 = (bf16[128,3072]{1,0:T(8,128)(2,1)S(1)}, bf16[128,3072]{1,0:T(8,128)(2,1)S(1)}, u32[]{:S(2)}, u32[]{:S(2)}) collective-permute-start(bf16[128,3072]{1,0:T(8,128)(2,1)S(1)} %get-tuple-element.88), channel_id=1, source_target_pairs={{0,4},{4,0},{8,12},{12,8},{16,20},{20,16},{24,28},{28,24},{1,5},{5... | collective-permute-start | bytes 2359304 | tf_op jit(solution)/shard_map/ppermute | solution.py:286
  152.2 5.3 %copy-start.21 = (bf16[1024,3072]{1,0:T(8,128)(2,1)}, bf16[1024,3072]{1,0:T(8,128)(2,1)S(1)}, u32[]{:S(2)}) copy-start(bf16[1024,3072]{1,0:T(8,128)(2,1)S(1)} %get-tuple-element.112) | copy-start | bytes 18874372
  152.2 25.5 %collective-permute-start.33 = (bf16[128,3072]{1,0:T(8,128)(2,1)}, bf16[128,3072]{1,0:T(8,128)(2,1)S(1)}, u32[]{:S(2)}, u32[]{:S(2)}) collective-permute-start(bf16[128,3072]{1,0:T(8,128)(2,1)} %get-tuple-element.113), channel_id=1, source_target_pairs={{0,8},{4,12},{8,0},{12,4},{16,24},{20,28},{24,16},{28,20},{1,9},{5... | collective-permute-start | bytes 2359304 | tf_op jit(solution)/shard_map/ppermute | solution.py:286
  154.0 23.8 %collective-permute-start.34 = (bf16[128,3072]{1,0:T(8,128)(2,1)}, bf16[128,3072]{1,0:T(8,128)(2,1)S(1)}, u32[]{:S(2)}, u32[]{:S(2)}) collective-permute-start(bf16[128,3072]{1,0:T(8,128)(2,1)} %get-tuple-element.113), channel_id=1, source_target_pairs={{0,4},{4,0},{8,12},{12,8},{16,20},{20,16},{24,28},{28,24},{1,5},{5... | collective-permute-start | bytes 2359304 | tf_op jit(solution)/shard_map/ppermute | solution.py:286
  156.4 19.1 %collective-permute-start.36 = (bf16[512,128]{1,0:T(8,128)(2,1)}, bf16[512,128]{1,0:T(8,128)(2,1)S(1)}, u32[]{:S(2)}, u32[]{:S(2)}) collective-permute-start(bf16[512,128]{1,0:T(8,128)(2,1)} %get-tuple-element.94), channel_id=1, source_target_pairs={{0,8},{4,12},{8,0},{12,4},{16,24},{20,28},{24,16},{28,20},{1,9},{5... | collective-permute-start | bytes 393224 | tf_op jit(solution)/shard_map/ppermute | solution.py:286
  157.6 17.9 %collective-permute-start.37 = (bf16[512,128]{1,0:T(8,128)(2,1)}, bf16[512,128]{1,0:T(8,128)(2,1)S(1)}, u32[]{:S(2)}, u32[]{:S(2)}) collective-permute-start(bf16[512,128]{1,0:T(8,128)(2,1)} %get-tuple-element.95), channel_id=1, source_target_pairs={{0,16},{4,20},{8,24},{12,28},{16,0},{20,4},{24,8},{28,12},{1,17},{... | collective-permute-start | bytes 393224 | tf_op jit(solution)/shard_map/ppermute | solution.py:286
  158.9 18.8 %collective-permute-start.38 = (bf16[512,128]{1,0:T(8,128)(2,1)}, bf16[512,128]{1,0:T(8,128)(2,1)}, u32[]{:S(2)}, u32[]{:S(2)}) collective-permute-start(bf16[512,128]{1,0:T(8,128)(2,1)} %get-tuple-element.96), channel_id=1, source_target_pairs={{0,24},{4,28},{8,16},{12,20},{16,8},{20,12},{24,0},{28,4},{1,25},{... | collective-permute-start | bytes 393224 | tf_op jit(solution)/shard_map/ppermute | solution.py:286
  160.8 25.5 %copy-start.4 = (bf16[256,1024]{1,0:T(8,128)(2,1)S(1)}, bf16[256,1024]{1,0:T(8,128)(2,1)}, u32[]{:S(2)}) copy-start(bf16[256,1024]{1,0:T(8,128)(2,1)} %refs_0_.3) | copy-start | bytes 1572868
  160.8 25.5 %copy-start.6 = (bf16[256,1024]{1,0:T(8,128)(2,1)S(1)}, bf16[256,1024]{1,0:T(8,128)(2,1)}, u32[]{:S(2)}) copy-start(bf16[256,1024]{1,0:T(8,128)(2,1)} %refs_1_.3) | copy-start | bytes 1572868
  178.7 7.6 %collective-permute-start.39 = (bf16[4,256,128]{2,1,0:T(8,128)(2,1)S(1)}, bf16[4,256,128]{2,1,0:T(8,128)(2,1)S(1)}, u32[]{:S(2)}, u32[]{:S(2)}) collective-permute-start(bf16[4,256,128]{2,1,0:T(8,128)(2,1)S(1)} %pad_maximum_fusion.1.refs_2_), channel_id=1, source_target_pairs={{0,4},{4,0},{8,12},{12,8},{16,20},{20,16},{24,28},{28,24},{1,5},{5... | collective-permute-start | bytes 786440 | tf_op jit(solution)/shard_map/ppermute | solution.py:286
  180.3 10.2 %collective-permute-start.40 = (bf16[64,3072]{1,0:T(8,128)(2,1)S(1)}, bf16[64,3072]{1,0:T(8,128)(2,1)S(1)}, u32[]{:S(2)}, u32[]{:S(2)}) collective-permute-start(bf16[64,3072]{1,0:T(8,128)(2,1)S(1)} %slice.30), channel_id=1, source_target_pairs={{0,4},{4,0},{8,12},{12,8},{16,20},{20,16},{24,28},{28,24},{1,5},{5... | collective-permute-start | bytes 1179656 | tf_op jit(solution)/shard_map/ppermute | solution.py:286
  180.9 10.4 %collective-permute-start.41 = (bf16[64,3072]{1,0:T(8,128)(2,1)S(1)}, bf16[64,3072]{1,0:T(8,128)(2,1)S(1)}, u32[]{:S(2)}, u32[]{:S(2)}) collective-permute-start(bf16[64,3072]{1,0:T(8,128)(2,1)S(1)} %slice.31), channel_id=1, source_target_pairs={{0,8},{4,12},{8,0},{12,4},{16,24},{20,28},{24,16},{28,20},{1,9},{5... | collective-permute-start | bytes 1179656 | tf_op jit(solution)/shard_map/ppermute | solution.py:286
  (1 other events, 0.7 us)

commit v6 on v5

--- a/solution.py
+++ b/solution.py
@@ -400,7 +400,7 @@
     near, own_x, mid = across(own, 2), across(own, 1), line(own, MIDDLE)
     mine_sum = shaped((CELL * tokens, part), F32)
     mine, sent = call(add_body, (mine_sum,) * 2, (spot, keep, give), moved=6 << 20)
-    near, own_x, mid, sent, own = together(near, own_x, mid, sent, own)
+    near, own_x, mid, own = together(near, own_x, mid, own, after=(sent,))
     end, near_x, came = line(own, ROUND), across(near, 1), swap(sent, 2)
     end, near_x = together(end, near_x)
     last = jnp.where(ends, end, mid)

time: 193 us -> 192 us (level)
  no operation moved by 1% of the time
where the time goes in v6:
time: 192 us; the launch traced here: 191 us
  waiting for transfers between devices  83.4 us (43%)
  starting transfers between devices  57.2 us (30%)
  Pallas kernels  30.5 us (16%)
  local copies, waits for them, and re-layouts  16 us (8%)
  other arithmetic  3.27 us (2%)
    ppermute x25, waiting for transfers between devices, across(): return lax.ppermute(value, 'dp', [(i, i ^ m) for i in range(n)])  64.2 us
    ppermute x25, starting transfers between devices, across(): return lax.ppermute(value, 'dp', [(i, i ^ m) for i in range(n)])  36.5 us
    pallas_call x8, Pallas kernels, call(): pl.pallas_call(kernel, out_shape=tuple(outs), in_specs=[SMEM] + specs + [...  30.5 us
    ppermute x4, waiting for transfers between devices, line(): lax.ppermute(value, 'dp', [(i, i - i % CELL + b * 2 + i % 2) for i, b in...  13.7 us
    ppermute x4, starting transfers between devices, line(): lax.ppermute(value, 'dp', [(i, i - i % CELL + b * 2 + i % 2) for i, b in...  11.4 us
    unnamed x46, local copies, waits for them, and re-layouts  9.35 us
    ppermute x13, starting transfers between devices, swap(): return lax.ppermute(value, 'tensor', [(i, i ^ m) for i in range(4)])  9.26 us
    ppermute x13, waiting for transfers between devices, swap(): return lax.ppermute(value, 'tensor', [(i, i ^ m) for i in range(4)])  5.43 us
  transfers between devices with their start and end apart: 42, of which 20 were waited for; matrix products, arithmetic and copies ran while one was open for 3% of the time, Pallas kernels for 13%

profile of v6, /device:TPU:0, one launch (start us, length us, event | category | flops | bytes accessed | tf_op | source)
XLA Modules:
  0.0 191.4 jit_solution(3151057131493404372)
XLA Ops:
  0.7 1.4 copy-done
  2.1 3.1 %collective-permute-start = (bf16[256,768]{1,0:T(8,128)(2,1)S(1)}, bf16[256,768]{1,0:T(8,128)(2,1)}, u32[]{:S(2)}, u32[]{:S(2)}) collective-permute-start(bf16[256,768]{1,0:T(8,128)(2,1)S(1)} %constant_dynamic-slice_fusion.refs_4_), channel_id=1, source_target_pairs={{0,8},{4,12},{8,0},{12,4},{16,24},{20,28},{24,16},{28,20},{1,9},{5... | collective-permute-start | bytes 1179656 | tf_op jit(solution)/shard_map/ppermute | solution.py:286
  5.2 1.5 collective-permute-start.1
  6.7 1.4 collective-permute-start.2
  8.2 1.0 copy-done.3
  9.2 1.0 copy-done.5
  10.3 2.0 %shard_map.109 = (bf16[4,128,256]{2,1,0:T(8,128)(2,1)S(1)}, bf16[4,128,256]{2,1,0:T(8,128)(2,1)}) custom-call(s32[3]{0:T(128)S(1)} %pad_add_fusion.spot, bf16[256,1024]{1,0:T(8,128)(2,1)S(1)} %copy-done.3, bf16[256,1024]{1,0:T(8,128)(2,1)S(1)} %copy-done.5), custom_call_target="tpu_custom_call" | custom-call | bytes 2097152 | tf_op jit(solution)/shard_map/pallas_call | solution.py:102
  12.3 2.1 %collective-permute-done.refs_0_ = bf16[256,768]{1,0:T(8,128)(2,1)} collective-permute-done((bf16[256,768]{1,0:T(8,128)(2,1)S(1)}, bf16[256,768]{1,0:T(8,128)(2,1)}, u32[]{:S(2)}, u32[]{:S(2)}) %collective-permute-start) | collective-permute-done | bytes 393248 | tf_op jit(solution)/shard_map/ppermute | solution.py:286
  14.4 1.5 collective-permute-done.1.refs_1_
  15.9 4.4 %collective-permute-start.3 = (bf16[256,768]{1,0:T(8,128)(2,1)S(1)}, bf16[256,768]{1,0:T(8,128)(2,1)}, u32[]{:S(2)}, u32[]{:S(2)}) collective-permute-start(bf16[256,768]{1,0:T(8,128)(2,1)S(1)} %get-tuple-element.59.refs_4_.refs_0_), channel_id=1, source_target_pairs={{0,24},{4,28},{24,0},{28,4},{1,25},{5,29},{25,1},{29,5},{2,26},{6,... | collective-permute-start | bytes 1179656 | tf_op jit(solution)/shard_map/ppermute | solution.py:290
  20.2 1.6 collective-permute-start.5
  22.3 13.5 %collective-permute-done.4.refs_1_ = bf16[4,128,256]{2,1,0:T(8,128)(2,1)} collective-permute-done((bf16[4,128,256]{2,1,0:T(8,128)(2,1)}, bf16[4,128,256]{2,1,0:T(8,128)(2,1)}, u32[]{:S(2)}, u32[]{:S(2)}) %collective-permute-start.4) | collective-permute-done | bytes 262176 | tf_op jit(solution)/shard_map/ppermute | solution.py:286
  35.8 1.0 broadcast_select_fusion.1.refs_11_.refs_7_
  36.9 1.7 collective-permute-start.6
  39.0 0.9 copy-done.14
  40.0 2.5 %shard_map.112 = (bf16[2,128,256]{2,1,0:T(8,128)(2,1)S(1)}, bf16[2,128,256]{2,1,0:T(8,128)(2,1)S(1)}, bf16[2,128,256]{2,1,0:T(8,128)(2,1)S(1)}, bf16[2,128,256]{2,1,0:T(8,128)(2,1)S(1)}) custom-call(s32[3]{0:T(128)S(1)} %pad_add_fusion.spot, bf16[4,128,256]{2,1,0:T(8,128)(2,1)S(1)} %copy-done.14, bf16[4,128,256]{2,1,0:T(8,128)(2,1)} %get-tuple-element.65.refs_1_), custom_call_target="tpu_custom_call" | custom-call | bytes 1048576 | tf_op jit(solution)/shard_map/pallas_call | solution.py:102
  42.5 2.4 %collective-permute-start.10 = (bf16[2,128,256]{2,1,0:T(8,128)(2,1)S(1)}, bf16[2,128,256]{2,1,0:T(8,128)(2,1)S(1)}, u32[]{:S(2)}, u32[]{:S(2)}) collective-permute-start(bf16[2,128,256]{2,1,0:T(8,128)(2,1)S(1)} %get-tuple-element.69), channel_id=1, source_target_pairs={{0,24},{4,28},{8,16},{12,20},{16,8},{20,12},{24,0},{28,4},{1,25},{... | collective-permute-start | bytes 393224 | tf_op jit(solution)/shard_map/ppermute | solution.py:286
  44.9 2.0 %collective-permute-start.9 = (bf16[2,128,256]{2,1,0:T(8,128)(2,1)S(1)}, bf16[2,128,256]{2,1,0:T(8,128)(2,1)S(1)}, u32[]{:S(2)}, u32[]{:S(2)}) collective-permute-start(bf16[2,128,256]{2,1,0:T(8,128)(2,1)S(1)} %get-tuple-element.68), channel_id=1, source_target_pairs={{0,16},{4,20},{8,24},{12,28},{16,0},{20,4},{24,8},{28,12},{1,17},{... | collective-permute-start | bytes 393224 | tf_op jit(solution)/shard_map/ppermute | solution.py:286
  47.0 6.0 %collective-permute-done.10.refs_5_ = bf16[2,128,256]{2,1,0:T(8,128)(2,1)S(1)} collective-permute-done((bf16[2,128,256]{2,1,0:T(8,128)(2,1)S(1)}, bf16[2,128,256]{2,1,0:T(8,128)(2,1)S(1)}, u32[]{:S(2)}, u32[]{:S(2)}) %collective-permute-start.10) | collective-permute-done | bytes 131104 | tf_op jit(solution)/shard_map/ppermute | solution.py:286
  53.0 1.0 collective-permute-done.8.refs_3_
  54.0 1.0 pad_maximum_fusion.refs_0_
  55.0 1.5 collective-permute-start.12
  56.5 1.6 collective-permute-start.13
  58.1 1.4 collective-permute-start.14
  59.5 2.8 %collective-permute-done.13.refs_1_.refs_9_.refs_5_ = bf16[128,768]{1,0:T(8,128)(2,1)S(1)} collective-permute-done((bf16[128,768]{1,0:T(8,128)(2,1)S(1)}, bf16[128,768]{1,0:T(8,128)(2,1)S(1)}, u32[]{:S(2)}, u32[]{:S(2)}) %collective-permute-start.13) | collective-permute-done | bytes 196640 | tf_op jit(solution)/shard_map/ppermute | solution.py:286
  62.3 1.6 collective-permute-done.14.refs_2_.refs_10_.refs_6_
  63.8 2.1 %collective-permute-done.12.refs_0_ = bf16[4,2,128,256]{3,2,1,0:T(8,128)(2,1)} collective-permute-done((bf16[4,2,128,256]{3,2,1,0:T(8,128)(2,1)}, bf16[4,2,128,256]{3,2,1,0:T(8,128)(2,1)}, u32[]{:S(2)}, u32[]{:S(2)}) %collective-permute-start.12) | collective-permute-done | bytes 524320 | tf_op jit(solution)/shard_map/ppermute | solution.py:293
  67.4 1.5 collective-permute-start.28
  70.8 6.7 %shard_map.115 = (f32[128,768]{1,0:T(8,128)S(1)}, bf16[128,768]{1,0:T(8,128)(2,1)S(1)}, bf16[128,768]{1,0:T(8,128)(2,1)S(1)}, bf16[128,768]{1,0:T(8,128)(2,1)S(1)}, f32[8,128]{1,0:T(8,128)S(1)}) custom-call(s32[3]{0:T(128)S(1)} %pad_add_fusion.spot, bf16[4,2,128,256]{3,2,1,0:T(8,128)(2,1)} %pad_maximum_fusion.refs_0_, ...), custom_call_target="tpu_custom_call" | custom-call | flops 1610612736 | bytes 8388608 | tf_op jit(solution)/shard_map/pallas_call | solution.py:102
  78.2 5.5 %shard_map.117 = (f32[2,2048,128]{2,1,0:T(8,128)}, f32[2,2048,128]{2,1,0:T(8,128)}) custom-call(s32[3]{0:T(128)S(1)} %pad_add_fusion.spot, bf16[256,768]{1,0:T(8,128)(2,1)S(1)} %get-tuple-element.59.refs_4_.refs_0_, bf16[256,768]{1,0:T(8,128)(2,1)} %get-tuple-element.76.refs_5_.refs_1_, bf16[256,768]{1,0:T(8,128)(2,1)} %get-tuple-element.61.refs_6_.refs_2_, ...), custom_call_target="tpu_custom_call" | custom-call | flops 1610612736 | bytes 10485760 | tf_op jit(solution)/shard_map/pallas_call | solution.py:102
  84.5 1.5 collective-permute-start.22
  86.3 2.4 %collective-permute-start.16 = (f32[8,128]{1,0:T(8,128)S(1)}, f32[8,128]{1,0:T(8,128)S(1)}, u32[]{:S(2)}, u32[]{:S(2)}) collective-permute-start(f32[8,128]{1,0:T(8,128)S(1)} %get-tuple-element.77), channel_id=1, source_target_pairs={{0,4},{4,0},{8,12},{12,8},{16,20},{20,16},{24,28},{28,24},{1,5},{5... | collective-permute-start | bytes 12296 | tf_op jit(solution)/shard_map/ppermute | solution.py:286
  88.7 1.6 collective-permute-done.16
  90.3 1.9 collective-permute-start.17
  92.2 1.7 collective-permute-done.17
  93.9 2.4 %collective-permute-start.18 = (f32[8,128]{1,0:T(8,128)S(1)}, f32[8,128]{1,0:T(8,128)S(1)}, u32[]{:S(2)}, u32[]{:S(2)}) collective-permute-start(f32[8,128]{1,0:T(8,128)S(1)} %add.81), channel_id=1, source_target_pairs={{0,16},{4,20},{8,24},{12,28},{16,0},{20,4},{24,8},{28,12},{1,17},{... | collective-permute-start | bytes 12296 | tf_op jit(solution)/shard_map/ppermute | solution.py:286
  96.4 2.1 %collective-permute-done.18 = f32[8,128]{1,0:T(8,128)S(1)} collective-permute-done((f32[8,128]{1,0:T(8,128)S(1)}, f32[8,128]{1,0:T(8,128)S(1)}, u32[]{:S(2)}, u32[]{:S(2)}) %collective-permute-start.18) | collective-permute-done | bytes 4128 | tf_op jit(solution)/shard_map/ppermute | solution.py:286
  98.4 1.2 collective-permute-done.19
  99.6 1.5 collective-permute-start.20
  101.1 2.1 %collective-permute-done.20 = f32[8,128]{1,0:T(8,128)S(1)} collective-permute-done((f32[8,128]{1,0:T(8,128)S(1)}, f32[8,128]{1,0:T(8,128)S(1)}, u32[]{:S(2)}, u32[]{:S(2)}) %collective-permute-start.20) | collective-permute-done | bytes 4128 | tf_op jit(solution)/shard_map/ppermute | solution.py:293
  103.3 5.1 %shard_map.116 = (f32[128,3072]{1,0:T(8,128)}, f32[128,3072]{1,0:T(8,128)}, f32[128,3072]{1,0:T(8,128)}, bf16[128,3072]{1,0:T(8,128)(2,1)}) custom-call(s32[3]{0:T(128)S(1)} %pad_add_fusion.spot, f32[8,128]{1,0:T(8,128)S(1)} %add.84.refs_0_, f32[128,768]{1,0:T(8,128)S(1)} %copy-done.12, bf16[128,768]{1,0:T(8,128)(2,1)S(1)} %collective-permute-done.21.refs_2_, ...), custom_call_target="tpu_custom_call" | custom-call | bytes 12582912 | tf_op jit(solution)/shard_map/pallas_call | solution.py:102
  108.4 1.9 %collective-permute-start.24 = (bf16[128,3072]{1,0:T(8,128)(2,1)}, bf16[128,3072]{1,0:T(8,128)(2,1)S(1)}, u32[]{:S(2)}, u32[]{:S(2)}) collective-permute-start(bf16[128,3072]{1,0:T(8,128)(2,1)} %get-tuple-element.82.refs_3_), channel_id=1, source_target_pairs={{0,8},{4,12},{8,0},{12,4},{16,24},{20,28},{24,16},{28,20},{1,9},{5... | collective-permute-start | bytes 2359304 | tf_op jit(solution)/shard_map/ppermute | solution.py:286
  110.3 1.4 collective-permute-start.25
  111.7 1.5 collective-permute-start.26
  113.3 1.6 copy-done.2
  114.9 3.0 %shard_map.118 = (f32[2048,128]{1,0:T(8,128)S(1)}, f32[2048,128]{1,0:T(8,128)S(1)}) custom-call(s32[3]{0:T(128)S(1)} %pad_add_fusion.spot, f32[2,2048,128]{2,1,0:T(8,128)S(1)} %copy-done.2, f32[2,2048,128]{2,1,0:T(8,128)} %collective-permute-done.30.refs_1_), custom_call_target="tpu_custom_call" | custom-call | bytes 6291456 | tf_op jit(solution)/shard_map/pallas_call | solution.py:102
  117.8 1.6 collective-permute-start.35
  119.4 7.8 %collective-permute-done.24.refs_0_ = bf16[128,3072]{1,0:T(8,128)(2,1)S(1)} collective-permute-done((bf16[128,3072]{1,0:T(8,128)(2,1)}, bf16[128,3072]{1,0:T(8,128)(2,1)S(1)}, u32[]{:S(2)}, u32[]{:S(2)}) %collective-permute-start.24) | collective-permute-done | bytes 786464 | tf_op jit(solution)/shard_map/ppermute | solution.py:286
  127.2 1.5 collective-permute-done.25.refs_1_
  128.7 4.1 %collective-permute-start.31 = (bf16[128,3072]{1,0:T(8,128)(2,1)}, bf16[128,3072]{1,0:T(8,128)(2,1)S(1)}, u32[]{:S(2)}, u32[]{:S(2)}) collective-permute-start(bf16[128,3072]{1,0:T(8,128)(2,1)} %get-tuple-element.86), channel_id=1, source_target_pairs={{0,24},{4,28},{24,0},{28,4},{1,25},{5,29},{25,1},{29,5},{2,26},{6,... | collective-permute-start | bytes 2359304 | tf_op jit(solution)/shard_map/ppermute | solution.py:290
  132.8 1.1 collective-permute-start.32
  134.7 1.2 constant_dynamic-update-slice_fusion.8
  136.1 13.7 %collective-permute-done.31.refs_0_ = bf16[128,3072]{1,0:T(8,128)(2,1)S(1)} collective-permute-done((bf16[128,3072]{1,0:T(8,128)(2,1)}, bf16[128,3072]{1,0:T(8,128)(2,1)S(1)}, u32[]{:S(2)}, u32[]{:S(2)}) %collective-permute-start.31) | collective-permute-done | bytes 786464 | tf_op jit(solution)/shard_map/ppermute | solution.py:290
  149.9 1.1 constant_dynamic-update-slice_fusion.4
  151.0 1.8 collective-permute-start.33
  153.4 1.8 shard_map.121
  155.1 1.2 collective-permute-start.36
  156.3 1.4 collective-permute-start.37
  157.7 1.9 collective-permute-start.38
  159.6 15.0 %collective-permute-done.36.refs_3_ = bf16[512,128]{1,0:T(8,128)(2,1)S(1)} collective-permute-done((bf16[512,128]{1,0:T(8,128)(2,1)}, bf16[512,128]{1,0:T(8,128)(2,1)S(1)}, u32[]{:S(2)}, u32[]{:S(2)}) %collective-permute-start.36) | collective-permute-done | bytes 131104 | tf_op jit(solution)/shard_map/ppermute | solution.py:286
  174.5 2.3 %collective-permute-done.38.refs_5_ = bf16[512,128]{1,0:T(8,128)(2,1)} collective-permute-done((bf16[512,128]{1,0:T(8,128)(2,1)}, bf16[512,128]{1,0:T(8,128)(2,1)}, u32[]{:S(2)}, u32[]{:S(2)}) %collective-permute-start.38) | collective-permute-done | bytes 131104 | tf_op jit(solution)/shard_map/ppermute | solution.py:286
  177.8 1.6 collective-permute-start.39
  181.9 3.7 %collective-permute-done.39.refs_6_ = bf16[4,256,128]{2,1,0:T(8,128)(2,1)S(1)} collective-permute-done((bf16[4,256,128]{2,1,0:T(8,128)(2,1)S(1)}, bf16[4,256,128]{2,1,0:T(8,128)(2,1)S(1)}, u32[]{:S(2)}, u32[]{:S(2)}) %collective-permute-start.39) | collective-permute-done | bytes 262176 | tf_op jit(solution)/shard_map/ppermute | solution.py:286
  185.7 4.0 %shard_map.123 = (bf16[256,1024]{1,0:T(8,128)(2,1)}, bf16[256,1024]{1,0:T(8,128)(2,1)}) custom-call(s32[3]{0:T(128)S(1)} %pad_add_fusion.spot, bf16[256,1024]{1,0:T(8,128)(2,1)S(1)} %copy-done.4, bf16[256,1024]{1,0:T(8,128)(2,1)S(1)} %copy-done.6, bf16[512,128]{1,0:T(8,128)(2,1)S(1)} %get-tuple-element.95.refs_2_, ...), custom_call_target="tpu_custom_call" | custom-call | bytes 4194304 | tf_op jit(solution)/shard_map/pallas_call | solution.py:102
  (109 shorter events, 13.2 us)
Async XLA Ops:
  0.6 1.4 copy-start
  0.6 66.0 %copy-start.1 = (f32[128,3072]{1,0:T(8,128)S(1)}, f32[128,3072]{1,0:T(8,128)}, u32[]{:S(2)}) copy-start(f32[128,3072]{1,0:T(8,128)} %refs_5_.1) | copy-start | bytes 4718596
  2.1 12.3 %collective-permute-start = (bf16[256,768]{1,0:T(8,128)(2,1)S(1)}, bf16[256,768]{1,0:T(8,128)(2,1)}, u32[]{:S(2)}, u32[]{:S(2)}) collective-permute-start(bf16[256,768]{1,0:T(8,128)(2,1)S(1)} %constant_dynamic-slice_fusion.refs_4_), channel_id=1, source_target_pairs={{0,8},{4,12},{8,0},{12,4},{16,24},{20,28},{24,16},{28,20},{1,9},{5... | collective-permute-start | bytes 1179656 | tf_op jit(solution)/shard_map/ppermute | solution.py:286
  5.2 10.7 %collective-permute-start.1 = (bf16[256,768]{1,0:T(8,128)(2,1)S(1)}, bf16[256,768]{1,0:T(8,128)(2,1)}, u32[]{:S(2)}, u32[]{:S(2)}) collective-permute-start(bf16[256,768]{1,0:T(8,128)(2,1)S(1)} %constant_dynamic-slice_fusion.refs_4_), channel_id=1, source_target_pairs={{0,4},{4,0},{8,12},{12,8},{16,20},{20,16},{24,28},{28,24},{1,5},{5... | collective-permute-start | bytes 1179656 | tf_op jit(solution)/shard_map/ppermute | solution.py:286
  6.7 9.2 %collective-permute-start.2 = (bf16[256,768]{1,0:T(8,128)(2,1)S(1)}, bf16[256,768]{1,0:T(8,128)(2,1)}, u32[]{:S(2)}, u32[]{:S(2)}) collective-permute-start(bf16[256,768]{1,0:T(8,128)(2,1)S(1)} %constant_dynamic-slice_fusion.refs_4_), channel_id=1, source_target_pairs={{8,16},{12,20},{16,8},{20,12},{9,17},{13,21},{17,9},{21,13},{10,18... | collective-permute-start | bytes 1179656 | tf_op jit(solution)/shard_map/ppermute | solution.py:290
  8.2 1.0 copy-start.3
  9.2 1.0 copy-start.5
  12.2 3.6 %copy-start.13 = (bf16[4,128,256]{2,1,0:T(8,128)(2,1)}, bf16[4,128,256]{2,1,0:T(8,128)(2,1)S(1)}, u32[]{:S(2)}) copy-start(bf16[4,128,256]{2,1,0:T(8,128)(2,1)S(1)} %get-tuple-element.64.refs_0_) | copy-start | bytes 786436
  15.9 19.9 %collective-permute-start.3 = (bf16[256,768]{1,0:T(8,128)(2,1)S(1)}, bf16[256,768]{1,0:T(8,128)(2,1)}, u32[]{:S(2)}, u32[]{:S(2)}) collective-permute-start(bf16[256,768]{1,0:T(8,128)(2,1)S(1)} %get-tuple-element.59.refs_4_.refs_0_), channel_id=1, source_target_pairs={{0,24},{4,28},{24,0},{28,4},{1,25},{5,29},{25,1},{29,5},{2,26},{6,... | collective-permute-start | bytes 1179656 | tf_op jit(solution)/shard_map/ppermute | solution.py:290
  20.2 15.6 %collective-permute-start.5 = (bf16[256,768]{1,0:T(8,128)(2,1)}, bf16[256,768]{1,0:T(8,128)(2,1)}, u32[]{:S(2)}, u32[]{:S(2)}) collective-permute-start(bf16[256,768]{1,0:T(8,128)(2,1)} %get-tuple-element.61.refs_6_.refs_2_), channel_id=1, source_target_pairs={{0,4},{4,0},{8,12},{12,8},{16,20},{20,16},{24,28},{28,24},{1,5},{5... | collective-permute-start | bytes 1179656 | tf_op jit(solution)/shard_map/ppermute | solution.py:286
  21.8 14.0 %collective-permute-start.4 = (bf16[4,128,256]{2,1,0:T(8,128)(2,1)}, bf16[4,128,256]{2,1,0:T(8,128)(2,1)}, u32[]{:S(2)}, u32[]{:S(2)}) collective-permute-start(bf16[4,128,256]{2,1,0:T(8,128)(2,1)} %get-tuple-element.60), channel_id=1, source_target_pairs={{0,4},{4,0},{8,12},{12,8},{16,20},{20,16},{24,28},{28,24},{1,5},{5... | collective-permute-start | bytes 786440 | tf_op jit(solution)/shard_map/ppermute | solution.py:286
  36.8 29.1 %copy-start.22 = (bf16[256,768]{1,0:T(8,128)(2,1)}, bf16[256,768]{1,0:T(8,128)(2,1)S(1)}, u32[]{:S(2)}) copy-start(bf16[256,768]{1,0:T(8,128)(2,1)S(1)} %broadcast_select_fusion.1.refs_11_.refs_7_) | copy-start | bytes 1179652
  36.9 17.1 %collective-permute-start.6 = (bf16[256,768]{1,0:T(8,128)(2,1)S(1)}, bf16[256,768]{1,0:T(8,128)(2,1)S(1)}, u32[]{:S(2)}, u32[]{:S(2)}) collective-permute-start(bf16[256,768]{1,0:T(8,128)(2,1)S(1)} %broadcast_select_fusion.1.refs_11_.refs_7_), channel_id=1, source_target_pairs={{0,8},{4,12},{8,0},{12,4},{16,24},{20,28},{24,16},{28,20},{1,9},{5... | collective-permute-start | bytes 1179656 | tf_op jit(solution)/shard_map/ppermute | solution.py:286
  38.5 15.5 %collective-permute-start.7 = (bf16[256,768]{1,0:T(8,128)(2,1)S(1)}, bf16[256,768]{1,0:T(8,128)(2,1)S(1)}, u32[]{:S(2)}, u32[]{:S(2)}) collective-permute-start(bf16[256,768]{1,0:T(8,128)(2,1)S(1)} %broadcast_select_fusion.1.refs_11_.refs_7_), channel_id=1, source_target_pairs={{0,4},{4,0},{8,12},{12,8},{16,20},{20,16},{24,28},{28,24},{1,5},{5... | collective-permute-start | bytes 1179656 | tf_op jit(solution)/shard_map/ppermute | solution.py:286
  39.0 0.9 copy-start.14
  42.5 10.5 %collective-permute-start.10 = (bf16[2,128,256]{2,1,0:T(8,128)(2,1)S(1)}, bf16[2,128,256]{2,1,0:T(8,128)(2,1)S(1)}, u32[]{:S(2)}, u32[]{:S(2)}) collective-permute-start(bf16[2,128,256]{2,1,0:T(8,128)(2,1)S(1)} %get-tuple-element.69), channel_id=1, source_target_pairs={{0,24},{4,28},{8,16},{12,20},{16,8},{20,12},{24,0},{28,4},{1,25},{... | collective-permute-start | bytes 393224 | tf_op jit(solution)/shard_map/ppermute | solution.py:286
  44.9 9.1 %collective-permute-start.8 = (bf16[2,128,256]{2,1,0:T(8,128)(2,1)S(1)}, bf16[2,128,256]{2,1,0:T(8,128)(2,1)S(1)}, u32[]{:S(2)}, u32[]{:S(2)}) collective-permute-start(bf16[2,128,256]{2,1,0:T(8,128)(2,1)S(1)} %get-tuple-element.67), channel_id=1, source_target_pairs={{0,8},{4,12},{8,0},{12,4},{16,24},{20,28},{24,16},{28,20},{1,9},{5... | collective-permute-start | bytes 393224 | tf_op jit(solution)/shard_map/ppermute | solution.py:286
  44.9 9.1 %collective-permute-start.9 = (bf16[2,128,256]{2,1,0:T(8,128)(2,1)S(1)}, bf16[2,128,256]{2,1,0:T(8,128)(2,1)S(1)}, u32[]{:S(2)}, u32[]{:S(2)}) collective-permute-start(bf16[2,128,256]{2,1,0:T(8,128)(2,1)S(1)} %get-tuple-element.68), channel_id=1, source_target_pairs={{0,16},{4,20},{8,24},{12,28},{16,0},{20,4},{24,8},{28,12},{1,17},{... | collective-permute-start | bytes 393224 | tf_op jit(solution)/shard_map/ppermute | solution.py:286
  54.0 2.5 %copy-start.9 = (bf16[256,768]{1,0:T(8,128)(2,1)}, bf16[256,768]{1,0:T(8,128)(2,1)S(1)}, u32[]{:S(2)}) copy-start(bf16[256,768]{1,0:T(8,128)(2,1)S(1)} %get-tuple-element.74.refs_8_.refs_4_) | copy-start | bytes 1179652
  54.0 4.1 %copy-start.10 = (bf16[256,768]{1,0:T(8,128)(2,1)}, bf16[256,768]{1,0:T(8,128)(2,1)S(1)}, u32[]{:S(2)}) copy-start(bf16[256,768]{1,0:T(8,128)(2,1)S(1)} %get-tuple-element.75.refs_12_.refs_8_) | copy-start | bytes 1179652
  55.0 11.0 %collective-permute-start.12 = (bf16[4,2,128,256]{3,2,1,0:T(8,128)(2,1)}, bf16[4,2,128,256]{3,2,1,0:T(8,128)(2,1)}, u32[]{:S(2)}, u32[]{:S(2)}) collective-permute-start(bf16[4,2,128,256]{3,2,1,0:T(8,128)(2,1)} %pad_maximum_fusion.refs_0_), channel_id=1, source_target_pairs={{0,2},{1,3},{2,0},{3,1},{4,6},{5,7},{6,4},{7,5},{8,10},{9,11},{10,... | collective-permute-start | bytes 1572872 | tf_op jit(solution)/shard_map/ppermute | solution.py:293
  56.5 5.7 %collective-permute-start.13 = (bf16[128,768]{1,0:T(8,128)(2,1)S(1)}, bf16[128,768]{1,0:T(8,128)(2,1)S(1)}, u32[]{:S(2)}, u32[]{:S(2)}) collective-permute-start(bf16[128,768]{1,0:T(8,128)(2,1)S(1)} %slice.24), channel_id=1, source_target_pairs={{0,4},{4,0},{8,12},{12,8},{16,20},{20,16},{24,28},{28,24},{1,5},{5... | collective-permute-start | bytes 589832 | tf_op jit(solution)/shard_map/ppermute | solution.py:286
  58.1 5.7 %collective-permute-start.14 = (bf16[128,768]{1,0:T(8,128)(2,1)S(1)}, bf16[128,768]{1,0:T(8,128)(2,1)S(1)}, u32[]{:S(2)}, u32[]{:S(2)}) collective-permute-start(bf16[128,768]{1,0:T(8,128)(2,1)S(1)} %slice.25), channel_id=1, source_target_pairs={{0,8},{4,12},{8,0},{12,4},{16,24},{20,28},{24,16},{28,20},{1,9},{5... | collective-permute-start | bytes 589832 | tf_op jit(solution)/shard_map/ppermute | solution.py:286
  59.5 9.4 %collective-permute-start.11 = (bf16[4,2,128,256]{3,2,1,0:T(8,128)(2,1)}, bf16[4,2,128,256]{3,2,1,0:T(8,128)(2,1)}, u32[]{:S(2)}, u32[]{:S(2)}) collective-permute-start(bf16[4,2,128,256]{3,2,1,0:T(8,128)(2,1)} %pad_maximum_fusion.refs_0_), channel_id=1, source_target_pairs={{0,1},{1,0},{2,3},{3,2},{4,5},{5,4},{6,7},{7,6},{8,9},{9,8},{10,11... | collective-permute-start | bytes 1572872 | tf_op jit(solution)/shard_map/ppermute | solution.py:293
  63.8 2.2 %copy-start.18 = (bf16[128,768]{1,0:T(8,128)(2,1)}, bf16[128,768]{1,0:T(8,128)(2,1)S(1)}, u32[]{:S(2)}) copy-start(bf16[128,768]{1,0:T(8,128)(2,1)S(1)} %collective-permute-done.14.refs_2_.refs_10_.refs_6_) | copy-start | bytes 589828
  66.7 2.3 %collective-permute-start.15 = (bf16[4,2,128,256]{3,2,1,0:T(8,128)(2,1)}, bf16[4,2,128,256]{3,2,1,0:T(8,128)(2,1)}, u32[]{:S(2)}, u32[]{:S(2)}) collective-permute-start(bf16[4,2,128,256]{3,2,1,0:T(8,128)(2,1)} %shard_map.114.refs_2_), channel_id=1, source_target_pairs={{0,1},{1,0},{2,3},{3,2},{4,5},{5,4},{6,7},{7,6},{8,9},{9,8},{10,11... | collective-permute-start | bytes 1572872 | tf_op jit(solution)/shard_map/ppermute | solution.py:293
  66.7 11.5 %copy-start.17 = (bf16[128,768]{1,0:T(8,128)(2,1)S(1)}, bf16[128,768]{1,0:T(8,128)(2,1)}, u32[]{:S(2)}) copy-start(bf16[128,768]{1,0:T(8,128)(2,1)} %copy-done.15) | copy-start | bytes 589828
  66.7 11.5 %copy-start.20 = (bf16[128,768]{1,0:T(8,128)(2,1)S(1)}, bf16[128,768]{1,0:T(8,128)(2,1)}, u32[]{:S(2)}) copy-start(bf16[128,768]{1,0:T(8,128)(2,1)} %copy-done.18) | copy-start | bytes 589828
  66.8 36.4 %copy-start.7 = (f32[128,3072]{1,0:T(8,128)S(1)}, f32[128,3072]{1,0:T(8,128)}, u32[]{:S(2)}) copy-start(f32[128,3072]{1,0:T(8,128)} %refs_6_.1) | copy-start | bytes 4718596
  66.8 36.4 %copy-start.8 = (f32[128,3072]{1,0:T(8,128)S(1)}, f32[128,3072]{1,0:T(8,128)}, u32[]{:S(2)}) copy-start(f32[128,3072]{1,0:T(8,128)} %refs_7_.1) | copy-start | bytes 4718596
  66.8 11.4 %collective-permute-start.27 = (bf16[128,768]{1,0:T(8,128)(2,1)S(1)}, bf16[128,768]{1,0:T(8,128)(2,1)S(1)}, u32[]{:S(2)}, u32[]{:S(2)}) collective-permute-start(bf16[128,768]{1,0:T(8,128)(2,1)S(1)} %get-tuple-element.113), channel_id=1, source_target_pairs={{0,1},{1,0},{2,3},{3,2},{4,5},{5,4},{6,7},{7,6},{8,9},{9,8},{10,11... | collective-permute-start | bytes 589832 | tf_op jit(solution)/shard_map/ppermute | solution.py:293
  67.4 10.8 %collective-permute-start.28 = (bf16[128,768]{1,0:T(8,128)(2,1)S(1)}, bf16[128,768]{1,0:T(8,128)(2,1)S(1)}, u32[]{:S(2)}, u32[]{:S(2)}) collective-permute-start(bf16[128,768]{1,0:T(8,128)(2,1)S(1)} %get-tuple-element.115), channel_id=1, source_target_pairs={{0,2},{1,3},{2,0},{3,1},{4,6},{5,7},{6,4},{7,5},{8,10},{9,11},{10,... | collective-permute-start | bytes 589832 | tf_op jit(solution)/shard_map/ppermute | solution.py:293
  68.9 9.3 %collective-permute-start.29 = (bf16[128,768]{1,0:T(8,128)(2,1)S(1)}, bf16[128,768]{1,0:T(8,128)(2,1)S(1)}, u32[]{:S(2)}, u32[]{:S(2)}) collective-permute-start(bf16[128,768]{1,0:T(8,128)(2,1)S(1)} %get-tuple-element.112), channel_id=1, source_target_pairs={{0,3},{1,2},{2,1},{3,0},{4,7},{5,6},{6,5},{7,4},{8,11},{9,10},{10,... | collective-permute-start | bytes 589832 | tf_op jit(solution)/shard_map/ppermute | solution.py:293
  68.9 0.9 copy-start.16
  69.9 0.9 copy-start.19
  77.5 0.7 copy-start.11
  78.2 25.0 %copy-start.12 = (f32[128,768]{1,0:T(8,128)S(1)}, f32[128,768]{1,0:T(8,128)}, u32[]{:S(2)}) copy-start(f32[128,768]{1,0:T(8,128)} %copy-done.11) | copy-start | bytes 1179652
  83.8 29.5 %collective-permute-start.30 = (f32[2,2048,128]{2,1,0:T(8,128)}, f32[2,2048,128]{2,1,0:T(8,128)}, u32[]{:S(2)}, u32[]{:S(2)}) collective-permute-start(f32[2,2048,128]{2,1,0:T(8,128)} %get-tuple-element.84), channel_id=1, source_target_pairs={{0,1},{1,0},{2,3},{3,2},{4,5},{5,4},{6,7},{7,6},{8,9},{9,8},{10,11... | collective-permute-start | bytes 6291464 | tf_op jit(solution)/shard_map/ppermute | solution.py:293
  84.4 18.8 %collective-permute-start.21 = (bf16[128,768]{1,0:T(8,128)(2,1)S(1)}, bf16[128,768]{1,0:T(8,128)(2,1)S(1)}, u32[]{:S(2)}, u32[]{:S(2)}) collective-permute-start(bf16[128,768]{1,0:T(8,128)(2,1)S(1)} %get-tuple-element.79), channel_id=1, source_target_pairs={{0,1},{1,0},{2,3},{3,2},{4,5},{5,4},{6,7},{7,6},{8,9},{9,8},{10,11... | collective-permute-start | bytes 589832 | tf_op jit(solution)/shard_map/ppermute | solution.py:293
  84.5 18.7 %collective-permute-start.22 = (bf16[128,768]{1,0:T(8,128)(2,1)S(1)}, bf16[128,768]{1,0:T(8,128)(2,1)S(1)}, u32[]{:S(2)}, u32[]{:S(2)}) collective-permute-start(bf16[128,768]{1,0:T(8,128)(2,1)S(1)} %get-tuple-element.80), channel_id=1, source_target_pairs={{0,2},{1,3},{2,0},{3,1},{4,6},{5,7},{6,4},{7,5},{8,10},{9,11},{10,... | collective-permute-start | bytes 589832 | tf_op jit(solution)/shard_map/ppermute | solution.py:293
  86.0 17.2 %collective-permute-start.23 = (bf16[128,768]{1,0:T(8,128)(2,1)S(1)}, bf16[128,768]{1,0:T(8,128)(2,1)S(1)}, u32[]{:S(2)}, u32[]{:S(2)}) collective-permute-start(bf16[128,768]{1,0:T(8,128)(2,1)S(1)} %get-tuple-element.81), channel_id=1, source_target_pairs={{0,3},{1,2},{2,1},{3,0},{4,7},{5,6},{6,5},{7,4},{8,11},{9,10},{10,... | collective-permute-start | bytes 589832 | tf_op jit(solution)/shard_map/ppermute | solution.py:293
  86.3 4.0 %collective-permute-start.16 = (f32[8,128]{1,0:T(8,128)S(1)}, f32[8,128]{1,0:T(8,128)S(1)}, u32[]{:S(2)}, u32[]{:S(2)}) collective-permute-start(f32[8,128]{1,0:T(8,128)S(1)} %get-tuple-element.77), channel_id=1, source_target_pairs={{0,4},{4,0},{8,12},{12,8},{16,20},{20,16},{24,28},{28,24},{1,5},{5... | collective-permute-start | bytes 12296 | tf_op jit(solution)/shard_map/ppermute | solution.py:286
  90.3 3.6 %collective-permute-start.17 = (f32[8,128]{1,0:T(8,128)S(1)}, f32[8,128]{1,0:T(8,128)S(1)}, u32[]{:S(2)}, u32[]{:S(2)}) collective-permute-start(f32[8,128]{1,0:T(8,128)S(1)} %add.80), channel_id=1, source_target_pairs={{0,8},{4,12},{8,0},{12,4},{16,24},{20,28},{24,16},{28,20},{1,9},{5... | collective-permute-start | bytes 12296 | tf_op jit(solution)/shard_map/ppermute | solution.py:286
  93.9 4.5 %collective-permute-start.18 = (f32[8,128]{1,0:T(8,128)S(1)}, f32[8,128]{1,0:T(8,128)S(1)}, u32[]{:S(2)}, u32[]{:S(2)}) collective-permute-start(f32[8,128]{1,0:T(8,128)S(1)} %add.81), channel_id=1, source_target_pairs={{0,16},{4,20},{8,24},{12,28},{16,0},{20,4},{24,8},{28,12},{1,17},{... | collective-permute-start | bytes 12296 | tf_op jit(solution)/shard_map/ppermute | solution.py:286
  98.4 1.2 collective-permute-start.19
  99.6 3.6 %collective-permute-start.20 = (f32[8,128]{1,0:T(8,128)S(1)}, f32[8,128]{1,0:T(8,128)S(1)}, u32[]{:S(2)}, u32[]{:S(2)}) collective-permute-start(f32[8,128]{1,0:T(8,128)S(1)} %add.83), channel_id=1, source_target_pairs={{0,2},{1,3},{2,0},{3,1},{4,6},{5,7},{6,4},{7,5},{8,10},{9,11},{10,... | collective-permute-start | bytes 12296 | tf_op jit(solution)/shard_map/ppermute | solution.py:293
  108.4 18.8 %collective-permute-start.24 = (bf16[128,3072]{1,0:T(8,128)(2,1)}, bf16[128,3072]{1,0:T(8,128)(2,1)S(1)}, u32[]{:S(2)}, u32[]{:S(2)}) collective-permute-start(bf16[128,3072]{1,0:T(8,128)(2,1)} %get-tuple-element.82.refs_3_), channel_id=1, source_target_pairs={{0,8},{4,12},{8,0},{12,4},{16,24},{20,28},{24,16},{28,20},{1,9},{5... | collective-permute-start | bytes 2359304 | tf_op jit(solution)/shard_map/ppermute | solution.py:286
  110.3 18.4 %collective-permute-start.25 = (bf16[128,3072]{1,0:T(8,128)(2,1)}, bf16[128,3072]{1,0:T(8,128)(2,1)S(1)}, u32[]{:S(2)}, u32[]{:S(2)}) collective-permute-start(bf16[128,3072]{1,0:T(8,128)(2,1)} %get-tuple-element.82.refs_3_), channel_id=1, source_target_pairs={{0,4},{4,0},{8,12},{12,8},{16,20},{20,16},{24,28},{28,24},{1,5},{5... | collective-permute-start | bytes 2359304 | tf_op jit(solution)/shard_map/ppermute | solution.py:286
  111.7 16.9 %collective-permute-start.26 = (bf16[128,3072]{1,0:T(8,128)(2,1)}, bf16[128,3072]{1,0:T(8,128)(2,1)}, u32[]{:S(2)}, u32[]{:S(2)}) collective-permute-start(bf16[128,3072]{1,0:T(8,128)(2,1)} %get-tuple-element.82.refs_3_), channel_id=1, source_target_pairs={{8,16},{12,20},{16,8},{20,12},{9,17},{13,21},{17,9},{21,13},{10,18... | collective-permute-start | bytes 2359304 | tf_op jit(solution)/shard_map/ppermute | solution.py:290
  113.3 1.6 copy-start.2
  117.8 35.5 %collective-permute-start.35 = (f32[2048,128]{1,0:T(8,128)S(1)}, f32[2048,128]{1,0:T(8,128)S(1)}, u32[]{:S(2)}, u32[]{:S(2)}) collective-permute-start(f32[2048,128]{1,0:T(8,128)S(1)} %get-tuple-element.85.refs_4_), channel_id=1, source_target_pairs={{0,2},{1,3},{2,0},{3,1},{4,6},{5,7},{6,4},{7,5},{8,10},{9,11},{10,... | collective-permute-start | bytes 3145736 | tf_op jit(solution)/shard_map/ppermute | solution.py:293
  128.7 21.1 %collective-permute-start.31 = (bf16[128,3072]{1,0:T(8,128)(2,1)}, bf16[128,3072]{1,0:T(8,128)(2,1)S(1)}, u32[]{:S(2)}, u32[]{:S(2)}) collective-permute-start(bf16[128,3072]{1,0:T(8,128)(2,1)} %get-tuple-element.86), channel_id=1, source_target_pairs={{0,24},{4,28},{24,0},{28,4},{1,25},{5,29},{25,1},{29,5},{2,26},{6,... | collective-permute-start | bytes 2359304 | tf_op jit(solution)/shard_map/ppermute | solution.py:290
  132.8 17.0 %collective-permute-start.32 = (bf16[128,3072]{1,0:T(8,128)(2,1)S(1)}, bf16[128,3072]{1,0:T(8,128)(2,1)S(1)}, u32[]{:S(2)}, u32[]{:S(2)}) collective-permute-start(bf16[128,3072]{1,0:T(8,128)(2,1)S(1)} %get-tuple-element.87), channel_id=1, source_target_pairs={{0,4},{4,0},{8,12},{12,8},{16,20},{20,16},{24,28},{28,24},{1,5},{5... | collective-permute-start | bytes 2359304 | tf_op jit(solution)/shard_map/ppermute | solution.py:286
  151.0 5.3 %copy-start.21 = (bf16[1024,3072]{1,0:T(8,128)(2,1)}, bf16[1024,3072]{1,0:T(8,128)(2,1)S(1)}, u32[]{:S(2)}) copy-start(bf16[1024,3072]{1,0:T(8,128)(2,1)S(1)} %get-tuple-element.110) | copy-start | bytes 18874372
  151.0 25.8 %collective-permute-start.33 = (bf16[128,3072]{1,0:T(8,128)(2,1)}, bf16[128,3072]{1,0:T(8,128)(2,1)S(1)}, u32[]{:S(2)}, u32[]{:S(2)}) collective-permute-start(bf16[128,3072]{1,0:T(8,128)(2,1)} %get-tuple-element.111), channel_id=1, source_target_pairs={{0,8},{4,12},{8,0},{12,4},{16,24},{20,28},{24,16},{28,20},{1,9},{5... | collective-permute-start | bytes 2359304 | tf_op jit(solution)/shard_map/ppermute | solution.py:286
  152.8 24.1 %collective-permute-start.34 = (bf16[128,3072]{1,0:T(8,128)(2,1)}, bf16[128,3072]{1,0:T(8,128)(2,1)S(1)}, u32[]{:S(2)}, u32[]{:S(2)}) collective-permute-start(bf16[128,3072]{1,0:T(8,128)(2,1)} %get-tuple-element.111), channel_id=1, source_target_pairs={{0,4},{4,0},{8,12},{12,8},{16,20},{20,16},{24,28},{28,24},{1,5},{5... | collective-permute-start | bytes 2359304 | tf_op jit(solution)/shard_map/ppermute | solution.py:286
  155.1 19.4 %collective-permute-start.36 = (bf16[512,128]{1,0:T(8,128)(2,1)}, bf16[512,128]{1,0:T(8,128)(2,1)S(1)}, u32[]{:S(2)}, u32[]{:S(2)}) collective-permute-start(bf16[512,128]{1,0:T(8,128)(2,1)} %get-tuple-element.92), channel_id=1, source_target_pairs={{0,8},{4,12},{8,0},{12,4},{16,24},{20,28},{24,16},{28,20},{1,9},{5... | collective-permute-start | bytes 393224 | tf_op jit(solution)/shard_map/ppermute | solution.py:286
  156.3 18.2 %collective-permute-start.37 = (bf16[512,128]{1,0:T(8,128)(2,1)}, bf16[512,128]{1,0:T(8,128)(2,1)S(1)}, u32[]{:S(2)}, u32[]{:S(2)}) collective-permute-start(bf16[512,128]{1,0:T(8,128)(2,1)} %get-tuple-element.93), channel_id=1, source_target_pairs={{0,16},{4,20},{8,24},{12,28},{16,0},{20,4},{24,8},{28,12},{1,17},{... | collective-permute-start | bytes 393224 | tf_op jit(solution)/shard_map/ppermute | solution.py:286
  157.7 19.1 %collective-permute-start.38 = (bf16[512,128]{1,0:T(8,128)(2,1)}, bf16[512,128]{1,0:T(8,128)(2,1)}, u32[]{:S(2)}, u32[]{:S(2)}) collective-permute-start(bf16[512,128]{1,0:T(8,128)(2,1)} %get-tuple-element.94), channel_id=1, source_target_pairs={{0,24},{4,28},{8,16},{12,20},{16,8},{20,12},{24,0},{28,4},{1,25},{... | collective-permute-start | bytes 393224 | tf_op jit(solution)/shard_map/ppermute | solution.py:286
  159.6 26.1 %copy-start.4 = (bf16[256,1024]{1,0:T(8,128)(2,1)S(1)}, bf16[256,1024]{1,0:T(8,128)(2,1)}, u32[]{:S(2)}) copy-start(bf16[256,1024]{1,0:T(8,128)(2,1)} %refs_0_.3) | copy-start | bytes 1572868
  159.6 26.1 %copy-start.6 = (bf16[256,1024]{1,0:T(8,128)(2,1)S(1)}, bf16[256,1024]{1,0:T(8,128)(2,1)}, u32[]{:S(2)}) copy-start(bf16[256,1024]{1,0:T(8,128)(2,1)} %refs_1_.3) | copy-start | bytes 1572868
  177.8 7.9 %collective-permute-start.39 = (bf16[4,256,128]{2,1,0:T(8,128)(2,1)S(1)}, bf16[4,256,128]{2,1,0:T(8,128)(2,1)S(1)}, u32[]{:S(2)}, u32[]{:S(2)}) collective-permute-start(bf16[4,256,128]{2,1,0:T(8,128)(2,1)S(1)} %pad_maximum_fusion.1.refs_2_), channel_id=1, source_target_pairs={{0,4},{4,0},{8,12},{12,8},{16,20},{20,16},{24,28},{28,24},{1,5},{5... | collective-permute-start | bytes 786440 | tf_op jit(solution)/shard_map/ppermute | solution.py:286
  179.3 10.5 %collective-permute-start.40 = (bf16[64,3072]{1,0:T(8,128)(2,1)S(1)}, bf16[64,3072]{1,0:T(8,128)(2,1)S(1)}, u32[]{:S(2)}, u32[]{:S(2)}) collective-permute-start(bf16[64,3072]{1,0:T(8,128)(2,1)S(1)} %slice.30), channel_id=1, source_target_pairs={{0,4},{4,0},{8,12},{12,8},{16,20},{20,16},{24,28},{28,24},{1,5},{5... | collective-permute-start | bytes 1179656 | tf_op jit(solution)/shard_map/ppermute | solution.py:286
  180.0 10.7 %collective-permute-start.41 = (bf16[64,3072]{1,0:T(8,128)(2,1)S(1)}, bf16[64,3072]{1,0:T(8,128)(2,1)S(1)}, u32[]{:S(2)}, u32[]{:S(2)}) collective-permute-start(bf16[64,3072]{1,0:T(8,128)(2,1)S(1)} %slice.31), channel_id=1, source_target_pairs={{0,8},{4,12},{8,0},{12,4},{16,24},{20,28},{24,16},{28,20},{1,9},{5... | collective-permute-start | bytes 1179656 | tf_op jit(solution)/shard_map/ppermute | solution.py:286
  (1 other events, 0.7 us)
